TPU v7x, 256 devices: a whole 4x4x8 slice. The times are simulated.
256 devices in a mesh: batch: 32 (over y, x, core), proto: 8 (over z).
Axes of the slice: x: 4, y: 4, z: 8, core: 2. Of those that a mesh axis runs over, the one named last changes fastest.
Arguments:
- student_feat: bfloat16 [5120, 256], P('batch'), may hold values from -30 to 30
- prototypes: bfloat16 [256, 131072], P('batch', 'proto'), may hold values from -480 to 480
- teacher_logits: float32 [1024, 131072], P('batch', 'proto'), may hold values from -1 to 1
Outputs:
- grad_feat: float32 [5120, 256], P('batch')
- grad_weight: float32 [256, 131072], P('batch', 'proto')
All inputs are finite; a program needn't handle non-finite values.
Results may differ from a plain program's by a relative error of at most 0.0009.
Values may be sent and summed in bfloat16 or wider, within the bound.
No kernel may reach another device: no remote copies, remote signals or barrier semaphores. Data moves between devices by JAX's collectives and lax.ppermute only.
A program may use at most 128 MiB of HBM per device.

v0:
```python
import jax
import jax.numpy as jnp
from jax import lax
from jax.sharding import PartitionSpec as P

CROPS = 10
GLOBAL = 2
ITERS = 3


STUDENT_TEMP = 0.1
TEACHER_TEMP = 0.04


def normalize_rows(student_feat):
    features = student_feat.astype(jnp.float32)
    feat_norm = jnp.sqrt(jnp.sum(features * features, axis=1) + 1e-06)
    unit_vec = features / feat_norm[:, None]
    return (feat_norm, unit_vec, unit_vec.astype(jnp.bfloat16))


def crop_targets(mass_block):
    images = mass_block.shape[0] // GLOBAL
    col_width = mass_block.shape[1]
    grouped = mass_block.reshape(images, GLOBAL, col_width)
    pair_sum = jnp.sum(grouped, axis=1, keepdims=True)
    others = pair_sum - grouped
    distant = jnp.broadcast_to(pair_sum, (images, CROPS - GLOBAL, col_width))
    return jnp.concatenate([others, distant], axis=1).reshape(images * CROPS, col_width)


def pair_weights(row_count):
    crop_index = jnp.arange(row_count, dtype=jnp.int32) % CROPS
    return jnp.where(crop_index < GLOBAL, GLOBAL - 1, GLOBAL).astype(jnp.float32)


def shards(student_feat, prototypes, teacher_logits):
    feat_norm, unit_vec, unit_bf = normalize_rows(student_feat)
    row_count = unit_bf.shape[0]
    full_weights = lax.all_gather(prototypes, "batch", axis=0, tiled=True)
    local_cols = full_weights.shape[1]
    weights_wide = full_weights.astype(jnp.float32)
    col_norm = jnp.sqrt(jnp.sum(weights_wide * weights_wide, axis=0) + 1e-06)
    col_scale = 1.0 / (col_norm * STUDENT_TEMP)
    block_width = min(4096, local_cols)
    block_count = local_cols // block_width
    exp_part = jnp.zeros((row_count,), jnp.float32)
    for block_index in range(block_count):
        col_low = block_index * block_width
        weight_block = full_weights[:, col_low : col_low + block_width]
        raw_scores = jnp.dot(unit_bf, weight_block, preferred_element_type=jnp.float32)
        logits = raw_scores * col_scale[None, col_low : col_low + block_width]
        exp_part = exp_part + jnp.sum(jnp.exp(logits), axis=1)
    teacher_mass = jnp.exp(teacher_logits / TEACHER_TEMP)
    for sweep_index in range(ITERS):
        row_total = lax.psum(jnp.sum(teacher_mass, axis=0), "batch")
        teacher_mass = teacher_mass / row_total[None, :]
        col_part = jnp.sum(teacher_mass, axis=1)
        if sweep_index == 0:
            col_total = lax.psum(col_part, "proto")
            partition = lax.psum(exp_part, "proto")
        else:
            col_total = lax.psum(col_part, "proto")
        teacher_mass = teacher_mass / col_total[:, None]
    pair_weight = pair_weights(row_count)
    pair_total = float(GLOBAL * CROPS - GLOBAL)
    unit_grad = jnp.zeros((row_count, unit_bf.shape[1]), jnp.float32)
    grad_pieces = []
    for block_index in range(block_count):
        col_low = block_index * block_width
        weight_block = full_weights[:, col_low : col_low + block_width]
        scale_block = col_scale[col_low : col_low + block_width]
        raw_scores = jnp.dot(unit_bf, weight_block, preferred_element_type=jnp.float32)
        logits = raw_scores * scale_block[None, :]
        prob = jnp.exp(logits) / partition[:, None]
        target = crop_targets(teacher_mass[:, col_low : col_low + block_width])
        grad_raw = (
            (pair_weight[:, None] * prob - target) / pair_total * scale_block[None, :]
        ).astype(jnp.bfloat16)
        unit_grad = unit_grad + lax.dot_general(
            grad_raw, weight_block, (((1,), (1,)), ((), ())), preferred_element_type=jnp.float32
        )
        grad_pieces.append(grad_raw)
    grad_all = jnp.concatenate(grad_pieces, axis=1)
    unit_total = lax.psum(unit_grad, "proto")
    grad_feat = (
        unit_total - unit_vec * jnp.sum(unit_vec * unit_total, axis=1, keepdims=True)
    ) / feat_norm[:, None]
    weight_term = lax.psum_scatter(
        lax.dot_general(
            unit_bf, grad_all, (((0,), (0,)), ((), ())), preferred_element_type=jnp.float32
        ),
        "batch",
        scatter_dimension=0,
        tiled=True,
    )
    local_weights = prototypes.astype(jnp.float32)
    col_dot = lax.psum(jnp.sum(local_weights * weight_term, axis=0), "batch")
    grad_weight = weight_term - local_weights * (col_dot / (col_norm * col_norm))[None, :]
    return (grad_feat, grad_weight)


def solution(mesh):
    placed = (P("batch", None), P("batch", "proto"), P("batch", "proto"))
    return jax.shard_map(
        shards,
        mesh=mesh,
        in_specs=placed,
        out_specs=(P("batch", None), P("batch", "proto")),
        check_vma=False,
    )
```

profile of v0, /device:TPU:1, one launch (start us, length us, event | category | flops | bytes accessed | tf_op | source)
XLA Modules:
  0.0 827.6 jit_solution(14771007627959620848)
XLA Ops:
  7.2 2.8 fusion.44
  10.1 111.6 %all-reduce.7.cloned.1.call-done = f32[16384]{0:T(1024)} async-done(((f32[16384]{0:T(1024)}), f32[16384]{0:T(1024)}) %all-reduce.7.cloned.1.call-update) | async-done | bytes 65552 | tf_op jit(solution)/shard_map/psum | solution.py:56
  123.1 14.1 %psum.65 = f32[32]{0:T(128)S(1)} all-reduce(f32[32]{0:T(128)S(1)} %divide_reduce_fusion), channel_id=1, replica_groups=mesh['batch'=32,'proto'=8] {'proto'}, use_global_device_ids=true, to_apply=%region_10.0 | all-reduce | flops 32 | bytes 256 | tf_op jit(solution)/shard_map/psum | solution.py:60
  138.6 105.5 %all-reduce.9.cloned.1.call-done = f32[16384]{0:T(1024)} async-done(((f32[16384]{0:T(1024)}), f32[16384]{0:T(1024)}) %all-reduce.9.cloned.1.call-update) | async-done | bytes 65552 | tf_op jit(solution)/shard_map/psum | solution.py:56
  245.7 14.1 %psum.67 = f32[32]{0:T(128)S(1)} all-reduce(f32[32]{0:T(128)S(1)} %fusion.20), channel_id=1, replica_groups=mesh['batch'=32,'proto'=8] {'proto'}, use_global_device_ids=true, to_apply=%region_14.0 | all-reduce | flops 32 | bytes 256 | tf_op jit(solution)/shard_map/psum | solution.py:63
  262.5 104.2 %all-reduce.11.cloned.1.call-done = f32[16384]{0:T(1024)} async-done(((f32[16384]{0:T(1024)}), f32[16384]{0:T(1024)}) %all-reduce.11.cloned.1.call-update) | async-done | bytes 65552 | tf_op jit(solution)/shard_map/psum | solution.py:56
  368.4 58.1 %all-gather.2.cloned.1.call-done = bf16[256,16384]{1,0:T(8,128)(2,1)} async-done(((bf16[8,16384]{1,0:T(8,128)(2,1)}), bf16[256,16384]{1,0:T(8,128)(2,1)}) %all-gather.2.cloned.1.call-update) | async-done | bytes 8388624 | tf_op jit(solution)/shard_map/all_gather | solution.py:40
  426.5 5.3 multiply_reduce_fusion
  432.4 2.2 fusion.57
  434.6 2.2 fusion.58
  436.8 2.2 fusion.60
  439.0 2.2 fusion.59
  441.1 14.6 %all-reduce = (f32[32]{0:T(128)S(1)}, f32[160]{0:T(256)}) all-reduce(f32[32]{0:T(128)S(1)} %fusion.22, f32[160]{0:T(256)S(1)} %add_add_fusion), channel_id=1, replica_groups=mesh['batch'=32,'proto'=8] {'proto'}, use_global_device_ids=true, to_apply=%region_18.0 | all-reduce | flops 192 | bytes 1536 | tf_op jit(solution)/shard_map/psum | solution.py:63
  464.2 2.6 pad_maximum_fusion.1
  466.8 2.4 reshape.64
  470.3 2.6 pad_maximum_fusion.2
  472.9 3.6 reshape.66
  477.5 2.6 pad_maximum_fusion.3
  480.1 3.5 reshape.68
  484.6 2.6 pad_maximum_fusion
  487.3 3.6 reshape.62
  490.9 7.8 multiply_convert_fusion.3
  498.7 4.1 fusion.29
  502.8 2.5 fusion.26
  505.3 2.5 fusion.23
  507.9 3.3 fusion.41
  511.3 9.9 %fusion = f32[256,16384]{1,0:T(8,128)} fusion(bf16[160,4096]{1,0:T(8,128)(2,1)} %copy-done.7, bf16[160,4096]{1,0:T(8,128)(2,1)S(1)} %copy-done.6, bf16[160,4096]{1,0:T(8,128)(2,1)S(1)} %copy-done.4, bf16[160,4096]{1,0:T(8,128)(2,1)} %copy-done.2, f32[160]{0:T(256)S(1)} %copy-done.21, bf16[160,256]{1,0:T(8,128)(2,1)S(1)} %copy-done.13), kind=kOutput, calls=%fused_computation.1 | convolution fusion | flops 1363271680 | bytes 22102656 | tf_op jit(solution)/shard_map/dot_general | solution.py:90
  521.2 57.9 %all-reduce.13.cloned.1.call-done = f32[160,256]{1,0:T(8,128)} async-done(((f32[160,256]{1,0:T(8,128)}), f32[160,256]{1,0:T(8,128)}) %all-reduce.13.cloned.1.call-update) | async-done | bytes 163856 | tf_op jit(solution)/shard_map/psum | solution.py:85
  580.2 127.1 %reduce-scatter.2.cloned.1.call-done = f32[8,16384]{1,0:T(8,128)} async-done(((f32[256,16384]{1,0:T(8,128)}), f32[8,16384]{1,0:T(8,128)}) %reduce-scatter.2.cloned.1.call-update) | async-done | bytes 524304 | tf_op jit(solution)/shard_map/reduce_scatter | solution.py:89
  707.3 1.8 fusion.45
  710.9 107.1 %all-reduce.15.cloned.1.call-done = f32[16384]{0:T(1024)} async-done(((f32[16384]{0:T(1024)}), f32[16384]{0:T(1024)}) %all-reduce.15.cloned.1.call-update) | async-done | bytes 65552 | tf_op jit(solution)/shard_map/psum | solution.py:98
  818.9 1.9 fusion.46
  (94 shorter events, 24.8 us)
Async XLA Ops:
  7.2 114.5 %copy-start = (f32[32,16384]{1,0:T(8,128)S(1)}, f32[32,16384]{1,0:T(8,128)}, u32[]{:S(2)}) copy-start(f32[32,16384]{1,0:T(8,128)} %param.5) | copy-start | bytes 6291460
  7.2 114.5 %all-reduce.7.cloned.1.call-start = ((), (), s32[]{:S(2)}) async-start(), calls=%async_computation.2 | async-start | bytes 131072 | tf_op jit(solution)/shard_map/psum | solution.py:56
  10.0 234.1 %all-reduce.9.cloned.1.call-start = ((), (), s32[]{:S(2)}) async-start(), calls=%async_computation.3 | async-start | bytes 131072 | tf_op jit(solution)/shard_map/psum | solution.py:56
  121.7 15.5 %copy-start.8 = (f32[16384]{0:T(1024)S(1)}, f32[16384]{0:T(1024)}, u32[]{:S(2)}) copy-start(f32[16384]{0:T(1024)} %all-reduce.7.cloned.1.call-done) | copy-start | bytes 196612
  138.5 123.8 %copy-start.13 = (bf16[160,256]{1,0:T(8,128)(2,1)S(1)}, bf16[160,256]{1,0:T(8,128)(2,1)}, u32[]{:S(2)}) copy-start(bf16[160,256]{1,0:T(8,128)(2,1)} %param.3) | copy-start | bytes 245764
  138.5 228.2 %all-reduce.11.cloned.1.call-start = ((), (), s32[]{:S(2)}) async-start(), calls=%async_computation.4 | async-start | bytes 131072 | tf_op jit(solution)/shard_map/psum | solution.py:56
  244.1 15.7 %copy-start.14 = (f32[16384]{0:T(1024)S(1)}, f32[16384]{0:T(1024)}, u32[]{:S(2)}) copy-start(f32[16384]{0:T(1024)} %all-reduce.9.cloned.1.call-done) | copy-start | bytes 196612
  261.2 165.3 %all-gather.2.cloned.1.call-start = ((), (), s32[]{:S(2)}) async-start(), calls=%async_computation.1 | async-start | bytes 8650752 | tf_op jit(solution)/shard_map/all_gather | solution.py:40
  261.8 317.4 %all-reduce.13.cloned.1.call-start = ((), (), s32[]{:S(2)}) async-start(), calls=%async_computation.5 | async-start | bytes 327680 | tf_op jit(solution)/shard_map/psum | solution.py:85
  262.5 176.5 %copy-start.20 = (f32[160]{0:T(256)}, f32[160]{0:T(256)S(1)}, u32[]{:S(2)}) copy-start(f32[160]{0:T(256)S(1)} %add_sqrt_fusion.1) | copy-start | bytes 1924
  426.5 5.9 copy-start.1
  439.0 16.8 %copy-start.15 = (f32[16384]{0:T(1024)S(1)}, f32[16384]{0:T(1024)}, u32[]{:S(2)}) copy-start(f32[16384]{0:T(1024)} %all-reduce.11.cloned.1.call-done) | copy-start | bytes 196612
  469.3 1.0 copy-start.12
  476.5 1.0 copy-start.11
  483.6 1.0 copy-start.10
  487.2 3.6 copy-start.16
  487.2 3.6 copy-start.17
  487.2 3.6 copy-start.18
  487.2 3.6 copy-start.19
  487.3 3.6 copy-start.22
  487.3 3.6 copy-start.23
  498.7 6.6 copy-start.3
  498.7 6.6 copy-start.5
  498.7 6.6 copy-start.7
  498.7 9.1 %copy-start.2 = (bf16[160,4096]{1,0:T(8,128)(2,1)}, bf16[160,4096]{1,0:T(8,128)(2,1)S(1)}, u32[]{:S(2)}) copy-start(bf16[160,4096]{1,0:T(8,128)(2,1)S(1)} %get-tuple-element.16) | copy-start | bytes 3932164
  507.8 3.4 copy-start.4
  507.8 3.4 copy-start.6
  507.8 3.4 copy-start.21
  511.2 196.1 %reduce-scatter.2.cloned.1.call-start = ((), (), s32[]{:S(2)}) async-start(), calls=%async_computation.6 | async-start | bytes 17301504 | tf_op jit(solution)/shard_map/reduce_scatter | solution.py:89
  521.1 186.2 %copy-start.9 = (bf16[8,16384]{1,0:T(8,128)(2,1)S(1)}, bf16[8,16384]{1,0:T(8,128)(2,1)}, u32[]{:S(2)}) copy-start(bf16[8,16384]{1,0:T(8,128)(2,1)} %param.4) | copy-start | bytes 786436
  521.2 296.8 %all-reduce.15.cloned.1.call-start = ((), (), s32[]{:S(2)}) async-start(), calls=%async_computation.7 | async-start | bytes 131072 | tf_op jit(solution)/shard_map/psum | solution.py:98
Sparse Core Ops, SparseCore 0:
  11.8 109.7 all-reduce.6
  138.6 105.4 all-reduce.8
  261.3 105.3 all-reduce.10
  369.4 56.9 all-gather.1
  511.3 67.7 all-reduce.12
  583.2 124.0 reduce-scatter.1
  711.2 106.8 all-reduce.14
where the time goes:
time: 828 us
  waiting for transfers between devices  672 us (81%)
  other arithmetic  49.2 us (6%)
  blocking collectives  42.8 us (5%)
  matrix products  30.9 us (4%)
  local copies, waits for them, and re-layouts  17.8 us (2%)
  between operations  14.5 us (2%)
    psum x3, waiting for transfers between devices, shards(): row_total = lax.psum(jnp.sum(teacher_mass, axis=0), 'batch')  321 us
    reduce_scatter x1, waiting for transfers between devices, shards(): lax.psum_scatter(lax.dot_general(unit_bf, grad_all, (((0,), (0,)), ((), (...  127 us
    psum x1, waiting for transfers between devices, shards(): col_dot = lax.psum(jnp.sum(local_weights * weight_term, axis=0), 'batch')  107 us
    all_gather x1, waiting for transfers between devices, shards(): full_weights = lax.all_gather(prototypes, 'batch', axis=0, tiled=True)  58.1 us
    psum x1, waiting for transfers between devices, shards(): unit_total = lax.psum(unit_grad, 'proto')  57.9 us
    psum x3, blocking collectives, shards(): col_total = lax.psum(col_part, 'proto')  42.8 us
  transfers between devices with their start and end apart: 7, of which 7 were waited for; matrix products, arithmetic and copies ran while one was open for 2% of the time, Pallas kernels for 0%

commit v1 on v0

v1 whole, which is shorter than its diff:
```python
import jax
import jax.numpy as jnp
from jax import lax
from jax.sharding import Mesh, PartitionSpec as P

CROPS = 10
GLOBAL = 2
STUDENT_TEMP = 0.1
TEACHER_TEMP = 0.04
PAIRS = float(GLOBAL * CROPS - GLOBAL)
F32 = jnp.float32
BF16 = jnp.bfloat16
PLANE = ("y", "x")
BATCH = ("y", "x", "core")
SWAP = ((0, 1), (1, 0))
SPAN = 250.0
LOW = 125.0
LOG2E = 1.4426950408889634


def normalize_rows(student_feat):
    features = student_feat.astype(F32)
    feat_norm = jnp.sqrt(jnp.sum(features * features, axis=1) + 1e-06)
    unit_vec = features / feat_norm[:, None]
    return (feat_norm, unit_vec, unit_vec.astype(BF16))


def encode_logits(x):
    mag = jnp.exp2(jnp.abs(x) * SPAN - LOW)
    return jnp.where(x < 0, -mag, mag).astype(BF16)


def decode_exp(code):
    v = code.astype(F32)
    mag = (jnp.log2(jnp.abs(v)) + LOW) * (LOG2E / (TEACHER_TEMP * SPAN))
    return jnp.exp2(jnp.where(v < 0, -mag, mag))


def root_code(x):
    y = x * x
    y = y * y
    y = y * y
    return jnp.where(x < 0, -y, y).astype(BF16)


def root_decode(code):
    v = code.astype(F32)
    y = jnp.sqrt(jnp.sqrt(jnp.sqrt(jnp.abs(v))))
    return jnp.where(v < 0, -y, y)


def split(x):
    hi = x.astype(BF16)
    return hi, (x - hi.astype(F32)).astype(BF16)


def dot(a, b, dims):
    return lax.dot_general(a, b, (dims, ((), ())), preferred_element_type=F32)


def shards(student_feat, prototypes, teacher_logits):
    core = lax.axis_index("core")
    feat_norm, unit_vec, unit_bf = normalize_rows(student_feat)

    tc = encode_logits(teacher_logits).reshape(32, 16, 2, 512).transpose(1, 2, 0, 3)
    tc = jnp.where(core == 0, tc, tc[:, ::-1]).reshape(16, 64, 512)
    wc = prototypes.reshape(8, 16, 2, 512).transpose(1, 2, 0, 3).reshape(16, 16, 512)
    st = unit_bf.reshape(2, 80, 256).transpose(1, 0, 2).reshape(1, 80, 512)
    send = jnp.concatenate([tc, wc, jnp.broadcast_to(st, (16, 80, 512))], axis=1)
    got = lax.all_to_all(send, PLANE, 0, 0, tiled=True)
    mate = lax.ppermute(got[:, 32:80], "core", SWAP)

    def by_core(own, other, axis):
        return jnp.stack([jnp.where(core == 0, own, other), jnp.where(core == 0, other, own)], axis=axis)

    mass = decode_exp(by_core(got[:, :32], mate[:, :32], 1).reshape(1024, 512))
    weights = by_core(got[:, 64:80].reshape(16, 2, 8, 512), mate[:, 32:48].reshape(16, 2, 8, 512), 1)
    weights = weights.transpose(0, 1, 3, 2, 4).reshape(256, 1024)
    units = got[:, 80:].reshape(16, 80, 2, 256).transpose(0, 2, 1, 3).reshape(2560, 256)

    wide = weights.astype(F32)
    norm_sq = jnp.sum(wide * wide, axis=0) + 1e-06
    col_scale = 1.0 / (jnp.sqrt(norm_sq) * STUDENT_TEMP)
    my_cols = core * 512
    my_weights = lax.dynamic_slice_in_dim(weights, my_cols, 512, 1)
    my_scale = lax.dynamic_slice_in_dim(col_scale, my_cols, 512, 0)
    my_norm_sq = lax.dynamic_slice_in_dim(norm_sq, my_cols, 512, 0)

    raw = dot(units, weights, ((1,), (0,)))
    prob = jnp.exp2(raw * (col_scale * LOG2E)[None, :])
    exp_part = jnp.sum(prob, axis=1)
    grad_prob = (prob * col_scale[None, :]).astype(BF16)

    grouped = units.reshape(256, CROPS, 256).astype(F32)
    total = jnp.sum(grouped, axis=1, keepdims=True)
    seen = (total - grouped[:, :GLOBAL]).reshape(16, 32, 256)
    seen = by_core(seen, lax.ppermute(seen, "core", SWAP), 1).reshape(1024, 256)

    col_inv = 1.0 / jnp.sum(mass, axis=0)
    row_part = jnp.sum(mass * col_inv[None, :], axis=1)
    pack = jnp.concatenate([row_part, exp_part]).reshape(1, 28, 128)
    came = lax.all_to_all(jnp.broadcast_to(pack, (32, 28, 128)), BATCH, 0, 0, tiled=True).reshape(16, 2, 28, 128)
    row_sum = jnp.sum(came[:, :, :8], axis=(0, 1))
    mine = jnp.where(core == 0, came[:, 0, 8:], came[:, 1, 8:])
    pack = jnp.concatenate([row_sum, jnp.sum(mine, axis=0)], axis=0)
    came = lax.all_to_all(jnp.broadcast_to(pack[None], (8, 28, 128)), "proto", 0, 0, tiled=True)
    came = jnp.sum(came, axis=0)
    row_inv = 1.0 / came[:8].reshape(1024)
    crop = jnp.arange(2560, dtype=jnp.int32) % CROPS
    weight = jnp.where(crop < GLOBAL, GLOBAL - 1, GLOBAL).astype(F32) / PAIRS
    factor = weight / came[8:].reshape(2560)

    col_inv = 1.0 / jnp.sum(mass * row_inv[:, None], axis=0)
    row_part = jnp.sum(mass * col_inv[None, :], axis=1).reshape(4, 256)
    row_part = row_part + lax.ppermute(row_part, "core", SWAP)
    student_part = dot(grad_prob, weights, ((1,), (1,))) * factor[:, None]
    hi, lo = split(row_part)
    rows = jnp.broadcast_to(jnp.concatenate([hi, lo])[None], (16, 8, 256))
    pad = jnp.zeros((16, 8, 256), BF16)
    pack = jnp.concatenate([root_code(student_part * 16384.0).reshape(16, 160, 256), rows, pad], axis=1)
    came = lax.all_to_all(pack, PLANE, 0, 0, tiled=True)
    home = jnp.sum(root_decode(came[:, :160]), axis=0) * (1.0 / 16384.0)
    row_sum = jnp.sum(came[:, 160:168].astype(F32), axis=0)
    row_sum = row_sum[:4] + row_sum[4:]
    pack = jnp.concatenate([home.reshape(8, 20, 256), jnp.broadcast_to(row_sum[None], (8, 4, 256))], axis=1)
    came = jnp.sum(lax.all_to_all(pack, "proto", 0, 0, tiled=True), axis=0)
    home_slice = came[:20]
    row_inv = 1.0 / came[20:].reshape(1024)

    scaled = units.astype(F32) * factor[:, None]
    hi, lo = split(scaled)
    term = dot(hi, grad_prob, ((0,), (0,))) + dot(lo, grad_prob, ((0,), (0,)))
    term = term.reshape(256, 2, 512)
    own = jnp.where(core == 0, term[:, 0], term[:, 1])
    other = jnp.where(core == 0, term[:, 1], term[:, 0])
    term = own + lax.ppermute(other, "core", SWAP)

    col_inv = 1.0 / jnp.sum(mass * row_inv[:, None], axis=0)
    row_part = jnp.sum(mass * col_inv[None, :], axis=1).reshape(4, 256)
    grad_target = (mass * (col_inv * my_scale)[None, :]).astype(BF16)
    target_part = dot(grad_target, my_weights, ((1,), (1,)))
    pack = jnp.concatenate(
        [target_part.reshape(32, 32, 256), jnp.broadcast_to(row_part[None], (32, 4, 256))], axis=1
    )
    came = jnp.sum(lax.all_to_all(pack, BATCH, 0, 0, tiled=True), axis=0)
    pack = jnp.concatenate([came, home_slice], axis=0)
    came = lax.all_to_all(jnp.broadcast_to(pack[None], (8, 56, 256)), "proto", 0, 0, tiled=True)
    student_home = came[:, 36:].reshape(160, 256)
    came = jnp.sum(came[:, :36], axis=0)
    row_inv = 1.0 / came[32:].reshape(1024)

    hi, lo = split(seen * (row_inv * (1.0 / PAIRS))[:, None])
    term = term - dot(hi, grad_target, ((0,), (0,))) - dot(lo, grad_target, ((0,), (0,)))
    my_wide = my_weights.astype(F32)
    col_dot = jnp.sum(my_wide * term, axis=0)
    grad = term - my_wide * (col_dot / my_norm_sq)[None, :]
    grad = lax.all_to_all(grad.reshape(32, 8, 512), BATCH, 0, 0, tiled=True)
    grad_weight = grad.transpose(1, 0, 2).reshape(8, 16384)

    index = lax.axis_index(BATCH)
    home_inv = lax.dynamic_slice_in_dim(row_inv, index * 32, 32, 0)
    target = (came[:32] * (home_inv * (1.0 / PAIRS))[:, None]).reshape(16, GLOBAL, 256)
    both = jnp.sum(target, axis=1, keepdims=True)
    rest = jnp.broadcast_to(both, (16, CROPS - GLOBAL, 256))
    target = jnp.concatenate([both - target, rest], axis=1).reshape(160, 256)
    unit_total = student_home - target
    grad_feat = (unit_total - unit_vec * jnp.sum(unit_vec * unit_total, axis=1, keepdims=True)) / feat_norm[:, None]
    return (grad_feat, grad_weight)


def solution(mesh):
    split_mesh = Mesh(mesh.devices.reshape(4, 4, 2, 8), ("y", "x", "core", "proto"))
    return jax.shard_map(
        shards,
        mesh=split_mesh,
        in_specs=(P(BATCH, None), P(BATCH, "proto"), P(BATCH, "proto")),
        out_specs=(P(BATCH, None), P(BATCH, "proto")),
        check_vma=False,
    )
```

time: 828 us -> 232 us (0.28)
  waiting for transfers between devices: 672 us -> 54.4 us
  starting transfers between devices: 0.29 us -> 39.9 us
  between operations: 14.5 us -> 1.24 us
  blocking collectives: 42.8 us -> 55.3 us
  other arithmetic: 49.2 us -> 37.9 us
    psum x5 -> x0, waiting for transfers between devices: 486 us -> none  [the longest x3 321 us: shards(): row_total = lax.psum(jnp.sum(teacher_mass, axis=0), 'batch')]
    reduce_scatter x1 -> x0, waiting for transfers between devices: 127 us -> none  [shards(): lax.psum_scatter(lax.dot_general(unit_bf, grad_all, (((0,), (0,)), ((), (...]
    all_gather x1 -> x0, waiting for transfers between devices: 58.1 us -> none  [shards(): full_weights = lax.all_gather(prototypes, 'batch', axis=0, tiled=True)]
    all_to_all x0 -> x2, blocking collectives: none -> 55.3 us  [the longest x1 40.4 us: shards(): got = lax.all_to_all(send, PLANE, 0, 0, tiled=True)]
    all_to_all x0 -> x6, waiting for transfers between devices: none -> 54.1 us  [the longest x1 19.8 us: shards(): came = lax.all_to_all(pack, PLANE, 0, 0, tiled=True)]
    psum x3 -> x0, blocking collectives: 42.8 us -> none  [shards(): col_total = lax.psum(col_part, 'proto')]
    all_to_all x0 -> x6, starting transfers between devices: none -> 32.8 us  [the longest x1 8.19 us: shards(): lax.all_to_all(jnp.broadcast_to(pack[None], (8, 28, 128)), 'proto', 0, 0,...]
    reshape x8, local copies, waits for them, and re-layouts: 14.2 us -> 2.8 us  [the longest x2 1.38 us: shards(): encode_logits(teacher_logits).reshape(32, 16, 2, 512).transpose(1, 2, 0, 3)]
  transfers between devices with their start and end apart: 7 -> 10, of which waited for: 7 -> 7; matrix products, arithmetic and copies ran while one was open for 2% -> 19% of each run, Pallas kernels for 0% -> 0%
where the time goes in v1:
time: 232 us; the launch traced here: 231 us
  blocking collectives  55.3 us (24%)
  waiting for transfers between devices  54.4 us (23%)
  starting transfers between devices  39.9 us (17%)
  other arithmetic  37.9 us (16%)
  matrix products  28.5 us (12%)
  local copies, waits for them, and re-layouts  13.3 us (6%)
    all_to_all x1, blocking collectives, shards(): got = lax.all_to_all(send, PLANE, 0, 0, tiled=True)  40.4 us
    dot_general x7, matrix products, dot(): return lax.dot_general(a, b, (dims, ((), ())), preferred_element_type=F32)  28.5 us
    all_to_all x1, waiting for transfers between devices, shards(): came = lax.all_to_all(pack, PLANE, 0, 0, tiled=True)  19.8 us
    all_to_all x1, blocking collectives, shards(): lax.all_to_all(jnp.broadcast_to(pack, (32, 28, 128)), BATCH, 0, 0, tiled=...  14.9 us
    all_to_all x1, waiting for transfers between devices, shards(): came = jnp.sum(lax.all_to_all(pack, BATCH, 0, 0, tiled=True), axis=0)  11.2 us
    all_to_all x1, waiting for transfers between devices, shards(): grad = lax.all_to_all(grad.reshape(32, 8, 512), BATCH, 0, 0, tiled=True)  10.4 us
    all_to_all x1, starting transfers between devices, shards(): lax.all_to_all(jnp.broadcast_to(pack[None], (8, 28, 128)), 'proto', 0, 0,...  8.19 us
    all_to_all x1, waiting for transfers between devices, shards(): lax.all_to_all(jnp.broadcast_to(pack[None], (8, 28, 128)), 'proto', 0, 0,...  7.7 us
  transfers between devices with their start and end apart: 10, of which 7 were waited for; matrix products, arithmetic and copies ran while one was open for 19% of the time, Pallas kernels for 0%

profile of v1, /device:TPU:1, one launch (start us, length us, event | category | flops | bytes accessed | tf_op | source)
XLA Modules:
  0.0 230.6 jit_solution(7187757462132834965)
XLA Ops:
  2.7 2.2 fusion.12
  7.6 40.4 %all_to_all.40 = bf16[16,160,512]{2,1,0:T(8,128)(2,1)S(1)} all-to-all(bf16[16,160,512]{2,1,0:T(8,128)(2,1)S(1)} %pad_maximum_fusion), channel_id=1, replica_groups=mesh['y'=4,'x'=4,'core'=2,'proto'=8] {'y','x'}, dimensions={0} | all-to-all | bytes 5242880 | tf_op jit(solution)/shard_map/all_to_all | solution.py:70
  48.0 2.1 collective-permute-start
  54.1 2.4 %fusion.11 = (f32[16,2,32,512]{3,2,1,0:T(8,128)}, f32[16,2,32]{2,1,0:T(2,128)S(1)}) fusion(bf16[16,1,32,512]{3,2,1,0:T(8,128)(2,1)S(1)} %get-tuple-element.7, bf16[16,1,32,512]{3,2,1,0:T(8,128)(2,1)S(1)} %get-tuple-element.6, f32[512]{0:T(512)S(1)} %broadcast_divide_fusion.2), kind=kLoop, calls=%fused_computation.26 | loop fusion | flops 7339008 | bytes 3151872 | tf_op jit(solution)/shard_map/mul | solution.py:35
  56.6 6.4 %multiply_convert_fusion = (bf16[2560,1024]{0,1:T(8,128)(2,1)}, f32[2560]{0:T(1024)S(1)}) fusion(f32[1024]{0:T(1024)S(1)} %get-tuple-element.22, f32[1024]{0:T(1024)S(1)} %get-tuple-element.23, bf16[2560,256]{1,0:T(8,128)(2,1)} %bitcast.114, bf16[256,1024]{1,0:T(8,128)(2,1)} %bitcast.106), kind=kOutput, calls=%fused_computation | convolution fusion | flops 1355281920 | bytes 7096320 | tf_op jit(solution)/shard_map/dot_general | solution.py:58
  63.1 14.9 %all_to_all.41 = f32[32,28,128]{2,1,0:T(8,128)S(1)} all-to-all(f32[32,28,128]{2,1,0:T(8,128)S(1)} %broadcast_in_dim.34), channel_id=1, replica_groups=mesh['y'=4,'x'=4,'core'=2,'proto'=8] {'y','x','core'}, dimensions={0} | all-to-all | bytes 917504 | tf_op jit(solution)/shard_map/all_to_all | solution.py:102
  79.2 8.2 %all-to-all-start.2 = ((f32[8,28,128]{2,1,0:T(8,128)}), f32[8,28,128]{2,1,0:T(8,128)S(1)}, u32[]{:S(2)}, u32[]{:S(2)}) async-start(f32[8,28,128]{2,1,0:T(8,128)} %broadcast_in_dim.35), calls=%async_computation.2 | async-start | bytes 262144 | tf_op jit(solution)/shard_map/all_to_all | solution.py:106
  87.5 7.7 %all-to-all-done.2 = f32[8,28,128]{2,1,0:T(8,128)S(1)} async-done(((f32[8,28,128]{2,1,0:T(8,128)}), f32[8,28,128]{2,1,0:T(8,128)S(1)}, u32[]{:S(2)}, u32[]{:S(2)}) %all-to-all-start.2) | async-done | bytes 114720 | tf_op jit(solution)/shard_map/all_to_all | solution.py:106
  95.3 2.1 multiply_reduce_fusion.3
  97.4 2.2 multiply_reduce_fusion.2
  99.7 2.3 collective-permute-start.1
  101.9 4.8 %fusion.5 = bf16[2560,256]{1,0:T(8,128)(2,1)S(1)} fusion(bf16[2560,1024]{0,1:T(8,128)(2,1)} %get-tuple-element.4, bf16[256,1024]{1,0:T(8,128)(2,1)} %bitcast.107, f32[2560]{0:T(1024)S(1)} %fusion.39), kind=kOutput, calls=%fused_computation.17 | convolution fusion | flops 1348075520 | bytes 7088128 | tf_op jit(solution)/shard_map/dot_general | solution.py:58
  106.9 1.7 maximum_maximum_fusion
  108.5 4.4 %all-to-all-start.3 = ((bf16[16,176,256]{2,1,0:T(8,128)(2,1)}), bf16[16,176,256]{2,1,0:T(8,128)(2,1)}, u32[]{:S(2)}, u32[]{:S(2)}) async-start(bf16[16,176,256]{2,1,0:T(8,128)(2,1)} %maximum_maximum_fusion), calls=%async_computation.3 | async-start | bytes 2883584 | tf_op jit(solution)/shard_map/all_to_all | solution.py:121
  112.9 2.2 reshape.295
  115.2 2.9 %reduce_sum.211 = f32[256,256]{1,0:T(8,128)S(1)} reduce(f32[256,10,256]{2,1,0:T(8,128)} %reshape.295, f32[]{:T(128)} %constant.29.clone.1), dimensions={1}, to_apply=%region_19.20 | reduce | flops 589824 | bytes 2883588 | tf_op jit(solution)/shard_map/reduce_sum | solution.py:95
  118.1 19.8 %all-to-all-done.3 = bf16[16,176,256]{2,1,0:T(8,128)(2,1)} async-done(((bf16[16,176,256]{2,1,0:T(8,128)(2,1)}), bf16[16,176,256]{2,1,0:T(8,128)(2,1)}, u32[]{:S(2)}, u32[]{:S(2)}) %all-to-all-start.3) | async-done | bytes 1441824 | tf_op jit(solution)/shard_map/all_to_all | solution.py:121
  138.8 3.7 %fusion.6 = f32[160,256]{1,0:T(8,128)S(1)} fusion(bf16[16,176,256]{2,1,0:T(8,128)(2,1)} %all-to-all-done.3), kind=kLoop, calls=%fused_computation.18 | loop fusion | flops 3891200 | bytes 1474560 | tf_op jit(solution)/shard_map/reduce_sum | solution.py:122
  143.2 3.4 %all-to-all-start.4 = ((f32[8,24,256]{2,1,0:T(8,128)}), f32[8,24,256]{2,1,0:T(8,128)S(1)}, u32[]{:S(2)}, u32[]{:S(2)}) async-start(f32[8,24,256]{2,1,0:T(8,128)} %pad_maximum_fusion.5), calls=%async_computation.4 | async-start | bytes 393216 | tf_op jit(solution)/shard_map/all_to_all | solution.py:126
  146.6 1.9 slice_subtract_fusion
  151.7 4.1 %all-to-all-done.4 = f32[8,24,256]{2,1,0:T(8,128)S(1)} async-done(((f32[8,24,256]{2,1,0:T(8,128)}), f32[8,24,256]{2,1,0:T(8,128)S(1)}, u32[]{:S(2)}, u32[]{:S(2)}) %all-to-all-start.4) | async-done | bytes 196640 | tf_op jit(solution)/shard_map/all_to_all | solution.py:126
  161.0 5.8 %all-to-all-start.5 = ((f32[32,36,256]{2,1,0:T(8,128)}), f32[32,36,256]{2,1,0:T(8,128)S(1)}, u32[]{:S(2)}, u32[]{:S(2)}) async-start(f32[32,36,256]{2,1,0:T(8,128)} %pad_maximum_fusion.1), calls=%async_computation.5 | async-start | bytes 2621440 | tf_op jit(solution)/shard_map/all_to_all | solution.py:145
  166.8 2.4 %select_bitcast_fusion.1 = (f32[16,1,32,256]{3,2,1,0:T(8,128)}, f32[16,1,32,256]{3,2,1,0:T(8,128)}) fusion(f32[16,32,256]{2,1,0:T(8,128)} %reshape.290, f32[16,32,256]{2,1,0:T(8,128)} %collective-permute-done.3, pred[]{:T(512)S(6)} %eq.3), kind=kLoop, calls=%fused_computation.71 | loop fusion | flops 262144 | bytes 2097153 | tf_op jit(solution)/shard_map/stack | solution.py:74
  169.3 5.5 %fusion.19 = f32[256,1024]{1,0:T(8,128)} fusion(bf16[2560,1024]{0,1:T(8,128)(2,1)} %get-tuple-element.4, bf16[2560,256]{1,0:T(8,128)(2,1)S(1)} %bitcast.116, f32[2560]{0:T(1024)S(1)} %fusion.39), kind=kOutput, calls=%fused_computation.40 | convolution fusion | flops 1344143360 | bytes 7612416 | tf_op jit(solution)/shard_map/dot_general | solution.py:58
  174.8 11.2 %all-to-all-done.5 = f32[32,36,256]{2,1,0:T(8,128)S(1)} async-done(((f32[32,36,256]{2,1,0:T(8,128)}), f32[32,36,256]{2,1,0:T(8,128)S(1)}, u32[]{:S(2)}, u32[]{:S(2)}) %all-to-all-start.5) | async-done | bytes 1179680 | tf_op jit(solution)/shard_map/all_to_all | solution.py:145
  186.9 3.5 %all-to-all-start.6 = ((f32[8,56,256]{2,1,0:T(8,128)}), f32[8,56,256]{2,1,0:T(8,128)S(1)}, u32[]{:S(2)}, u32[]{:S(2)}) async-start(f32[8,56,256]{2,1,0:T(8,128)} %broadcast_in_dim.41), calls=%async_computation.6 | async-start | bytes 917504 | tf_op jit(solution)/shard_map/all_to_all | solution.py:147
  190.4 6.2 %fusion.24 = f32[256,1024]{1,0:T(8,128)} fusion(f32[256,1024]{1,0:T(8,128)} %fusion.19, bf16[2560,1024]{0,1:T(8,128)(2,1)} %get-tuple-element.4, bf16[2560,256]{1,0:T(8,128)(2,1)} %bitcast.115, f32[2560]{0:T(1024)S(1)} %fusion.39), kind=kOutput, calls=%fused_computation.49 | convolution fusion | flops 1346371584 | bytes 8660992 | tf_op jit(solution)/shard_map/dot_general | solution.py:58
  201.3 2.0 collective-permute-start.2
  204.6 2.5 %convolution_bitcast_fusion.1 = f32[256,512]{1,0:T(8,128)S(1)} fusion(f32[16,1,32,256]{3,2,1,0:T(8,128)} %get-tuple-element.15, f32[16,1,32,256]{3,2,1,0:T(8,128)S(1)} %copy-done.8, f32[16,2,32]{2,1,0:T(2,128)S(1)} %mul.297, f32[512]{0:T(512)S(1)} %get-tuple-element.24, bf16[16,1,32,512]{3,2,1,0:T(8,128)(2,1)S(1)} %copy-done.2, ...), kind=kOutput, calls=%fused_computation.51 | convolution fusion | flops 276561920 | bytes 2627584 | tf_op jit(solution)/shard_map/dot_general | solution.py:58
  207.1 2.6 %fusion.27 = (f32[512]{0:T(512)S(1)}, f32[256,512]{1,0:T(8,128)S(1)}) fusion(bf16[256,1024]{1,0:T(8,128)(2,1)S(1)} %bitcast.109, s32[]{:T(128)S(6)} %select_n.164, f32[512]{0:T(512)S(1)} %get-tuple-element.24, bf16[16,1,32,512]{3,2,1,0:T(8,128)(2,1)S(1)} %copy-done.2, bf16[16,1,32,512]{3,2,1,0:T(8,128)(2,1)S(1)} %get-tuple-element.6, ...), kind=kOutput, calls=%fused_computation.60 | convolution fusion | flops 278265344 | bytes 4988933 | tf_op jit(solution)/shard_map/dot_general | solution.py:58
  210.7 7.6 %all-to-all-start.7 = ((f32[32,8,512]{2,1,0:T(8,128)}), f32[32,8,512]{2,1,0:T(8,128)S(1)}, u32[]{:S(2)}, u32[]{:S(2)}) async-start(f32[32,8,512]{2,1,0:T(8,128)} %fusion.29), calls=%async_computation.7 | async-start | bytes 1048576 | tf_op jit(solution)/shard_map/all_to_all | solution.py:157
  219.4 10.4 %all-to-all-done.7 = f32[32,8,512]{2,1,0:T(8,128)S(1)} async-done(((f32[32,8,512]{2,1,0:T(8,128)}), f32[32,8,512]{2,1,0:T(8,128)S(1)}, u32[]{:S(2)}, u32[]{:S(2)}) %all-to-all-start.7) | async-done | bytes 524320 | tf_op jit(solution)/shard_map/all_to_all | solution.py:157
  (116 shorter events, 30.1 us)
Async XLA Ops:
  6.4 1.0 copy-start.10
  48.0 4.0 %collective-permute-start = (bf16[16,48,512]{2,1,0:T(8,128)(2,1)S(1)}, bf16[16,48,512]{2,1,0:T(8,128)(2,1)S(1)}, u32[]{:S(2)}, u32[]{:S(2)}) collective-permute-start(bf16[16,48,512]{2,1,0:T(8,128)(2,1)S(1)} %slice.99), channel_id=1, source_target_pairs={{0,8},{8,0},{1,9},{9,1},{2,10},{10,2},{3,11},{11,3},{4,12},{12,4},... | collective-permute-start | bytes 2359304 | tf_op jit(solution)/shard_map/ppermute | solution.py:71
  53.1 3.4 %copy-start.1 = (bf16[16,1,32,512]{3,2,1,0:T(8,128)(2,1)}, bf16[16,1,32,512]{3,2,1,0:T(8,128)(2,1)S(1)}, u32[]{:S(2)}) copy-start(bf16[16,1,32,512]{3,2,1,0:T(8,128)(2,1)S(1)} %get-tuple-element.7) | copy-start | bytes 1572868
  79.2 16.0 %all-to-all-start.2 = ((f32[8,28,128]{2,1,0:T(8,128)}), f32[8,28,128]{2,1,0:T(8,128)S(1)}, u32[]{:S(2)}, u32[]{:S(2)}) async-start(f32[8,28,128]{2,1,0:T(8,128)} %broadcast_in_dim.35), calls=%async_computation.2 | async-start | bytes 262144 | tf_op jit(solution)/shard_map/all_to_all | solution.py:106
  99.7 7.1 %collective-permute-start.1 = (f32[4,256]{1,0:T(4,128)S(1)}, f32[4,256]{1,0:T(4,128)S(1)}, u32[]{:S(2)}, u32[]{:S(2)}) collective-permute-start(f32[4,256]{1,0:T(4,128)S(1)} %reshape.285), channel_id=1, source_target_pairs={{0,8},{8,0},{1,9},{9,1},{2,10},{10,2},{3,11},{11,3},{4,12},{12,4},... | collective-permute-start | bytes 12296 | tf_op jit(solution)/shard_map/ppermute | solution.py:115
  108.5 29.4 %all-to-all-start.3 = ((bf16[16,176,256]{2,1,0:T(8,128)(2,1)}), bf16[16,176,256]{2,1,0:T(8,128)(2,1)}, u32[]{:S(2)}, u32[]{:S(2)}) async-start(bf16[16,176,256]{2,1,0:T(8,128)(2,1)} %maximum_maximum_fusion), calls=%async_computation.3 | async-start | bytes 2883584 | tf_op jit(solution)/shard_map/all_to_all | solution.py:121
  142.5 8.0 %copy-start.2 = (bf16[16,1,32,512]{3,2,1,0:T(8,128)(2,1)S(1)}, bf16[16,1,32,512]{3,2,1,0:T(8,128)(2,1)}, u32[]{:S(2)}) copy-start(bf16[16,1,32,512]{3,2,1,0:T(8,128)(2,1)} %copy-done.1) | copy-start | bytes 1572868
  143.2 12.5 %all-to-all-start.4 = ((f32[8,24,256]{2,1,0:T(8,128)}), f32[8,24,256]{2,1,0:T(8,128)S(1)}, u32[]{:S(2)}, u32[]{:S(2)}) async-start(f32[8,24,256]{2,1,0:T(8,128)} %pad_maximum_fusion.5), calls=%async_computation.4 | async-start | bytes 393216 | tf_op jit(solution)/shard_map/all_to_all | solution.py:126
  149.7 17.1 %collective-permute-start.3 = (f32[16,32,256]{2,1,0:T(8,128)}, f32[16,32,256]{2,1,0:T(8,128)}, u32[]{:S(2)}, u32[]{:S(2)}) collective-permute-start(f32[16,32,256]{2,1,0:T(8,128)} %reshape.290), channel_id=1, source_target_pairs={{0,8},{8,0},{1,9},{9,1},{2,10},{10,2},{3,11},{11,3},{4,12},{12,4},... | collective-permute-start | bytes 1572872 | tf_op jit(solution)/shard_map/ppermute | solution.py:97
  151.7 6.4 %copy-start = (f32[16,2,32,512]{3,2,1,0:T(8,128)S(1)}, f32[16,2,32,512]{3,2,1,0:T(8,128)}, u32[]{:S(2)}) copy-start(f32[16,2,32,512]{3,2,1,0:T(8,128)} %get-tuple-element.16) | copy-start | bytes 6291460
  155.9 2.3 copy-start.3
  158.1 1.0 copy-start.4
  161.0 25.0 %all-to-all-start.5 = ((f32[32,36,256]{2,1,0:T(8,128)}), f32[32,36,256]{2,1,0:T(8,128)S(1)}, u32[]{:S(2)}, u32[]{:S(2)}) async-start(f32[32,36,256]{2,1,0:T(8,128)} %pad_maximum_fusion.1), calls=%async_computation.5 | async-start | bytes 2621440 | tf_op jit(solution)/shard_map/all_to_all | solution.py:145
  166.8 2.5 %copy-start.6 = (bf16[16,80,2,256]{3,1,2,0:T(8,128)(2,1)S(1)}, bf16[16,80,2,256]{3,1,2,0:T(8,128)(2,1)}, u32[]{:S(2)}) copy-start(bf16[16,80,2,256]{3,1,2,0:T(8,128)(2,1)} %get-tuple-element.11) | copy-start | bytes 3932164
  186.9 17.3 %all-to-all-start.6 = ((f32[8,56,256]{2,1,0:T(8,128)}), f32[8,56,256]{2,1,0:T(8,128)S(1)}, u32[]{:S(2)}, u32[]{:S(2)}) async-start(f32[8,56,256]{2,1,0:T(8,128)} %broadcast_in_dim.41), calls=%async_computation.6 | async-start | bytes 917504 | tf_op jit(solution)/shard_map/all_to_all | solution.py:147
  200.4 4.2 %copy-start.8 = (f32[16,1,32,256]{3,2,1,0:T(8,128)S(1)}, f32[16,1,32,256]{3,2,1,0:T(8,128)}, u32[]{:S(2)}) copy-start(f32[16,1,32,256]{3,2,1,0:T(8,128)} %get-tuple-element.14) | copy-start | bytes 1572868
  201.3 5.8 %collective-permute-start.2 = (f32[256,512]{1,0:T(8,128)}, f32[256,512]{1,0:T(8,128)}, u32[]{:S(2)}, u32[]{:S(2)}) collective-permute-start(f32[256,512]{1,0:T(8,128)} %select_bitcast_fusion.2), channel_id=1, source_target_pairs={{0,8},{8,0},{1,9},{9,1},{2,10},{10,2},{3,11},{11,3},{4,12},{12,4},... | collective-permute-start | bytes 1572872 | tf_op jit(solution)/shard_map/ppermute | solution.py:136
  204.6 2.5 %copy-start.5 = (bf16[16,2,2,8,512]{4,3,2,1,0:T(8,128)(2,1)S(1)}, bf16[16,2,2,8,512]{4,3,2,1,0:T(8,128)(2,1)}, u32[]{:S(2)}) copy-start(bf16[16,2,2,8,512]{4,3,2,1,0:T(8,128)(2,1)} %pad_maximum_fusion.3) | copy-start | bytes 1572868
  204.6 2.5 %copy-start.9 = (f32[16,1,32,256]{3,2,1,0:T(8,128)S(1)}, f32[16,1,32,256]{3,2,1,0:T(8,128)}, u32[]{:S(2)}) copy-start(f32[16,1,32,256]{3,2,1,0:T(8,128)} %get-tuple-element.15) | copy-start | bytes 1572868
  209.7 8.7 %copy-start.7 = (bf16[160,256]{1,0:T(8,128)(2,1)S(1)}, bf16[160,256]{1,0:T(8,128)(2,1)}, u32[]{:S(2)}) copy-start(bf16[160,256]{1,0:T(8,128)(2,1)} %param.3) | copy-start | bytes 245764
  210.7 19.1 %all-to-all-start.7 = ((f32[32,8,512]{2,1,0:T(8,128)}), f32[32,8,512]{2,1,0:T(8,128)S(1)}, u32[]{:S(2)}, u32[]{:S(2)}) async-start(f32[32,8,512]{2,1,0:T(8,128)} %fusion.29), calls=%async_computation.7 | async-start | bytes 1048576 | tf_op jit(solution)/shard_map/all_to_all | solution.py:157

commit v2 on v1

v2 whole, which is shorter than its diff:
```python
import jax
import jax.numpy as jnp
from jax import lax
from jax.experimental import pallas as pl
from jax.experimental.pallas import tpu as pltpu
from jax.sharding import Mesh, PartitionSpec as P

CROPS = 10
GLOBAL = 2
STUDENT_TEMP = 0.1
TEACHER_TEMP = 0.04
PAIRS = float(GLOBAL * CROPS - GLOBAL)
F32 = jnp.float32
BF16 = jnp.bfloat16
PLANE = ("y", "x")
BATCH = ("y", "x", "core")
SWAP = ((0, 1), (1, 0))
SPAN = 250.0
LOW = 125.0
LOG2E = 1.4426950408889634
ROOT = 3276.8
WIDE = 16384.0
TINY = 1e-38


def encode_logits(x):
    mag = jnp.exp2(jnp.abs(x) * SPAN - LOW)
    return jnp.where(x < 0, -mag, mag).astype(BF16)


def decode_exp(code):
    v = code.astype(F32)
    mag = (jnp.log2(jnp.abs(v)) + LOW) * (LOG2E / (TEACHER_TEMP * SPAN))
    return jnp.exp2(jnp.where(v < 0, -mag, mag))


def root_code(x):
    y = x * x
    y = y * y
    return jnp.where(x < 0, -y, y)


def root_decode(code):
    v = code.astype(F32)
    y = lax.rsqrt(lax.rsqrt(jnp.abs(v) + TINY))
    return jnp.where(v < 0, -y, y)


def fine_code(x):
    y = x * x
    y = y * y
    y = y * y
    return jnp.where(x < 0, -y, y)


def fine_decode(code):
    v = code.astype(F32)
    y = jnp.sqrt(lax.rsqrt(lax.rsqrt(jnp.abs(v) + TINY)))
    return jnp.where(v < 0, -y, y)


def sum_code(x):
    y = x * (1.0 / 1024.0)
    y = y * y
    y = y * y
    return y * y


def sum_decode(code):
    return jnp.sqrt(lax.rsqrt(lax.rsqrt(code.astype(F32)))) * 1024.0


def split(x):
    hi = x.astype(BF16)
    return hi, (x - hi.astype(F32)).astype(BF16)


def dot(a, b, dims):
    return lax.dot_general(a, b, (dims, ((), ())), preferred_element_type=F32)


NN = ((1,), (0,))
NT = ((1,), (1,))
TN = ((0,), (0,))


def lanes(x8):
    return jnp.concatenate([x8[i : i + 1] for i in range(8)], axis=1)


def rows8(x):
    return jnp.concatenate([x[:, 128 * i : 128 * (i + 1)] for i in range(8)], axis=0)


def split_row(x8):
    hi = x8.astype(BF16).astype(F32)
    return jnp.concatenate([hi, x8 - hi], axis=1)


def join_row(x):
    return x[:, :128] + x[:, 128:]


def padded(x8):
    return jnp.concatenate([x8, jnp.zeros_like(x8)], axis=0).astype(BF16)


def sweep(mass_ref, row_inv, keep_ref=None, copies=None):
    total = jnp.zeros((8, 1024), F32)
    for low in range(0, 512, 32):
        if copies is not None and low % 128 == 0:
            copies[low // 128].wait()
        x = mass_ref[low : low + 32, :]
        y = x if row_inv is None else x * row_inv
        x = x * (1.0 / jnp.sum(y, axis=1, keepdims=True))
        if keep_ref is not None:
            keep_ref[low : low + 32, :] = x.astype(BF16)
        total = total + ((x[:8] + x[8:16]) + (x[16:24] + x[24:]))
    return jnp.sum(total, axis=0, keepdims=True)


def pack_kernel(core_ref, teacher_ref, proto_ref, feat_ref, out_ref, unit_ref):
    first = core_ref[0] == 0

    @pl.when(pl.program_id(0) == 0)
    def _():
        x = feat_ref[...].astype(F32)
        unit = x / jnp.sqrt(jnp.sum(x * x, axis=1, keepdims=True) + 1e-06)
        unit = unit.astype(BF16)
        unit_ref[:, :256] = unit[:80]
        unit_ref[:, 256:] = unit[80:]

    for p in range(4):
        left = encode_logits(teacher_ref[:, 1024 * p : 1024 * p + 512])
        right = encode_logits(teacher_ref[:, 1024 * p + 512 : 1024 * p + 1024])
        out_ref[p, 0:32, :] = jnp.where(first, left, right)
        out_ref[p, 32:64, :] = jnp.where(first, right, left)
        w = proto_ref[:, 1024 * p : 1024 * p + 1024].astype(F32)
        out_ref[p, 64:80, :] = jnp.concatenate([w[:, :512], w[:, 512:]], axis=0).astype(BF16)
        out_ref[p, 80:160, :] = unit_ref[...]


def first_kernel(core_ref, own_ref, mate_ref, mass_ref, out_ref):
    first = core_ref[0] == 0
    for j in range(4):
        own = decode_exp(own_ref[4 * j : 4 * j + 4].reshape(128, 512)).T
        mate = decode_exp(mate_ref[4 * j : 4 * j + 4].reshape(128, 512)).T
        mass_ref[:, 128 * j : 128 * j + 128] = jnp.where(first, own, mate)
        mass_ref[:, 512 + 128 * j : 640 + 128 * j] = jnp.where(first, mate, own)
    part = rows8(sweep(mass_ref, None))
    out_ref[...] = jnp.broadcast_to(part[None], (32, 8, 128))


def fetch(mass_hbm, mass_ref, sems):
    copies = [
        pltpu.make_async_copy(
            mass_hbm.at[pl.ds(128 * i, 128), :], mass_ref.at[pl.ds(128 * i, 128), :], sems.at[i]
        )
        for i in range(4)
    ]
    for copy in copies:
        copy.start()
    return copies


def second_kernel(came_ref, mass_hbm, out_ref, mass_ref, sems):
    copies = fetch(mass_hbm, mass_ref, sems)
    row_inv = lanes(1.0 / jnp.sum(came_ref[...], axis=0))
    out_ref[...] = rows8(sweep(mass_ref, row_inv, copies=copies))


def insert_kernel(own_ref, mate_ref, pack_ref, out_ref):
    row = padded(split_row(own_ref[...] + mate_ref[...]))
    out_ref[...] = jnp.broadcast_to(row[None], (16, 16, 256))


def home_kernel(place_ref, came_ref, out_ref, home_ref, exp_ref, row_ref, part_ref):
    step = pl.program_id(0)

    @pl.when(step == 0)
    def _():
        home_ref[...] = jnp.zeros_like(home_ref)
        exp_ref[...] = jnp.zeros_like(exp_ref)
        row_ref[...] = jnp.zeros_like(row_ref)
        part_ref[...] = jnp.zeros_like(part_ref)

    pick = lax.broadcasted_iota(jnp.int32, (16, 256), 0) == place_ref[0]
    exp_sum = exp_ref[...]
    row_sum = row_ref[...]
    parts = []
    for p in range(4):
        exp_part = sum_decode(came_ref[p, 160:176, :])
        exp_sum = exp_sum + exp_part
        row_sum = row_sum + came_ref[p, 176:192, :].astype(F32)[:8]
        parts.append(jnp.sum(jnp.where(pick, exp_part, 0.0), axis=0, keepdims=True))
    exp_ref[...] = exp_sum
    row_ref[...] = row_sum
    parts = columns(jnp.concatenate(parts + [jnp.zeros((4, 256), F32)], axis=0) * (1.0 / ROOT))
    part_ref[...] += jnp.sum(parts, axis=1, keepdims=True)
    for low in range(0, 160, 32):
        home = home_ref[low : low + 32, :]
        for p in range(4):
            home = home + root_decode(came_ref[p, low : low + 32, :]) * parts[low : low + 32, p : p + 1]
        home_ref[low : low + 32, :] = home

    @pl.when(step == 3)
    def _():
        code = fine_code(home_ref[...] / part_ref[:160, :1])
        tail = [jnp.zeros((4, 256), F32), split_row(join_row(row_ref[...])), sum_code(exp_ref[...] * (1.0 / 16.0))]
        for z in range(8):
            out_ref[z] = jnp.concatenate([code[20 * z : 20 * z + 20]] + tail, axis=0).astype(BF16)


def slice_kernel(place_ref, came_ref, out_ref):
    pick = lax.broadcasted_iota(jnp.int32, (16, 256), 0) == place_ref[0]
    parts = []
    for p in range(8):
        exp_part = sum_decode(came_ref[p, 32:48, :]) * 16.0
        parts.append(jnp.sum(jnp.where(pick, exp_part, 0.0), axis=0, keepdims=True))
    parts = pltpu.roll(jnp.concatenate(parts, axis=0), (256 - 20 * place_ref[1]) % 256, 1)
    parts = columns(parts)[:32]
    home = jnp.zeros((32, 256), F32)
    for p in range(8):
        home = home + fine_decode(came_ref[p, 0:32, :]) * parts[:, p : p + 1]
    row = lax.broadcasted_iota(jnp.int32, (32, 1), 0)
    weight = jnp.where(row % CROPS < GLOBAL, (GLOBAL - 1) / PAIRS, GLOBAL / PAIRS) * (WIDE / ROOT)
    out_ref[...] = fine_code(home * (weight / jnp.sum(parts, axis=1, keepdims=True)))[:24]


def third_kernel(came_ref, mass_ref, hi_ref, lo_ref, keep_ref, out_ref):
    rows = came_ref[0, 16:32, :].astype(F32)
    for p in range(1, 8):
        rows = rows + came_ref[p, 16:32, :].astype(F32)
    row_inv = lanes(1.0 / join_row(rows[8:]))
    part = sweep(mass_ref, row_inv, keep_ref)
    scale = ROOT / part
    for j in range(8):
        keep = keep_ref[:, 128 * j : 128 * j + 128]
        x = jnp.dot(hi_ref[...], keep, preferred_element_type=F32)
        x = x + jnp.dot(lo_ref[...], keep, preferred_element_type=F32)
        x = (x * scale[:, 128 * j : 128 * j + 128]).T
        x = root_code(x).astype(BF16)
        for i in range(4):
            block = 4 * j + i
            out_ref[block % 16 * 2 + block // 16, 0:32, :] = x[32 * i : 32 * i + 32]
    out_ref[:, 32:48, :] = jnp.broadcast_to(padded(split_row(rows8(part)))[None], (32, 16, 256))


def target_kernel(index_ref, came_ref, slice_ref, out_ref, turn_ref):
    index = index_ref[0]
    pick = lax.broadcasted_iota(jnp.int32, (8, 128), 0) == index // 4
    row_sum = jnp.zeros((8, 128), F32)
    parts = []
    for p in range(32):
        row = join_row(came_ref[p, 32:48, :].astype(F32)[:8])
        row_sum = row_sum + row
        parts.append(jnp.sum(jnp.where(pick, row, 0.0), axis=0, keepdims=True))
    parts = jnp.concatenate(parts, axis=0) * (1.0 / ROOT)
    turn_ref[...] = jnp.concatenate([parts, jnp.zeros((96, 128), F32)], axis=0).T
    parts = turn_ref[pl.ds(pl.multiple_of(index % 4 * 32, 32), 32), :]
    total = jnp.zeros((32, 256), F32)
    for p in range(32):
        total = total + root_decode(came_ref[p, 0:32, :]) * parts[:, p : p + 1]
    code = fine_code(total / jnp.sum(parts, axis=1, keepdims=True))
    code = jnp.concatenate([code, slice_ref[...], split_row(row_sum)], axis=0).astype(BF16)
    out_ref[...] = jnp.broadcast_to(code[None], (8, 64, 256))


def feat_kernel(index_ref, came_ref, feat_ref, out_ref, turn_ref):
    index = index_ref[0]
    pick = lax.broadcasted_iota(jnp.int32, (8, 128), 0) == index // 4
    parts = []
    for p in range(8):
        row = join_row(came_ref[p, 48:64, :].astype(F32)[8:])
        parts.append(jnp.sum(jnp.where(pick, row, 0.0), axis=0, keepdims=True))
    parts = jnp.concatenate(parts + [jnp.zeros((120, 128), F32)], axis=0)
    turn_ref[...] = parts.T
    parts = turn_ref[pl.ds(pl.multiple_of(index % 4 * 32, 32), 32), :]
    target = jnp.zeros((32, 256), F32)
    for p in range(8):
        target = target + fine_decode(came_ref[p, 0:32, :]) * parts[:, p : p + 1]
    target = target / jnp.sum(parts, axis=1, keepdims=True) * (1.0 / (ROOT * PAIRS))
    hi, lo = split(target)
    row = lax.broadcasted_iota(jnp.int32, (160, 32), 0)
    col = lax.broadcasted_iota(jnp.int32, (160, 32), 1)
    keep = jnp.where((row // CROPS == col // GLOBAL) & (row % CROPS != col % GLOBAL), 1.0, 0.0).astype(BF16)
    student = [fine_decode(came_ref[p, 32:64, :])[:20] for p in range(8)]
    total = jnp.concatenate(student, axis=0) * (1.0 / WIDE) - (dot(keep, hi, NN) + dot(keep, lo, NN))
    x = feat_ref[...].astype(F32)
    norm = jnp.sqrt(jnp.sum(x * x, axis=1, keepdims=True) + 1e-06)
    unit = x / norm
    out_ref[...] = (total - unit * jnp.sum(unit * total, axis=1, keepdims=True)) / norm


def final_kernel(
    core_ref, came_ref, keep_ref, seen_ref, mate_ref, term_ref, term_mate_ref, weight_ref, scale_ref, inv_ref, out_ref,
    hi_ref, lo_ref,
):
    @pl.when(pl.program_id(0) == 0)
    def _():
        first = core_ref[0] == 0
        rows = came_ref[0, 48:64, :].astype(F32)
        for p in range(1, 8):
            rows = rows + came_ref[p, 48:64, :].astype(F32)
        row_inv = lanes(1.0 / join_row(rows[8:])) * (1.0 / PAIRS)
        seen = seen_ref[...]
        mate = mate_ref[...]
        hi_ref[:, :512], lo_ref[:, :512] = split(jnp.where(first, seen, mate) * row_inv[:, :512])
        hi_ref[:, 512:], lo_ref[:, 512:] = split(jnp.where(first, mate, seen) * row_inv[:, 512:])

    keep = keep_ref[...]
    x = dot(hi_ref[...], keep, NT) + dot(lo_ref[...], keep, NT)
    x = term_ref[...] + term_mate_ref[...] - x * scale_ref[...]
    w = weight_ref[...].astype(F32)
    dots = jnp.sum(w * x, axis=0, keepdims=True) * inv_ref[...]
    out_ref[...] = x - w * dots


def columns(x):
    return jnp.concatenate([x, jnp.zeros((120, 256), F32)], axis=0).T


def exp_kernel(
    core_ref, own_ref, mate_ref, unit_ref, out_ref, sum_ref, all_ref, my_ref, my_scale_ref, my_inv_ref, hi_ref, lo_ref,
    scale_ref,
):
    step = pl.program_id(0)

    @pl.when(step == 0)
    def _():
        first = core_ref[0] == 0
        squares = jnp.zeros((8, 1024), F32)
        for p in range(16):
            own = own_ref[p].astype(F32)
            mate = mate_ref[p].astype(F32)
            low = jnp.where(first, own, mate)
            high = jnp.where(first, mate, own)
            left = jnp.concatenate([low[:8], high[:8]], axis=0)
            right = jnp.concatenate([low[8:], high[8:]], axis=0)
            rows = slice(16 * p, 16 * p + 16)
            all_ref[rows, :512] = left.astype(BF16)
            all_ref[rows, 512:] = right.astype(BF16)
            my_ref[rows, :] = jnp.where(first, left, right).astype(BF16)
            both = jnp.concatenate([left, right], axis=1)
            both = both * both
            squares = squares + (both[:8] + both[8:])
        norm_sq = jnp.sum(squares, axis=0, keepdims=True) + 1e-06
        scale = 1.0 / (jnp.sqrt(norm_sq) * STUDENT_TEMP)
        scale_ref[...] = scale
        my_inv_ref[...] = 1.0 / jnp.where(first, norm_sq[:, :512], norm_sq[:, 512:])
        my_scale = jnp.where(first, scale[:, :512], scale[:, 512:])
        my_scale_ref[...] = my_scale
        for p in range(8):
            rows = slice(32 * p, 32 * p + 32)
            hi, lo = split(my_ref[rows, :].astype(F32) * my_scale)
            hi_ref[rows, :] = hi
            lo_ref[rows, :] = lo

    scale = scale_ref[...]
    power = scale * LOG2E
    sums = []
    for p in range(4):
        for half in range(2):
            raw = dot(unit_ref[p, :, 256 * half : 256 * half + 256], all_ref[...], NN)
            prob = jnp.exp2(raw * power)
            sums.append(jnp.sum(prob, axis=1, keepdims=True))
            out_ref[160 * p + 80 * half : 160 * p + 80 * half + 80, :] = (prob * scale).astype(BF16)
    sums = [jnp.concatenate(sums[2 * p : 2 * p + 2], axis=0) for p in range(4)]
    sums = jnp.concatenate(sums + [jnp.ones((160, 124), F32)], axis=1)
    sums = jnp.concatenate([sums, jnp.ones((96, 128), F32)], axis=0).T[:4]
    row = lax.broadcasted_iota(jnp.int32, (16, 256), 0)
    sum_ref[...] = jnp.where(row // 4 == step, jnp.concatenate([sums] * 4, axis=0), sum_ref[...])


def student_kernel(grad_ref, weight_ref, part_ref, sum_ref, out_ref):
    scale = columns(ROOT / part_ref[...])
    sums = sum_code(sum_ref[...]).astype(BF16)
    for p in range(8):
        x = dot(grad_ref[160 * p : 160 * p + 160, :], weight_ref[...], NT)
        out_ref[p, 0:160, :] = root_code(x * scale[:160, p : p + 1]).astype(BF16)
        out_ref[p, 160:176, :] = sums


def seen_kernel(unit_ref, out_ref):
    row = lax.broadcasted_iota(jnp.int32, (32, 80), 0)
    col = lax.broadcasted_iota(jnp.int32, (32, 80), 1)
    keep = (col // CROPS == row // GLOBAL) & (col % CROPS != row % GLOBAL)
    after = (col // CROPS + 80 // CROPS == row // GLOBAL) & (col % CROPS != row % GLOBAL)
    keep = jnp.where(keep, 1.0, 0.0).astype(BF16)
    after = jnp.where(after, 1.0, 0.0).astype(BF16)
    for j in range(4):
        block = [
            dot(keep, unit_ref[p, :, :256], NN) + dot(after, unit_ref[p, :, 256:], NN)
            for p in range(4 * j, 4 * j + 4)
        ]
        out_ref[:, 128 * j : 128 * j + 128] = jnp.concatenate(block, axis=0).T


def term_kernel(core_ref, unit_ref, grad_ref, came_ref, own_ref, other_ref, total_ref):
    step = pl.program_id(0)
    first = core_ref[0] == 0
    exp_sum = sum_decode(came_ref[0, 32:48, :])
    for p in range(1, 8):
        exp_sum = exp_sum + sum_decode(came_ref[p, 32:48, :])
    exp_sum = jnp.where(step == 0, exp_sum[:8], exp_sum[8:]) * 16.0
    row = lax.broadcasted_iota(jnp.int32, (8, 256), 1)
    weight = jnp.where(row % CROPS < GLOBAL, (GLOBAL - 1) / PAIRS, GLOBAL / PAIRS)
    factor = columns(jnp.where(row < 160, weight / exp_sum, 0.0))
    for j in range(2):
        parts = []
        for p in range(4 * j, 4 * j + 4):
            unit = jnp.concatenate([unit_ref[p, :, :256], unit_ref[p, :, 256:]], axis=0).astype(F32)
            parts.append(unit * factor[:160, p : p + 1])
        hi, lo = split(jnp.concatenate(parts, axis=0))
        grad = grad_ref[640 * j : 640 * j + 640, :]
        x = dot(hi, grad, TN) + dot(lo, grad, TN)
        if j == 0:
            total_ref[...] = x + jnp.where(step == 0, 0.0, total_ref[...])
        else:
            total_ref[...] += x

    @pl.when(step == 1)
    def _():
        left = total_ref[:, :512]
        right = total_ref[:, 512:]
        own_ref[...] = jnp.where(first, left, right)
        other_ref[...] = jnp.where(first, right, left)


VMEM = pl.BlockSpec(memory_space=pltpu.VMEM)
SMEM = pl.BlockSpec(memory_space=pltpu.SMEM)


def call(kernel, shapes, flops, moved, *args, specs=None, room=32, **more):
    if specs is None:
        specs = [SMEM if x.ndim == 1 and x.dtype == jnp.int32 else VMEM for x in args]
    return pl.pallas_call(
        kernel,
        out_shape=shapes,
        in_specs=specs,
        cost_estimate=pl.CostEstimate(flops=flops, bytes_accessed=moved, transcendentals=0),
        compiler_params=pltpu.CompilerParams(vmem_limit_bytes=room * 1024 * 1024),
        **more,
    )(*args)


def shape(dims, dtype=F32):
    return pltpu.HBM(dims, dtype)


def hbm(x):
    return pltpu.with_memory_space_constraint(x, pltpu.HBM)


def shards(student_feat, prototypes, teacher_logits):
    core = lax.axis_index("core")
    core_arg = core.reshape(1)
    chip = lax.axis_index(PLANE)
    block = core * 16 + chip
    place = jnp.stack([chip, lax.axis_index("proto")])

    send = call(
        pack_kernel,
        shape((16, 160, 512), BF16),
        10**7,
        5 * 10**6,
        core_arg,
        teacher_logits,
        prototypes,
        student_feat,
        specs=[
            SMEM,
            pl.BlockSpec((32, 4096), lambda i: (0, i)),
            pl.BlockSpec((8, 4096), lambda i: (0, i)),
            pl.BlockSpec((160, 256), lambda i: (0, 0)),
        ],
        out_specs=pl.BlockSpec((4, 160, 512), lambda i: (i, 0, 0)),
        scratch_shapes=[pltpu.VMEM((80, 512), BF16)],
        grid=(4,),
        room=56,
    )
    got = lax.all_to_all(send, PLANE, 0, 0, tiled=True)
    mate = lax.ppermute(got[:, 32:80], "core", SWAP)
    half = pl.BlockSpec((16, 32, 512), lambda i: (0, 0, 0))

    mass, pack = call(
        first_kernel,
        (shape((512, 1024)), shape((32, 8, 128))),
        10**7,
        3 * 10**6,
        core_arg,
        got,
        mate,
        specs=[SMEM, half, half],
        out_specs=(VMEM, VMEM),
        grid=(1,),
    )
    came = lax.all_to_all(pack, BATCH, 0, 0, tiled=True)
    row_sum = jnp.sum(came, axis=0)
    got, mate, _ = lax.optimization_barrier((got, mate, pack))
    whole = lambda *dims: pl.BlockSpec(dims, lambda i: (0,) * len(dims))
    grad_prob, exp_part, weights, my_weights, my_scale, my_inv, unit_hi, unit_lo = call(
        exp_kernel,
        (
            shape((2560, 1024), BF16),
            shape((16, 256)),
            shape((256, 1024), BF16),
            shape((256, 512), BF16),
            shape((1, 512)),
            shape((1, 512)),
            shape((256, 512), BF16),
            shape((256, 512), BF16),
        ),
        2 * 10**9,
        9 * 10**6,
        core_arg,
        got,
        mate,
        got,
        specs=[
            SMEM,
            pl.BlockSpec((16, 16, 512), lambda i: (0, 4, 0)),
            pl.BlockSpec((16, 16, 512), lambda i: (0, 2, 0)),
            pl.BlockSpec((4, 80, 512), lambda i: (i, 1, 0)),
        ],
        out_specs=(
            pl.BlockSpec((640, 1024), lambda i: (i, 0)),
            whole(16, 256),
            whole(256, 1024),
            whole(256, 512),
            whole(1, 512),
            whole(1, 512),
            whole(256, 512),
            whole(256, 512),
        ),
        scratch_shapes=[pltpu.VMEM((1, 1024), F32)],
        grid=(4,),
    )
    unit_spec = pl.BlockSpec((8, 80, 512), lambda i: (i, 1, 0))

    grad_prob, row_sum = lax.optimization_barrier((grad_prob, row_sum))
    came_one = lax.all_to_all(jnp.broadcast_to(row_sum[None], (8, 8, 128)), "proto", 0, 0, tiled=True)
    student_pack = call(
        student_kernel,
        shape((16, 192, 256), BF16),
        2 * 10**9,
        7 * 10**6,
        hbm(grad_prob),
        weights,
        exp_part,
        exp_part,
        specs=[
            pl.BlockSpec((1280, 1024), lambda i: (i, 0)),
            VMEM,
            pl.BlockSpec((8, 256), lambda i: (i, 0)),
            VMEM,
        ],
        out_specs=pl.BlockSpec((8, 192, 256), lambda i: (i, 0, 0)),
        grid=(2,),
    )
    came_one, student_pack = lax.optimization_barrier((came_one, student_pack))

    part = call(
        second_kernel,
        shape((8, 128)),
        10**7,
        2 * 10**6,
        came_one,
        hbm(mass),
        specs=[VMEM, pl.BlockSpec(memory_space=pltpu.HBM)],
        out_specs=VMEM,
        scratch_shapes=[pltpu.VMEM((512, 1024), F32), pltpu.SemaphoreType.DMA((4,))],
    )
    part_mate = lax.ppermute(part, "core", SWAP)
    pack = call(
        insert_kernel,
        shape((16, 192, 256), BF16),
        10**4,
        10**5,
        part,
        part_mate,
        hbm(student_pack),
        specs=[VMEM, VMEM, pl.BlockSpec(memory_space=pltpu.HBM)],
        out_specs=pl.BlockSpec((16, 16, 256), lambda i: (0, 11, 0)),
        grid=(1,),
        input_output_aliases={2: 0},
    )
    came = lax.all_to_all(pack, PLANE, 0, 0, tiled=True)

    got, _ = lax.optimization_barrier((got, pack))
    seen = call(
        seen_kernel,
        shape((256, 512)),
        10**8,
        2 * 10**6,
        got,
        specs=[pl.BlockSpec((16, 80, 512), lambda i: (0, 1, 0))],
        out_specs=VMEM,
        grid=(1,),
    )
    seen_mate = lax.ppermute(seen, "core", SWAP)

    pack = call(
        home_kernel,
        shape((8, 48, 256), BF16),
        10**7,
        2 * 10**6,
        place,
        hbm(came),
        specs=[SMEM, pl.BlockSpec((4, 192, 256), lambda i: (i, 0, 0))],
        out_specs=pl.BlockSpec((8, 48, 256), lambda i: (0, 0, 0)),
        scratch_shapes=[
            pltpu.VMEM((160, 256), F32),
            pltpu.VMEM((16, 256), F32),
            pltpu.VMEM((8, 256), F32),
            pltpu.VMEM((256, 128), F32),
        ],
        grid=(4,),
    )
    came_two = lax.all_to_all(pack, "proto", 0, 0, tiled=True)

    keep, pack = call(
        third_kernel,
        (shape((512, 1024), BF16), shape((32, 48, 256), BF16)),
        10**9,
        4 * 10**6,
        came_two,
        mass,
        unit_hi,
        unit_lo,
        out_specs=(VMEM, VMEM),
    )
    came = lax.all_to_all(pack, BATCH, 0, 0, tiled=True)

    came_two, _ = lax.optimization_barrier((came_two, pack))
    term, other = call(
        term_kernel,
        (shape((256, 512)), shape((256, 512))),
        3 * 10**9,
        7 * 10**6,
        core_arg,
        got,
        hbm(grad_prob),
        came_two,
        specs=[SMEM, unit_spec, pl.BlockSpec((1280, 1024), lambda i: (i, 0)), VMEM],
        out_specs=(VMEM, VMEM),
        scratch_shapes=[pltpu.VMEM((256, 1024), F32)],
        grid=(2,),
    )
    term_mate = lax.ppermute(other, "core", SWAP)
    home_slice = call(slice_kernel, shape((24, 256)), 10**6, 10**5, place, came_two, out_specs=VMEM)

    pack = call(
        target_kernel,
        shape((8, 64, 256), BF16),
        10**7,
        10**6,
        block.reshape(1),
        came,
        home_slice,
        out_specs=VMEM,
        scratch_shapes=[pltpu.VMEM((128, 128), F32)],
    )
    came = lax.all_to_all(pack, "proto", 0, 0, tiled=True)

    column = pl.BlockSpec((256, 128), lambda i: (0, i))
    line = pl.BlockSpec((1, 128), lambda i: (0, i))
    grad = call(
        final_kernel,
        shape((256, 512)),
        10**9,
        4 * 10**6,
        core_arg,
        came,
        hbm(keep),
        hbm(seen),
        hbm(seen_mate),
        hbm(term),
        hbm(term_mate),
        hbm(my_weights),
        my_scale,
        my_inv,
        specs=[SMEM, VMEM, pl.BlockSpec((128, 1024), lambda i: (i, 0)), VMEM, VMEM, column, column, column, line, line],
        out_specs=column,
        scratch_shapes=[pltpu.VMEM((256, 1024), BF16), pltpu.VMEM((256, 1024), BF16)],
        grid=(4,),
    )
    came, student_feat, _ = lax.optimization_barrier((came, student_feat, grad))
    grad = lax.all_to_all(grad.reshape(32, 8, 512), BATCH, 0, 0, tiled=True)
    grad_weight = grad.transpose(1, 0, 2).reshape(8, 16384)
    grad_feat = call(
        feat_kernel,
        shape((160, 256)),
        10**7,
        10**6,
        block.reshape(1),
        came,
        student_feat,
        out_specs=VMEM,
        scratch_shapes=[pltpu.VMEM((128, 128), F32)],
    )
    return (grad_feat, grad_weight)


def solution(mesh):
    split_mesh = Mesh(mesh.devices.reshape(4, 4, 2, 8), ("y", "x", "core", "proto"))
    return jax.shard_map(
        shards,
        mesh=split_mesh,
        in_specs=(P(BATCH, None), P(BATCH, "proto"), P(BATCH, "proto")),
        out_specs=(P(BATCH, None), P(BATCH, "proto")),
        check_vma=False,
    )
```

time: 232 us -> 201 us (0.87)
  Pallas kernels: 0 us -> 47.2 us
  other arithmetic: 37.9 us -> 0.11 us
  matrix products: 28.5 us -> 0 us
  local copies, waits for them, and re-layouts: 13.3 us -> 5.62 us
    pallas_call x0 -> x14, Pallas kernels: none -> 47.2 us  [call(): pl.pallas_call(kernel, out_shape=shapes, in_specs=specs, cost_estimate=pl...]
    dot_general x7 -> x0, matrix products: 28.5 us -> none  [dot(): return lax.dot_general(a, b, (dims, ((), ())), preferred_element_type=F32)]
    reduce_sum x18 -> x1, other arithmetic: 16.4 us -> 0.04 us  [shards(): row_sum = jnp.sum(came, axis=0)]
    all_to_all x4, waiting for transfers between devices: 23.8 us -> 15.3 us  [the longest x1 11.6 us: shards(): came = lax.all_to_all(pack, 'proto', 0, 0, tiled=True)]
    convert_element_type x5 -> x0, other arithmetic: 5.32 us -> none  [the longest x1 2.24 us: encode_logits(): return jnp.where(x < 0, -mag, mag).astype(BF16)]
    all_to_all x1, waiting for transfers between devices: 19.8 us -> 24 us  [shards(): came = lax.all_to_all(pack, PLANE, 0, 0, tiled=True)]
    concatenate x8 -> x0, other arithmetic: 3.87 us -> none  [the longest x1 1.66 us: shards(): jnp.concatenate([root_code(student_part * 16384.0).reshape(16, 160, 256),...]
    ppermute x3, starting transfers between devices: 5.03 us -> 1.64 us  [the longest x1 1.13 us: shards(): part_mate = lax.ppermute(part, 'core', SWAP)]
  transfers between devices with their start and end apart: 10 -> 10, of which waited for: 7 -> 7; matrix products, arithmetic and copies ran while one was open for 19% -> 0% of each run, Pallas kernels for 0% -> 13%
where the time goes in v2:
time: 201 us; the launch traced here: 200 us
  blocking collectives  55.8 us (28%)
  waiting for transfers between devices  52.6 us (26%)
  Pallas kernels  47.2 us (23%)
  starting transfers between devices  37.6 us (19%)
  local copies, waits for them, and re-layouts  5.62 us (3%)
    pallas_call x14, Pallas kernels, call(): pl.pallas_call(kernel, out_shape=shapes, in_specs=specs, cost_estimate=pl...  47.2 us
    all_to_all x1, blocking collectives, shards(): got = lax.all_to_all(send, PLANE, 0, 0, tiled=True)  40.6 us
    all_to_all x1, waiting for transfers between devices, shards(): came = lax.all_to_all(pack, PLANE, 0, 0, tiled=True)  24 us
    all_to_all x1, blocking collectives, shards(): came_two = lax.all_to_all(pack, 'proto', 0, 0, tiled=True)  15.2 us
    all_to_all x1, waiting for transfers between devices, shards(): came = lax.all_to_all(pack, 'proto', 0, 0, tiled=True)  11.6 us
    all_to_all x2, starting transfers between devices, shards(): came = lax.all_to_all(pack, BATCH, 0, 0, tiled=True)  11 us
    all_to_all x1, waiting for transfers between devices, shards(): grad = lax.all_to_all(grad.reshape(32, 8, 512), BATCH, 0, 0, tiled=True)  10.3 us
    all_to_all x1, starting transfers between devices, shards(): lax.all_to_all(jnp.broadcast_to(row_sum[None], (8, 8, 128)), 'proto', 0,...  8.19 us
  transfers between devices with their start and end apart: 10, of which 7 were waited for; matrix products, arithmetic and copies ran while one was open for 0% of the time, Pallas kernels for 13%

profile of v2, /device:TPU:1, one launch (start us, length us, event | category | flops | bytes accessed | tf_op | source)
XLA Modules:
  0.0 199.7 jit_solution(14447226398386346831)
XLA Ops:
  0.6 4.4 %shard_map.50 = bf16[16,160,512]{2,1,0:T(8,128)(2,1)} custom-call(s32[1]{0:T(128)} %bitcast.3.core_ref, f32[32,16384]{1,0:T(8,128)} %teacher_ref.1, bf16[8,16384]{1,0:T(8,128)(2,1)} %proto_ref.1, bf16[160,256]{1,0:T(8,128)(2,1)} %feat_ref.2), custom_call_target="tpu_custom_call" | custom-call | flops 10000000 | bytes 5000000 | tf_op jit(solution)/shard_map/pallas_call | solution.py:437
  5.1 40.6 %all_to_all.40.own_ref.unit_ref = bf16[16,160,512]{2,1,0:T(8,128)(2,1)S(1)} all-to-all(bf16[16,160,512]{2,1,0:T(8,128)(2,1)} %shard_map.50), channel_id=1, replica_groups=mesh['y'=4,'x'=4,'core'=2,'proto'=8] {'y','x'}, dimensions={0} | all-to-all | bytes 5242880 | tf_op jit(solution)/shard_map/all_to_all | solution.py:482
  45.7 2.1 %collective-permute-start = (bf16[16,48,512]{2,1,0:T(8,128)(2,1)S(1)}, bf16[16,48,512]{2,1,0:T(8,128)(2,1)S(1)}, u32[]{:S(2)}, u32[]{:S(2)}) collective-permute-start(bf16[16,48,512]{2,1,0:T(8,128)(2,1)S(1)} %slice.4), channel_id=1, source_target_pairs={{0,8},{8,0},{1,9},{9,1},{2,10},{10,2},{3,11},{11,3},{4,12},{12,4},... | collective-permute-start | bytes 2359304 | tf_op jit(solution)/shard_map/ppermute | solution.py:483
  47.8 1.9 collective-permute-done.mate_ref
  49.7 2.2 %shard_map.51 = (f32[512,1024]{1,0:T(8,128)}, f32[32,8,128]{2,1,0:T(8,128)}) custom-call(s32[1]{0:T(128)} %bitcast.3.core_ref, bf16[16,160,512]{2,1,0:T(8,128)(2,1)S(1)} %all_to_all.40.own_ref.unit_ref, bf16[16,48,512]{2,1,0:T(8,128)(2,1)S(1)} %collective-permute-done.mate_ref), custom_call_target="tpu_custom_call" | custom-call | flops 10000000 | bytes 3000000 | tf_op jit(solution)/shard_map/pallas_call | solution.py:437
  51.9 3.9 %all-to-all-start.1 = ((f32[32,8,128]{2,1,0:T(8,128)}), f32[32,8,128]{2,1,0:T(8,128)S(1)}, u32[]{:S(2)}, u32[]{:S(2)}) async-start(f32[32,8,128]{2,1,0:T(8,128)} %get-tuple-element.26), calls=%async_computation.1 | async-start | bytes 262144 | tf_op jit(solution)/shard_map/all_to_all | solution.py:498
  55.7 6.6 %shard_map.52 = (bf16[2560,1024]{1,0:T(8,128)(2,1)}, f32[16,256]{1,0:T(8,128)}, bf16[256,1024]{1,0:T(8,128)(2,1)}, bf16[256,512]{1,0:T(8,128)(2,1)}, f32[1,512]{...) custom-call(s32[1]{0:T(128)} %bitcast.3.core_ref, ...), custom_call_target="tpu_custom_call" | custom-call | flops 2000000000 | bytes 9000000 | tf_op jit(solution)/shard_map/pallas_call | solution.py:437
  62.4 1.1 all-to-all-done.1
  64.1 8.2 %all-to-all-start.2 = ((f32[8,8,128]{2,1,0:T(8,128)}), f32[8,8,128]{2,1,0:T(8,128)S(1)}, u32[]{:S(2)}, u32[]{:S(2)}) async-start(f32[8,8,128]{2,1,0:T(8,128)} %broadcast_in_dim.2), calls=%async_computation.2 | async-start | bytes 65536 | tf_op jit(solution)/shard_map/all_to_all | solution.py:542
  72.3 1.0 copy-done.9
  74.1 5.9 %shard_map.53.pack_ref = bf16[16,192,256]{2,1,0:T(8,128)(2,1)} custom-call(bf16[2560,1024]{1,0:T(8,128)(2,1)} %get-tuple-element.31.grad_ref, bf16[256,1024]{1,0:T(8,128)(2,1)S(1)} %copy-done.9, f32[16,256]{1,0:T(8,128)S(1)} %copy-done.10, f32[16,256]{1,0:T(8,128)S(1)} %copy-done.10), custom_call_target="tpu_custom_call" | custom-call | flops 2000000000 | bytes 7000000 | tf_op jit(solution)/shard_map/pallas_call | solution.py:437
  80.0 2.3 %shard_map.54.own_ref = f32[8,128]{1,0:T(8,128)} custom-call(f32[8,8,128]{2,1,0:T(8,128)S(1)} %all-to-all-done.2.came_ref, f32[512,1024]{1,0:T(8,128)} %get-tuple-element.35.mass_hbm.mass_ref), custom_call_target="tpu_custom_call" | custom-call | flops 10000000 | bytes 2000000 | tf_op jit(solution)/shard_map/pallas_call | solution.py:437
  82.3 1.1 collective-permute-start.1
  83.4 1.0 collective-permute-done.1.mate_ref
  85.8 5.8 %all-to-all-start.3 = ((bf16[16,192,256]{2,1,0:T(8,128)(2,1)}), bf16[16,192,256]{2,1,0:T(8,128)(2,1)}, u32[]{:S(2)}, u32[]{:S(2)}) async-start(bf16[16,192,256]{2,1,0:T(8,128)(2,1)} %shard_map.55), calls=%async_computation.3 | async-start | bytes 3145728 | tf_op jit(solution)/shard_map/all_to_all | solution.py:588
  91.7 24.0 %all-to-all-done.3.came_ref = bf16[16,192,256]{2,1,0:T(8,128)(2,1)} async-done(((bf16[16,192,256]{2,1,0:T(8,128)(2,1)}), bf16[16,192,256]{2,1,0:T(8,128)(2,1)}, u32[]{:S(2)}, u32[]{:S(2)}) %all-to-all-start.3) | async-done | bytes 1572896 | tf_op jit(solution)/shard_map/all_to_all | solution.py:588
  115.7 4.6 %shard_map.56 = bf16[8,48,256]{2,1,0:T(8,128)(2,1)} custom-call(s32[2]{0:T(128)S(1)} %pad_add_fusion.place_ref, bf16[16,192,256]{2,1,0:T(8,128)(2,1)} %all-to-all-done.3.came_ref), custom_call_target="tpu_custom_call" | custom-call | flops 10000000 | bytes 2000000 | tf_op jit(solution)/shard_map/pallas_call | solution.py:437
  120.4 15.2 %all_to_all.41.came_ref = bf16[8,48,256]{2,1,0:T(8,128)(2,1)S(1)} all-to-all(bf16[8,48,256]{2,1,0:T(8,128)(2,1)} %shard_map.56), channel_id=1, replica_groups=mesh['y'=4,'x'=4,'core'=2,'proto'=8] {'proto'}, dimensions={0} | all-to-all | bytes 393216 | tf_op jit(solution)/shard_map/all_to_all | solution.py:620
  135.6 2.7 %shard_map.57 = (bf16[512,1024]{1,0:T(8,128)(2,1)}, bf16[32,48,256]{2,1,0:T(8,128)(2,1)}) custom-call(bf16[8,48,256]{2,1,0:T(8,128)(2,1)S(1)} %all_to_all.41.came_ref, f32[512,1024]{1,0:T(8,128)S(1)} %copy-done, bf16[256,512]{1,0:T(8,128)(2,1)S(1)} %copy-done.11, bf16[256,512]{1,0:T(8,128)(2,1)S(1)} %copy-done.12), custom_call_target="tpu_custom_call" | custom-call | flops 1000000000 | bytes 4000000 | tf_op jit(solution)/shard_map/pallas_call | solution.py:437
  138.3 7.1 %all-to-all-start.5 = ((bf16[32,48,256]{2,1,0:T(8,128)(2,1)}), bf16[32,48,256]{2,1,0:T(8,128)(2,1)S(1)}, u32[]{:S(2)}, u32[]{:S(2)}) async-start(bf16[32,48,256]{2,1,0:T(8,128)(2,1)} %get-tuple-element.39), calls=%async_computation.5 | async-start | bytes 1572864 | tf_op jit(solution)/shard_map/all_to_all | solution.py:633
  145.5 1.2 shard_map.60.seen_ref
  146.9 7.4 %shard_map.61 = (f32[256,512]{1,0:T(8,128)}, f32[256,512]{1,0:T(8,128)}) custom-call(s32[1]{0:T(128)} %bitcast.3.core_ref, bf16[16,160,512]{2,1,0:T(8,128)(2,1)S(1)} %all_to_all.40.own_ref.unit_ref, bf16[2560,1024]{1,0:T(8,128)(2,1)} %get-tuple-element.31.grad_ref, bf16[8,48,256]{2,1,0:T(8,128)(2,1)S(1)} %copy-done.2), custom_call_target="tpu_custom_call" | custom-call | flops 3000000000 | bytes 7000000 | tf_op jit(solution)/shard_map/pallas_call | solution.py:437
  154.6 0.9 copy-done.3
  155.5 1.5 shard_map.58.slice_ref
  157.1 2.6 %all-to-all-done.5.came_ref = bf16[32,48,256]{2,1,0:T(8,128)(2,1)S(1)} async-done(((bf16[32,48,256]{2,1,0:T(8,128)(2,1)}), bf16[32,48,256]{2,1,0:T(8,128)(2,1)S(1)}, u32[]{:S(2)}, u32[]{:S(2)}) %all-to-all-start.5) | async-done | bytes 786464 | tf_op jit(solution)/shard_map/all_to_all | solution.py:633
  160.4 1.2 shard_map.59
  161.7 3.4 %all-to-all-start.6 = ((bf16[8,64,256]{2,1,0:T(8,128)(2,1)}), bf16[8,64,256]{2,1,0:T(8,128)(2,1)S(1)}, u32[]{:S(2)}, u32[]{:S(2)}) async-start(bf16[8,64,256]{2,1,0:T(8,128)(2,1)} %shard_map.59), calls=%async_computation.6 | async-start | bytes 524288 | tf_op jit(solution)/shard_map/all_to_all | solution.py:664
  165.1 11.6 %all-to-all-done.6.came_ref = bf16[8,64,256]{2,1,0:T(8,128)(2,1)S(1)} async-done(((bf16[8,64,256]{2,1,0:T(8,128)(2,1)}), bf16[8,64,256]{2,1,0:T(8,128)(2,1)S(1)}, u32[]{:S(2)}, u32[]{:S(2)}) %all-to-all-start.6) | async-done | bytes 262176 | tf_op jit(solution)/shard_map/all_to_all | solution.py:664
  176.8 5.1 %shard_map.62 = f32[256,512]{1,0:T(8,128)} custom-call(s32[1]{0:T(128)} %bitcast.3.core_ref, bf16[8,64,256]{2,1,0:T(8,128)(2,1)S(1)} %all-to-all-done.6.came_ref, bf16[512,1024]{1,0:T(8,128)(2,1)} %get-tuple-element.41.keep_ref, f32[256,512]{1,0:T(8,128)} %shard_map.60.seen_ref, f32[256,512]{1,0:T(8,128)} %collective-permute-done.2.mate_ref, ...), custom_call_target="tpu_custom_call" | custom-call | flops 1000000000 | bytes 4000000 | tf_op jit(solution)/shard_map/pallas_call | solution.py:437
  181.9 5.5 %all-to-all-start.7 = ((f32[32,8,512]{2,1,0:T(8,128)}), f32[32,8,512]{2,1,0:T(8,128)S(1)}, u32[]{:S(2)}, u32[]{:S(2)}) async-start(f32[32,8,512]{2,1,0:T(8,128)} %bitcast.8), calls=%async_computation.7 | async-start | bytes 1048576 | tf_op jit(solution)/shard_map/all_to_all | solution.py:689
  187.4 1.3 shard_map.63
  188.7 10.3 %all-to-all-done.7 = f32[32,8,512]{2,1,0:T(8,128)S(1)} async-done(((f32[32,8,512]{2,1,0:T(8,128)}), f32[32,8,512]{2,1,0:T(8,128)S(1)}, u32[]{:S(2)}, u32[]{:S(2)}) %all-to-all-start.7) | async-done | bytes 524320 | tf_op jit(solution)/shard_map/all_to_all | solution.py:689
  (37 shorter events, 5.0 us)
Async XLA Ops:
  45.7 4.0 %collective-permute-start = (bf16[16,48,512]{2,1,0:T(8,128)(2,1)S(1)}, bf16[16,48,512]{2,1,0:T(8,128)(2,1)S(1)}, u32[]{:S(2)}, u32[]{:S(2)}) collective-permute-start(bf16[16,48,512]{2,1,0:T(8,128)(2,1)S(1)} %slice.4), channel_id=1, source_target_pairs={{0,8},{8,0},{1,9},{9,1},{2,10},{10,2},{3,11},{11,3},{4,12},{12,4},... | collective-permute-start | bytes 2359304 | tf_op jit(solution)/shard_map/ppermute | solution.py:483
  51.9 11.6 %all-to-all-start.1 = ((f32[32,8,128]{2,1,0:T(8,128)}), f32[32,8,128]{2,1,0:T(8,128)S(1)}, u32[]{:S(2)}, u32[]{:S(2)}) async-start(f32[32,8,128]{2,1,0:T(8,128)} %get-tuple-element.26), calls=%async_computation.1 | async-start | bytes 262144 | tf_op jit(solution)/shard_map/all_to_all | solution.py:498
  64.1 15.9 %all-to-all-start.2 = ((f32[8,8,128]{2,1,0:T(8,128)}), f32[8,8,128]{2,1,0:T(8,128)S(1)}, u32[]{:S(2)}, u32[]{:S(2)}) async-start(f32[8,8,128]{2,1,0:T(8,128)} %broadcast_in_dim.2), calls=%async_computation.2 | async-start | bytes 65536 | tf_op jit(solution)/shard_map/all_to_all | solution.py:542
  72.3 1.0 copy-start.9
  73.4 0.7 copy-start.10
  82.3 2.2 %collective-permute-start.1 = (f32[8,128]{1,0:T(8,128)}, f32[8,128]{1,0:T(8,128)S(1)}, u32[]{:S(2)}, u32[]{:S(2)}) collective-permute-start(f32[8,128]{1,0:T(8,128)} %shard_map.54.own_ref), channel_id=1, source_target_pairs={{0,8},{8,0},{1,9},{9,1},{2,10},{10,2},{3,11},{11,3},{4,12},{12,4},... | collective-permute-start | bytes 12296 | tf_op jit(solution)/shard_map/ppermute | solution.py:574
  84.4 0.7 copy-start.6
  85.8 49.8 %copy-start.11 = (bf16[256,512]{1,0:T(8,128)(2,1)S(1)}, bf16[256,512]{1,0:T(8,128)(2,1)}, u32[]{:S(2)}) copy-start(bf16[256,512]{1,0:T(8,128)(2,1)} %get-tuple-element.37.hi_ref) | copy-start | bytes 786436
  85.8 49.8 %copy-start.12 = (bf16[256,512]{1,0:T(8,128)(2,1)S(1)}, bf16[256,512]{1,0:T(8,128)(2,1)}, u32[]{:S(2)}) copy-start(bf16[256,512]{1,0:T(8,128)(2,1)} %get-tuple-element.38.lo_ref) | copy-start | bytes 786436
  85.8 29.9 %all-to-all-start.3 = ((bf16[16,192,256]{2,1,0:T(8,128)(2,1)}), bf16[16,192,256]{2,1,0:T(8,128)(2,1)}, u32[]{:S(2)}, u32[]{:S(2)}) async-start(bf16[16,192,256]{2,1,0:T(8,128)(2,1)} %shard_map.55), calls=%async_computation.3 | async-start | bytes 3145728 | tf_op jit(solution)/shard_map/all_to_all | solution.py:588
  115.7 19.9 %copy-start = (f32[512,1024]{1,0:T(8,128)S(1)}, f32[512,1024]{1,0:T(8,128)}, u32[]{:S(2)}) copy-start(f32[512,1024]{1,0:T(8,128)} %get-tuple-element.35.mass_hbm.mass_ref) | copy-start | bytes 6291460
  135.6 2.7 %copy-start.1 = (bf16[8,48,256]{2,1,0:T(8,128)(2,1)}, bf16[8,48,256]{2,1,0:T(8,128)(2,1)S(1)}, u32[]{:S(2)}) copy-start(bf16[8,48,256]{2,1,0:T(8,128)(2,1)S(1)} %all_to_all.41.came_ref) | copy-start | bytes 589828
  138.3 21.4 %all-to-all-start.5 = ((bf16[32,48,256]{2,1,0:T(8,128)(2,1)}), bf16[32,48,256]{2,1,0:T(8,128)(2,1)S(1)}, u32[]{:S(2)}, u32[]{:S(2)}) async-start(bf16[32,48,256]{2,1,0:T(8,128)(2,1)} %get-tuple-element.39), calls=%async_computation.5 | async-start | bytes 1572864 | tf_op jit(solution)/shard_map/all_to_all | solution.py:633
  145.5 1.4 copy-start.2
  146.7 30.1 %copy-start.7 = (f32[1,512]{1,0:T(1,128)S(1)}, f32[1,512]{1,0:T(1,128)}, u32[]{:S(2)}) copy-start(f32[1,512]{1,0:T(1,128)} %get-tuple-element.46.scale_ref) | copy-start | bytes 6148
  146.7 30.1 %copy-start.8 = (f32[1,512]{1,0:T(1,128)S(1)}, f32[1,512]{1,0:T(1,128)}, u32[]{:S(2)}) copy-start(f32[1,512]{1,0:T(1,128)} %get-tuple-element.47.inv_ref) | copy-start | bytes 6148
  146.7 18.4 %collective-permute-start.2 = (f32[256,512]{1,0:T(8,128)}, f32[256,512]{1,0:T(8,128)}, u32[]{:S(2)}, u32[]{:S(2)}) collective-permute-start(f32[256,512]{1,0:T(8,128)} %shard_map.60.seen_ref), channel_id=1, source_target_pairs={{0,8},{8,0},{1,9},{9,1},{2,10},{10,2},{3,11},{11,3},{4,12},{12,4},... | collective-permute-start | bytes 1572872 | tf_op jit(solution)/shard_map/ppermute | solution.py:601
  154.3 10.8 %collective-permute-start.3 = (f32[256,512]{1,0:T(8,128)}, f32[256,512]{1,0:T(8,128)S(1)}, u32[]{:S(2)}, u32[]{:S(2)}) collective-permute-start(f32[256,512]{1,0:T(8,128)} %get-tuple-element.44), channel_id=1, source_target_pairs={{0,8},{8,0},{1,9},{9,1},{2,10},{10,2},{3,11},{11,3},{4,12},{12,4},... | collective-permute-start | bytes 1572872 | tf_op jit(solution)/shard_map/ppermute | solution.py:650
  154.6 0.9 copy-start.3
  159.7 0.7 copy-start.5
  161.7 15.1 %all-to-all-start.6 = ((bf16[8,64,256]{2,1,0:T(8,128)(2,1)}), bf16[8,64,256]{2,1,0:T(8,128)(2,1)S(1)}, u32[]{:S(2)}, u32[]{:S(2)}) async-start(bf16[8,64,256]{2,1,0:T(8,128)(2,1)} %shard_map.59), calls=%async_computation.6 | async-start | bytes 524288 | tf_op jit(solution)/shard_map/all_to_all | solution.py:664
  165.1 11.6 %copy-start.13 = (f32[256,512]{1,0:T(8,128)}, f32[256,512]{1,0:T(8,128)S(1)}, u32[]{:S(2)}) copy-start(f32[256,512]{1,0:T(8,128)S(1)} %collective-permute-done.3.term_mate_ref) | copy-start | bytes 1572868
  176.7 10.6 %copy-start.4 = (bf16[160,256]{1,0:T(8,128)(2,1)S(1)}, bf16[160,256]{1,0:T(8,128)(2,1)}, u32[]{:S(2)}) copy-start(bf16[160,256]{1,0:T(8,128)(2,1)} %feat_ref.2) | copy-start | bytes 245764
  181.9 17.1 %all-to-all-start.7 = ((f32[32,8,512]{2,1,0:T(8,128)}), f32[32,8,512]{2,1,0:T(8,128)S(1)}, u32[]{:S(2)}, u32[]{:S(2)}) async-start(f32[32,8,512]{2,1,0:T(8,128)} %bitcast.8), calls=%async_computation.7 | async-start | bytes 1048576 | tf_op jit(solution)/shard_map/all_to_all | solution.py:689

commit v3 on v2

--- a/solution.py
+++ b/solution.py
@@ -108,8 +108,8 @@
 def sweep(mass_ref, row_inv, keep_ref=None, copies=None):
     total = jnp.zeros((8, 1024), F32)
     for low in range(0, 512, 32):
-        if copies is not None and low % 128 == 0:
-            copies[low // 128].wait()
+        if copies is not None and low % 64 == 0:
+            copies[low // 64].wait()
         x = mass_ref[low : low + 32, :]
         y = x if row_inv is None else x * row_inv
         x = x * (1.0 / jnp.sum(y, axis=1, keepdims=True))
@@ -130,7 +130,7 @@
         unit_ref[:, :256] = unit[:80]
         unit_ref[:, 256:] = unit[80:]
 
-    for p in range(4):
+    for p in range(8):
         left = encode_logits(teacher_ref[:, 1024 * p : 1024 * p + 512])
         right = encode_logits(teacher_ref[:, 1024 * p + 512 : 1024 * p + 1024])
         out_ref[p, 0:32, :] = jnp.where(first, left, right)
@@ -151,64 +151,40 @@
     out_ref[...] = jnp.broadcast_to(part[None], (32, 8, 128))
 
 
-def fetch(mass_hbm, mass_ref, sems):
+def second_kernel(came_ref, mass_hbm, pack_ref, out_ref, mass_ref, sems):
     copies = [
-        pltpu.make_async_copy(
-            mass_hbm.at[pl.ds(128 * i, 128), :], mass_ref.at[pl.ds(128 * i, 128), :], sems.at[i]
-        )
-        for i in range(4)
+        pltpu.make_async_copy(mass_hbm.at[pl.ds(64 * i, 64), :], mass_ref.at[pl.ds(64 * i, 64), :], sems.at[i])
+        for i in range(8)
     ]
     for copy in copies:
         copy.start()
-    return copies
-
-
-def second_kernel(came_ref, mass_hbm, out_ref, mass_ref, sems):
-    copies = fetch(mass_hbm, mass_ref, sems)
     row_inv = lanes(1.0 / jnp.sum(came_ref[...], axis=0))
-    out_ref[...] = rows8(sweep(mass_ref, row_inv, copies=copies))
-
-
-def insert_kernel(own_ref, mate_ref, pack_ref, out_ref):
-    row = padded(split_row(own_ref[...] + mate_ref[...]))
+    row = padded(split_row(rows8(sweep(mass_ref, row_inv, copies=copies))))
     out_ref[...] = jnp.broadcast_to(row[None], (16, 16, 256))
 
 
-def home_kernel(place_ref, came_ref, out_ref, home_ref, exp_ref, row_ref, part_ref):
-    step = pl.program_id(0)
-
-    @pl.when(step == 0)
-    def _():
-        home_ref[...] = jnp.zeros_like(home_ref)
-        exp_ref[...] = jnp.zeros_like(exp_ref)
-        row_ref[...] = jnp.zeros_like(row_ref)
-        part_ref[...] = jnp.zeros_like(part_ref)
-
+def home_kernel(place_ref, came_ref, out_ref):
     pick = lax.broadcasted_iota(jnp.int32, (16, 256), 0) == place_ref[0]
-    exp_sum = exp_ref[...]
-    row_sum = row_ref[...]
+    exp_sum = jnp.zeros((16, 256), F32)
+    row_sum = jnp.zeros((8, 256), F32)
     parts = []
-    for p in range(4):
+    for p in range(16):
         exp_part = sum_decode(came_ref[p, 160:176, :])
         exp_sum = exp_sum + exp_part
         row_sum = row_sum + came_ref[p, 176:192, :].astype(F32)[:8]
         parts.append(jnp.sum(jnp.where(pick, exp_part, 0.0), axis=0, keepdims=True))
-    exp_ref[...] = exp_sum
-    row_ref[...] = row_sum
-    parts = columns(jnp.concatenate(parts + [jnp.zeros((4, 256), F32)], axis=0) * (1.0 / ROOT))
-    part_ref[...] += jnp.sum(parts, axis=1, keepdims=True)
+    parts = columns(jnp.concatenate(parts, axis=0) * (1.0 / ROOT))
+    scale = 1.0 / jnp.sum(parts, axis=1, keepdims=True)
+    code = []
     for low in range(0, 160, 32):
-        home = home_ref[low : low + 32, :]
-        for p in range(4):
+        home = jnp.zeros((32, 256), F32)
+        for p in range(16):
             home = home + root_decode(came_ref[p, low : low + 32, :]) * parts[low : low + 32, p : p + 1]
-        home_ref[low : low + 32, :] = home
-
-    @pl.when(step == 3)
-    def _():
-        code = fine_code(home_ref[...] / part_ref[:160, :1])
-        tail = [jnp.zeros((4, 256), F32), split_row(join_row(row_ref[...])), sum_code(exp_ref[...] * (1.0 / 16.0))]
-        for z in range(8):
-            out_ref[z] = jnp.concatenate([code[20 * z : 20 * z + 20]] + tail, axis=0).astype(BF16)
+        code.append(fine_code(home * scale[low : low + 32]))
+    code = jnp.concatenate(code, axis=0)
+    tail = [jnp.zeros((4, 256), F32), split_row(join_row(row_sum)), sum_code(exp_sum * (1.0 / 16.0))]
+    for z in range(8):
+        out_ref[z] = jnp.concatenate([code[20 * z : 20 * z + 20]] + tail, axis=0).astype(BF16)
 
 
 def slice_kernel(place_ref, came_ref, out_ref):
@@ -227,23 +203,23 @@
     out_ref[...] = fine_code(home * (weight / jnp.sum(parts, axis=1, keepdims=True)))[:24]
 
 
-def third_kernel(came_ref, mass_ref, hi_ref, lo_ref, keep_ref, out_ref):
-    rows = came_ref[0, 16:32, :].astype(F32)
-    for p in range(1, 8):
-        rows = rows + came_ref[p, 16:32, :].astype(F32)
+def third_kernel(came_ref, came_mate_ref, mass_ref, hi_ref, lo_ref, keep_ref, out_ref):
+    rows = jnp.zeros((16, 256), F32)
+    for p in range(8):
+        rows = rows + (came_ref[p, 16:32, :].astype(F32) + came_mate_ref[p, 16:32, :].astype(F32))
     row_inv = lanes(1.0 / join_row(rows[8:]))
     part = sweep(mass_ref, row_inv, keep_ref)
     scale = ROOT / part
+    tail = split_row(rows8(part))
     for j in range(8):
         keep = keep_ref[:, 128 * j : 128 * j + 128]
         x = jnp.dot(hi_ref[...], keep, preferred_element_type=F32)
         x = x + jnp.dot(lo_ref[...], keep, preferred_element_type=F32)
         x = (x * scale[:, 128 * j : 128 * j + 128]).T
-        x = root_code(x).astype(BF16)
+        x = root_code(x)
         for i in range(4):
             block = 4 * j + i
-            out_ref[block % 16 * 2 + block // 16, 0:32, :] = x[32 * i : 32 * i + 32]
-    out_ref[:, 32:48, :] = jnp.broadcast_to(padded(split_row(rows8(part)))[None], (32, 16, 256))
+            out_ref[block % 16 * 2 + block // 16] = jnp.concatenate([x[32 * i : 32 * i + 32], tail], axis=0).astype(BF16)
 
 
 def target_kernel(index_ref, came_ref, slice_ref, out_ref, turn_ref):
@@ -252,7 +228,7 @@
     row_sum = jnp.zeros((8, 128), F32)
     parts = []
     for p in range(32):
-        row = join_row(came_ref[p, 32:48, :].astype(F32)[:8])
+        row = join_row(came_ref[p].astype(F32)[32:])
         row_sum = row_sum + row
         parts.append(jnp.sum(jnp.where(pick, row, 0.0), axis=0, keepdims=True))
     parts = jnp.concatenate(parts, axis=0) * (1.0 / ROOT)
@@ -260,7 +236,7 @@
     parts = turn_ref[pl.ds(pl.multiple_of(index % 4 * 32, 32), 32), :]
     total = jnp.zeros((32, 256), F32)
     for p in range(32):
-        total = total + root_decode(came_ref[p, 0:32, :]) * parts[:, p : p + 1]
+        total = total + root_decode(came_ref[p])[:32] * parts[:, p : p + 1]
     code = fine_code(total / jnp.sum(parts, axis=1, keepdims=True))
     code = jnp.concatenate([code, slice_ref[...], split_row(row_sum)], axis=0).astype(BF16)
     out_ref[...] = jnp.broadcast_to(code[None], (8, 64, 256))
@@ -293,31 +269,30 @@
 
 
 def final_kernel(
-    core_ref, came_ref, keep_ref, seen_ref, mate_ref, term_ref, term_mate_ref, weight_ref, scale_ref, inv_ref, out_ref,
-    hi_ref, lo_ref,
+    core_ref, came_ref, keep_ref, seen_ref, mate_ref, term_ref, term_mate_ref, weight_ref, scale_ref, inv_ref, out_ref
 ):
-    @pl.when(pl.program_id(0) == 0)
-    def _():
-        first = core_ref[0] == 0
-        rows = came_ref[0, 48:64, :].astype(F32)
-        for p in range(1, 8):
-            rows = rows + came_ref[p, 48:64, :].astype(F32)
-        row_inv = lanes(1.0 / join_row(rows[8:])) * (1.0 / PAIRS)
-        seen = seen_ref[...]
-        mate = mate_ref[...]
-        hi_ref[:, :512], lo_ref[:, :512] = split(jnp.where(first, seen, mate) * row_inv[:, :512])
-        hi_ref[:, 512:], lo_ref[:, 512:] = split(jnp.where(first, mate, seen) * row_inv[:, 512:])
-
-    keep = keep_ref[...]
-    x = dot(hi_ref[...], keep, NT) + dot(lo_ref[...], keep, NT)
-    x = term_ref[...] + term_mate_ref[...] - x * scale_ref[...]
-    w = weight_ref[...].astype(F32)
-    dots = jnp.sum(w * x, axis=0, keepdims=True) * inv_ref[...]
-    out_ref[...] = x - w * dots
+    first = core_ref[0] == 0
+    rows = came_ref[0, 48:64, :].astype(F32)
+    for p in range(1, 8):
+        rows = rows + came_ref[p, 48:64, :].astype(F32)
+    row_inv = lanes(1.0 / join_row(rows[8:])) * (1.0 / PAIRS)
+    seen = seen_ref[...]
+    mate = mate_ref[...]
+    low_hi, low_lo = split(jnp.where(first, seen, mate) * row_inv[:, :512])
+    high_hi, high_lo = split(jnp.where(first, mate, seen) * row_inv[:, 512:])
+    for j in range(4):
+        cols = slice(128 * j, 128 * j + 128)
+        keep = keep_ref[cols, :]
+        x = dot(low_hi, keep[:, :512], NT) + dot(low_lo, keep[:, :512], NT)
+        x = x + (dot(high_hi, keep[:, 512:], NT) + dot(high_lo, keep[:, 512:], NT))
+        x = term_ref[:, cols] + term_mate_ref[:, cols] - x * scale_ref[:, cols]
+        w = weight_ref[:, cols].astype(F32)
+        dots = jnp.sum(w * x, axis=0, keepdims=True) * inv_ref[:, cols]
+        out_ref[:, cols] = x - w * dots
 
 
 def columns(x):
-    return jnp.concatenate([x, jnp.zeros((120, 256), F32)], axis=0).T
+    return jnp.concatenate([x, jnp.zeros((128 - x.shape[0], 256), F32)], axis=0).T
 
 
 def exp_kernel(
@@ -470,13 +445,13 @@
         student_feat,
         specs=[
             SMEM,
-            pl.BlockSpec((32, 4096), lambda i: (0, i)),
-            pl.BlockSpec((8, 4096), lambda i: (0, i)),
+            pl.BlockSpec((32, 8192), lambda i: (0, i)),
+            pl.BlockSpec((8, 8192), lambda i: (0, i)),
             pl.BlockSpec((160, 256), lambda i: (0, 0)),
         ],
-        out_specs=pl.BlockSpec((4, 160, 512), lambda i: (i, 0, 0)),
+        out_specs=pl.BlockSpec((8, 160, 512), lambda i: (i, 0, 0)),
         scratch_shapes=[pltpu.VMEM((80, 512), BF16)],
-        grid=(4,),
+        grid=(2,),
         room=56,
     )
     got = lax.all_to_all(send, PLANE, 0, 0, tiled=True)
@@ -546,12 +521,12 @@
         2 * 10**9,
         7 * 10**6,
         hbm(grad_prob),
-        weights,
+        hbm(weights),
         exp_part,
         exp_part,
         specs=[
             pl.BlockSpec((1280, 1024), lambda i: (i, 0)),
-            VMEM,
+            whole(256, 1024),
             pl.BlockSpec((8, 256), lambda i: (i, 0)),
             VMEM,
         ],
@@ -560,28 +535,17 @@
     )
     came_one, student_pack = lax.optimization_barrier((came_one, student_pack))
 
-    part = call(
+    pack = call(
         second_kernel,
-        shape((8, 128)),
+        shape((16, 192, 256), BF16),
         10**7,
         2 * 10**6,
         came_one,
         hbm(mass),
-        specs=[VMEM, pl.BlockSpec(memory_space=pltpu.HBM)],
-        out_specs=VMEM,
-        scratch_shapes=[pltpu.VMEM((512, 1024), F32), pltpu.SemaphoreType.DMA((4,))],
-    )
-    part_mate = lax.ppermute(part, "core", SWAP)
-    pack = call(
-        insert_kernel,
-        shape((16, 192, 256), BF16),
-        10**4,
-        10**5,
-        part,
-        part_mate,
         hbm(student_pack),
-        specs=[VMEM, VMEM, pl.BlockSpec(memory_space=pltpu.HBM)],
+        specs=[VMEM, pl.BlockSpec(memory_space=pltpu.HBM), pl.BlockSpec(memory_space=pltpu.HBM)],
         out_specs=pl.BlockSpec((16, 16, 256), lambda i: (0, 11, 0)),
+        scratch_shapes=[pltpu.VMEM((512, 1024), F32), pltpu.SemaphoreType.DMA((8,))],
         grid=(1,),
         input_output_aliases={2: 0},
     )
@@ -607,24 +571,19 @@
         2 * 10**6,
         place,
         hbm(came),
-        specs=[SMEM, pl.BlockSpec((4, 192, 256), lambda i: (i, 0, 0))],
-        out_specs=pl.BlockSpec((8, 48, 256), lambda i: (0, 0, 0)),
-        scratch_shapes=[
-            pltpu.VMEM((160, 256), F32),
-            pltpu.VMEM((16, 256), F32),
-            pltpu.VMEM((8, 256), F32),
-            pltpu.VMEM((256, 128), F32),
-        ],
-        grid=(4,),
+        specs=[SMEM, whole(16, 192, 256)],
+        out_specs=whole(8, 48, 256),
+        grid=(1,),
     )
     came_two = lax.all_to_all(pack, "proto", 0, 0, tiled=True)
 
     keep, pack = call(
         third_kernel,
-        (shape((512, 1024), BF16), shape((32, 48, 256), BF16)),
+        (shape((512, 1024), BF16), shape((32, 40, 256), BF16)),
         10**9,
         4 * 10**6,
         came_two,
+        lax.ppermute(came_two, "core", SWAP),
         mass,
         unit_hi,
         unit_lo,
@@ -663,8 +622,6 @@
     )
     came = lax.all_to_all(pack, "proto", 0, 0, tiled=True)
 
-    column = pl.BlockSpec((256, 128), lambda i: (0, i))
-    line = pl.BlockSpec((1, 128), lambda i: (0, i))
     grad = call(
         final_kernel,
         shape((256, 512)),
@@ -680,10 +637,9 @@
         hbm(my_weights),
         my_scale,
         my_inv,
-        specs=[SMEM, VMEM, pl.BlockSpec((128, 1024), lambda i: (i, 0)), VMEM, VMEM, column, column, column, line, line],
-        out_specs=column,
-        scratch_shapes=[pltpu.VMEM((256, 1024), BF16), pltpu.VMEM((256, 1024), BF16)],
-        grid=(4,),
+        specs=[SMEM, VMEM, whole(512, 1024)] + [whole(256, 512)] * 5 + [VMEM, VMEM],
+        out_specs=whole(256, 512),
+        grid=(1,),
     )
     came, student_feat, _ = lax.optimization_barrier((came, student_feat, grad))
     grad = lax.all_to_all(grad.reshape(32, 8, 512), BATCH, 0, 0, tiled=True)

time: 201 us -> 193 us (0.960)
  Pallas kernels: 47.2 us -> 43.5 us
  waiting for transfers between devices: 52.6 us -> 49 us
  local copies, waits for them, and re-layouts: 5.62 us -> 2.96 us
    pallas_call x14 -> x13, Pallas kernels: 47.2 us -> 43.5 us  [call(): pl.pallas_call(kernel, out_shape=shapes, in_specs=specs, cost_estimate=pl...]
    all_to_all x1, waiting for transfers between devices: 24 us -> 20.5 us  [shards(): came = lax.all_to_all(pack, PLANE, 0, 0, tiled=True)]
    ppermute x1, starting transfers between devices: 1.13 us -> 4.5 us  [shards(): lax.ppermute(came_two, 'core', SWAP)]
    all_to_all x2, starting transfers between devices: 11 us -> 8.06 us  [shards(): came = lax.all_to_all(pack, BATCH, 0, 0, tiled=True)]
    unnamed x29 -> x19, local copies, waits for them, and re-layouts: 4.94 us -> 2.27 us
  transfers between devices with their start and end apart: 10 -> 10, of which waited for: 7 -> 8; matrix products, arithmetic and copies ran while one was open for 0% -> 0% of each run, Pallas kernels for 13% -> 13%
where the time goes in v3:
time: 193 us; the launch traced here: 192 us
  blocking collectives  57.3 us (30%)
  waiting for transfers between devices  49 us (25%)
  Pallas kernels  43.5 us (23%)
  starting transfers between devices  38.4 us (20%)
  local copies, waits for them, and re-layouts  2.96 us (2%)
    pallas_call x13, Pallas kernels, call(): pl.pallas_call(kernel, out_shape=shapes, in_specs=specs, cost_estimate=pl...  43.5 us
    all_to_all x1, blocking collectives, shards(): got = lax.all_to_all(send, PLANE, 0, 0, tiled=True)  40.6 us
    all_to_all x1, waiting for transfers between devices, shards(): came = lax.all_to_all(pack, PLANE, 0, 0, tiled=True)  20.5 us
    all_to_all x1, blocking collectives, shards(): came_two = lax.all_to_all(pack, 'proto', 0, 0, tiled=True)  16.7 us
    all_to_all x1, waiting for transfers between devices, shards(): came = lax.all_to_all(pack, 'proto', 0, 0, tiled=True)  11.7 us
    all_to_all x1, waiting for transfers between devices, shards(): grad = lax.all_to_all(grad.reshape(32, 8, 512), BATCH, 0, 0, tiled=True)  10.3 us
    all_to_all x1, starting transfers between devices, shards(): lax.all_to_all(jnp.broadcast_to(row_sum[None], (8, 8, 128)), 'proto', 0,...  8.19 us
    all_to_all x2, starting transfers between devices, shards(): came = lax.all_to_all(pack, BATCH, 0, 0, tiled=True)  8.06 us
  transfers between devices with their start and end apart: 10, of which 8 were waited for; matrix products, arithmetic and copies ran while one was open for 0% of the time, Pallas kernels for 13%

profile of v3, /device:TPU:1, one launch (start us, length us, event | category | flops | bytes accessed | tf_op | source)
XLA Modules:
  0.0 192.1 jit_solution(11503720022503086170)
XLA Ops:
  0.6 3.2 %shard_map.50 = bf16[16,160,512]{2,1,0:T(8,128)(2,1)} custom-call(s32[1]{0:T(128)} %bitcast.3.core_ref, f32[32,16384]{1,0:T(8,128)} %teacher_ref.1, bf16[8,16384]{1,0:T(8,128)(2,1)} %proto_ref.1, bf16[160,256]{1,0:T(8,128)(2,1)} %feat_ref.2), custom_call_target="tpu_custom_call" | custom-call | flops 10000000 | bytes 5000000 | tf_op jit(solution)/shard_map/pallas_call | solution.py:412
  3.8 40.6 %all_to_all.40.own_ref.unit_ref = bf16[16,160,512]{2,1,0:T(8,128)(2,1)S(1)} all-to-all(bf16[16,160,512]{2,1,0:T(8,128)(2,1)} %shard_map.50), channel_id=1, replica_groups=mesh['y'=4,'x'=4,'core'=2,'proto'=8] {'y','x'}, dimensions={0} | all-to-all | bytes 5242880 | tf_op jit(solution)/shard_map/all_to_all | solution.py:457
  44.5 2.1 %collective-permute-start = (bf16[16,48,512]{2,1,0:T(8,128)(2,1)S(1)}, bf16[16,48,512]{2,1,0:T(8,128)(2,1)S(1)}, u32[]{:S(2)}, u32[]{:S(2)}) collective-permute-start(bf16[16,48,512]{2,1,0:T(8,128)(2,1)S(1)} %slice.4), channel_id=1, source_target_pairs={{0,8},{8,0},{1,9},{9,1},{2,10},{10,2},{3,11},{11,3},{4,12},{12,4},... | collective-permute-start | bytes 2359304 | tf_op jit(solution)/shard_map/ppermute | solution.py:458
  46.5 1.9 collective-permute-done.mate_ref
  48.4 2.2 %shard_map.51 = (f32[512,1024]{1,0:T(8,128)}, f32[32,8,128]{2,1,0:T(8,128)}) custom-call(s32[1]{0:T(128)} %bitcast.3.core_ref, bf16[16,160,512]{2,1,0:T(8,128)(2,1)S(1)} %all_to_all.40.own_ref.unit_ref, bf16[16,48,512]{2,1,0:T(8,128)(2,1)S(1)} %collective-permute-done.mate_ref), custom_call_target="tpu_custom_call" | custom-call | flops 10000000 | bytes 3000000 | tf_op jit(solution)/shard_map/pallas_call | solution.py:412
  50.6 3.9 %all-to-all-start.1 = ((f32[32,8,128]{2,1,0:T(8,128)}), f32[32,8,128]{2,1,0:T(8,128)S(1)}, u32[]{:S(2)}, u32[]{:S(2)}) async-start(f32[32,8,128]{2,1,0:T(8,128)} %get-tuple-element.26), calls=%async_computation.1 | async-start | bytes 262144 | tf_op jit(solution)/shard_map/all_to_all | solution.py:473
  54.5 6.6 %shard_map.52 = (bf16[2560,1024]{1,0:T(8,128)(2,1)}, f32[16,256]{1,0:T(8,128)}, bf16[256,1024]{1,0:T(8,128)(2,1)}, bf16[256,512]{1,0:T(8,128)(2,1)}, f32[1,512]{...) custom-call(s32[1]{0:T(128)} %bitcast.3.core_ref, ...), custom_call_target="tpu_custom_call" | custom-call | flops 2000000000 | bytes 9000000 | tf_op jit(solution)/shard_map/pallas_call | solution.py:412
  61.1 1.1 all-to-all-done.1
  62.9 8.2 %all-to-all-start.2 = ((f32[8,8,128]{2,1,0:T(8,128)}), f32[8,8,128]{2,1,0:T(8,128)S(1)}, u32[]{:S(2)}, u32[]{:S(2)}) async-start(f32[8,8,128]{2,1,0:T(8,128)} %broadcast_in_dim.2), calls=%async_computation.2 | async-start | bytes 65536 | tf_op jit(solution)/shard_map/all_to_all | solution.py:517
  71.8 6.0 %shard_map.53.pack_ref = bf16[16,192,256]{2,1,0:T(8,128)(2,1)} custom-call(bf16[2560,1024]{1,0:T(8,128)(2,1)} %get-tuple-element.31.grad_ref, bf16[256,1024]{1,0:T(8,128)(2,1)} %get-tuple-element.32.weight_ref, f32[16,256]{1,0:T(8,128)S(1)} %copy-done.5, f32[16,256]{1,0:T(8,128)S(1)} %copy-done.5), custom_call_target="tpu_custom_call" | custom-call | flops 2000000000 | bytes 7000000 | tf_op jit(solution)/shard_map/pallas_call | solution.py:412
  78.0 2.6 %shard_map.54 = bf16[16,192,256]{2,1,0:T(8,128)(2,1)} custom-call(f32[8,8,128]{2,1,0:T(8,128)S(1)} %all-to-all-done.2.came_ref, f32[512,1024]{1,0:T(8,128)} %get-tuple-element.35.mass_hbm.mass_ref, bf16[16,192,256]{2,1,0:T(8,128)(2,1)} %shard_map.53.pack_ref), custom_call_target="tpu_custom_call", output_to_operand_aliasing={{}: (2, {})} | custom-call | flops 10000000 | bytes 2000000 | tf_op jit(solution)/shard_map/pallas_call | solution.py:412
  80.7 5.8 %all-to-all-start.3 = ((bf16[16,192,256]{2,1,0:T(8,128)(2,1)}), bf16[16,192,256]{2,1,0:T(8,128)(2,1)}, u32[]{:S(2)}, u32[]{:S(2)}) async-start(bf16[16,192,256]{2,1,0:T(8,128)(2,1)} %shard_map.54), calls=%async_computation.3 | async-start | bytes 3145728 | tf_op jit(solution)/shard_map/all_to_all | solution.py:552
  86.6 20.5 %all-to-all-done.3.came_ref = bf16[16,192,256]{2,1,0:T(8,128)(2,1)} async-done(((bf16[16,192,256]{2,1,0:T(8,128)(2,1)}), bf16[16,192,256]{2,1,0:T(8,128)(2,1)}, u32[]{:S(2)}, u32[]{:S(2)}) %all-to-all-start.3) | async-done | bytes 1572896 | tf_op jit(solution)/shard_map/all_to_all | solution.py:552
  107.1 3.5 %shard_map.55 = bf16[8,48,256]{2,1,0:T(8,128)(2,1)} custom-call(s32[2]{0:T(128)S(1)} %pad_add_fusion.place_ref, bf16[16,192,256]{2,1,0:T(8,128)(2,1)} %all-to-all-done.3.came_ref), custom_call_target="tpu_custom_call" | custom-call | flops 10000000 | bytes 2000000 | tf_op jit(solution)/shard_map/pallas_call | solution.py:412
  110.6 16.7 %all_to_all.41.came_ref = bf16[8,48,256]{2,1,0:T(8,128)(2,1)S(1)} all-to-all(bf16[8,48,256]{2,1,0:T(8,128)(2,1)} %shard_map.55), channel_id=1, replica_groups=mesh['y'=4,'x'=4,'core'=2,'proto'=8] {'proto'}, dimensions={0} | all-to-all | bytes 393216 | tf_op jit(solution)/shard_map/all_to_all | solution.py:578
  127.3 4.5 %collective-permute-start.1 = (bf16[8,48,256]{2,1,0:T(8,128)(2,1)S(1)}, bf16[8,48,256]{2,1,0:T(8,128)(2,1)S(1)}, u32[]{:S(2)}, u32[]{:S(2)}) collective-permute-start(bf16[8,48,256]{2,1,0:T(8,128)(2,1)S(1)} %all_to_all.41.came_ref), channel_id=1, source_target_pairs={{0,8},{8,0},{1,9},{9,1},{2,10},{10,2},{3,11},{11,3},{4,12},{12,4},... | collective-permute-start | bytes 589832 | tf_op jit(solution)/shard_map/ppermute | solution.py:586
  131.8 1.1 collective-permute-done.1.came_mate_ref
  132.9 2.7 %shard_map.56 = (bf16[512,1024]{1,0:T(8,128)(2,1)}, bf16[32,40,256]{2,1,0:T(8,128)(2,1)}) custom-call(bf16[8,48,256]{2,1,0:T(8,128)(2,1)S(1)} %all_to_all.41.came_ref, bf16[8,48,256]{2,1,0:T(8,128)(2,1)S(1)} %collective-permute-done.1.came_mate_ref, f32[512,1024]{1,0:T(8,128)S(1)} %copy-done, bf16[256,512]{1,0:T(8,128)(2,1)S(1)} %copy-done.6, ...), custom_call_target="tpu_custom_call" | custom-call | flops 1000000000 | bytes 4000000 | tf_op jit(solution)/shard_map/pallas_call | solution.py:412
  135.6 4.2 %all-to-all-start.5 = ((bf16[32,40,256]{2,1,0:T(8,128)(2,1)}), bf16[32,40,256]{2,1,0:T(8,128)(2,1)S(1)}, u32[]{:S(2)}, u32[]{:S(2)}) async-start(bf16[32,40,256]{2,1,0:T(8,128)(2,1)} %get-tuple-element.39), calls=%async_computation.5 | async-start | bytes 1310720 | tf_op jit(solution)/shard_map/all_to_all | solution.py:592
  139.8 1.2 shard_map.59.seen_ref
  141.2 7.5 %shard_map.60 = (f32[256,512]{1,0:T(8,128)}, f32[256,512]{1,0:T(8,128)}) custom-call(s32[1]{0:T(128)} %bitcast.3.core_ref, bf16[16,160,512]{2,1,0:T(8,128)(2,1)S(1)} %all_to_all.40.own_ref.unit_ref, bf16[2560,1024]{1,0:T(8,128)(2,1)} %get-tuple-element.31.grad_ref, bf16[8,48,256]{2,1,0:T(8,128)(2,1)S(1)} %all_to_all.41.came_ref), custom_call_target="tpu_custom_call" | custom-call | flops 3000000000 | bytes 7000000 | tf_op jit(solution)/shard_map/pallas_call | solution.py:412
  148.9 1.5 shard_map.57.slice_ref
  150.4 2.2 %all-to-all-done.5.came_ref = bf16[32,40,256]{2,1,0:T(8,128)(2,1)S(1)} async-done(((bf16[32,40,256]{2,1,0:T(8,128)(2,1)}), bf16[32,40,256]{2,1,0:T(8,128)(2,1)S(1)}, u32[]{:S(2)}, u32[]{:S(2)}) %all-to-all-start.5) | async-done | bytes 655392 | tf_op jit(solution)/shard_map/all_to_all | solution.py:592
  152.7 0.7 copy-done.2
  153.4 1.2 shard_map.58
  154.6 3.4 %all-to-all-start.6 = ((bf16[8,64,256]{2,1,0:T(8,128)(2,1)}), bf16[8,64,256]{2,1,0:T(8,128)(2,1)S(1)}, u32[]{:S(2)}, u32[]{:S(2)}) async-start(bf16[8,64,256]{2,1,0:T(8,128)(2,1)} %shard_map.58), calls=%async_computation.6 | async-start | bytes 524288 | tf_op jit(solution)/shard_map/all_to_all | solution.py:623
  158.1 11.7 %all-to-all-done.6.came_ref = bf16[8,64,256]{2,1,0:T(8,128)(2,1)S(1)} async-done(((bf16[8,64,256]{2,1,0:T(8,128)(2,1)}), bf16[8,64,256]{2,1,0:T(8,128)(2,1)S(1)}, u32[]{:S(2)}, u32[]{:S(2)}) %all-to-all-start.6) | async-done | bytes 262176 | tf_op jit(solution)/shard_map/all_to_all | solution.py:623
  169.8 4.1 %shard_map.61 = f32[256,512]{1,0:T(8,128)} custom-call(s32[1]{0:T(128)} %bitcast.3.core_ref, bf16[8,64,256]{2,1,0:T(8,128)(2,1)S(1)} %all-to-all-done.6.came_ref, bf16[512,1024]{1,0:T(8,128)(2,1)} %get-tuple-element.41.keep_ref, f32[256,512]{1,0:T(8,128)} %shard_map.59.seen_ref, f32[256,512]{1,0:T(8,128)} %collective-permute-done.2.mate_ref, ...), custom_call_target="tpu_custom_call" | custom-call | flops 1000000000 | bytes 4000000 | tf_op jit(solution)/shard_map/pallas_call | solution.py:412
  173.8 5.9 %all-to-all-start.7 = ((f32[32,8,512]{2,1,0:T(8,128)}), f32[32,8,512]{2,1,0:T(8,128)S(1)}, u32[]{:S(2)}, u32[]{:S(2)}) async-start(f32[32,8,512]{2,1,0:T(8,128)} %bitcast.8), calls=%async_computation.7 | async-start | bytes 1048576 | tf_op jit(solution)/shard_map/all_to_all | solution.py:645
  179.7 1.3 shard_map.62
  181.0 10.3 %all-to-all-done.7 = f32[32,8,512]{2,1,0:T(8,128)S(1)} async-done(((f32[32,8,512]{2,1,0:T(8,128)}), f32[32,8,512]{2,1,0:T(8,128)S(1)}, u32[]{:S(2)}, u32[]{:S(2)}) %all-to-all-start.7) | async-done | bytes 524320 | tf_op jit(solution)/shard_map/all_to_all | solution.py:645
  191.3 0.8 copy.8
  (26 shorter events, 2.3 us)
Async XLA Ops:
  44.5 4.0 %collective-permute-start = (bf16[16,48,512]{2,1,0:T(8,128)(2,1)S(1)}, bf16[16,48,512]{2,1,0:T(8,128)(2,1)S(1)}, u32[]{:S(2)}, u32[]{:S(2)}) collective-permute-start(bf16[16,48,512]{2,1,0:T(8,128)(2,1)S(1)} %slice.4), channel_id=1, source_target_pairs={{0,8},{8,0},{1,9},{9,1},{2,10},{10,2},{3,11},{11,3},{4,12},{12,4},... | collective-permute-start | bytes 2359304 | tf_op jit(solution)/shard_map/ppermute | solution.py:458
  50.6 11.6 %all-to-all-start.1 = ((f32[32,8,128]{2,1,0:T(8,128)}), f32[32,8,128]{2,1,0:T(8,128)S(1)}, u32[]{:S(2)}, u32[]{:S(2)}) async-start(f32[32,8,128]{2,1,0:T(8,128)} %get-tuple-element.26), calls=%async_computation.1 | async-start | bytes 262144 | tf_op jit(solution)/shard_map/all_to_all | solution.py:473
  62.9 15.2 %all-to-all-start.2 = ((f32[8,8,128]{2,1,0:T(8,128)}), f32[8,8,128]{2,1,0:T(8,128)S(1)}, u32[]{:S(2)}, u32[]{:S(2)}) async-start(f32[8,8,128]{2,1,0:T(8,128)} %broadcast_in_dim.2), calls=%async_computation.2 | async-start | bytes 65536 | tf_op jit(solution)/shard_map/all_to_all | solution.py:517
  71.1 0.7 copy-start.5
  80.6 52.3 %copy-start.6 = (bf16[256,512]{1,0:T(8,128)(2,1)S(1)}, bf16[256,512]{1,0:T(8,128)(2,1)}, u32[]{:S(2)}) copy-start(bf16[256,512]{1,0:T(8,128)(2,1)} %get-tuple-element.37.hi_ref) | copy-start | bytes 786436
  80.7 52.2 %copy-start.7 = (bf16[256,512]{1,0:T(8,128)(2,1)S(1)}, bf16[256,512]{1,0:T(8,128)(2,1)}, u32[]{:S(2)}) copy-start(bf16[256,512]{1,0:T(8,128)(2,1)} %get-tuple-element.38.lo_ref) | copy-start | bytes 786436
  80.7 26.5 %all-to-all-start.3 = ((bf16[16,192,256]{2,1,0:T(8,128)(2,1)}), bf16[16,192,256]{2,1,0:T(8,128)(2,1)}, u32[]{:S(2)}, u32[]{:S(2)}) async-start(bf16[16,192,256]{2,1,0:T(8,128)(2,1)} %shard_map.54), calls=%async_computation.3 | async-start | bytes 3145728 | tf_op jit(solution)/shard_map/all_to_all | solution.py:552
  107.1 25.8 %copy-start = (f32[512,1024]{1,0:T(8,128)S(1)}, f32[512,1024]{1,0:T(8,128)}, u32[]{:S(2)}) copy-start(f32[512,1024]{1,0:T(8,128)} %get-tuple-element.35.mass_hbm.mass_ref) | copy-start | bytes 6291460
  127.3 5.6 %collective-permute-start.1 = (bf16[8,48,256]{2,1,0:T(8,128)(2,1)S(1)}, bf16[8,48,256]{2,1,0:T(8,128)(2,1)S(1)}, u32[]{:S(2)}, u32[]{:S(2)}) collective-permute-start(bf16[8,48,256]{2,1,0:T(8,128)(2,1)S(1)} %all_to_all.41.came_ref), channel_id=1, source_target_pairs={{0,8},{8,0},{1,9},{9,1},{2,10},{10,2},{3,11},{11,3},{4,12},{12,4},... | collective-permute-start | bytes 589832 | tf_op jit(solution)/shard_map/ppermute | solution.py:586
  135.6 17.1 %all-to-all-start.5 = ((bf16[32,40,256]{2,1,0:T(8,128)(2,1)}), bf16[32,40,256]{2,1,0:T(8,128)(2,1)S(1)}, u32[]{:S(2)}, u32[]{:S(2)}) async-start(bf16[32,40,256]{2,1,0:T(8,128)(2,1)} %get-tuple-element.39), calls=%async_computation.5 | async-start | bytes 1310720 | tf_op jit(solution)/shard_map/all_to_all | solution.py:592
  140.9 28.8 %copy-start.3 = (f32[1,512]{1,0:T(1,128)S(1)}, f32[1,512]{1,0:T(1,128)}, u32[]{:S(2)}) copy-start(f32[1,512]{1,0:T(1,128)} %get-tuple-element.46.scale_ref) | copy-start | bytes 6148
  140.9 28.8 %copy-start.4 = (f32[1,512]{1,0:T(1,128)S(1)}, f32[1,512]{1,0:T(1,128)}, u32[]{:S(2)}) copy-start(f32[1,512]{1,0:T(1,128)} %get-tuple-element.47.inv_ref) | copy-start | bytes 6148
  140.9 17.1 %collective-permute-start.2 = (f32[256,512]{1,0:T(8,128)}, f32[256,512]{1,0:T(8,128)}, u32[]{:S(2)}, u32[]{:S(2)}) collective-permute-start(f32[256,512]{1,0:T(8,128)} %shard_map.59.seen_ref), channel_id=1, source_target_pairs={{0,8},{8,0},{1,9},{9,1},{2,10},{10,2},{3,11},{11,3},{4,12},{12,4},... | collective-permute-start | bytes 1572872 | tf_op jit(solution)/shard_map/ppermute | solution.py:565
  148.6 9.4 %collective-permute-start.3 = (f32[256,512]{1,0:T(8,128)}, f32[256,512]{1,0:T(8,128)S(1)}, u32[]{:S(2)}, u32[]{:S(2)}) collective-permute-start(f32[256,512]{1,0:T(8,128)} %get-tuple-element.44), channel_id=1, source_target_pairs={{0,8},{8,0},{1,9},{9,1},{2,10},{10,2},{3,11},{11,3},{4,12},{12,4},... | collective-permute-start | bytes 1572872 | tf_op jit(solution)/shard_map/ppermute | solution.py:609
  152.7 0.7 copy-start.2
  154.6 15.1 %all-to-all-start.6 = ((bf16[8,64,256]{2,1,0:T(8,128)(2,1)}), bf16[8,64,256]{2,1,0:T(8,128)(2,1)S(1)}, u32[]{:S(2)}, u32[]{:S(2)}) async-start(bf16[8,64,256]{2,1,0:T(8,128)(2,1)} %shard_map.58), calls=%async_computation.6 | async-start | bytes 524288 | tf_op jit(solution)/shard_map/all_to_all | solution.py:623
  158.1 11.7 %copy-start.8 = (f32[256,512]{1,0:T(8,128)}, f32[256,512]{1,0:T(8,128)S(1)}, u32[]{:S(2)}) copy-start(f32[256,512]{1,0:T(8,128)S(1)} %collective-permute-done.3.term_mate_ref) | copy-start | bytes 1572868
  169.8 10.0 %copy-start.1 = (bf16[160,256]{1,0:T(8,128)(2,1)S(1)}, bf16[160,256]{1,0:T(8,128)(2,1)}, u32[]{:S(2)}) copy-start(bf16[160,256]{1,0:T(8,128)(2,1)} %feat_ref.2) | copy-start | bytes 245764
  173.8 17.4 %all-to-all-start.7 = ((f32[32,8,512]{2,1,0:T(8,128)}), f32[32,8,512]{2,1,0:T(8,128)S(1)}, u32[]{:S(2)}, u32[]{:S(2)}) async-start(f32[32,8,512]{2,1,0:T(8,128)} %bitcast.8), calls=%async_computation.7 | async-start | bytes 1048576 | tf_op jit(solution)/shard_map/all_to_all | solution.py:645

commit v4 on v3

--- a/solution.py
+++ b/solution.py
@@ -119,39 +119,35 @@
     return jnp.sum(total, axis=0, keepdims=True)
 
 
-def pack_kernel(core_ref, teacher_ref, proto_ref, feat_ref, out_ref, unit_ref):
-    first = core_ref[0] == 0
-
+def pack_kernel(teacher_ref, proto_ref, feat_ref, out_ref, unit_ref):
     @pl.when(pl.program_id(0) == 0)
     def _():
         x = feat_ref[...].astype(F32)
         unit = x / jnp.sqrt(jnp.sum(x * x, axis=1, keepdims=True) + 1e-06)
-        unit = unit.astype(BF16)
-        unit_ref[:, :256] = unit[:80]
-        unit_ref[:, 256:] = unit[80:]
-
-    for p in range(8):
-        left = encode_logits(teacher_ref[:, 1024 * p : 1024 * p + 512])
-        right = encode_logits(teacher_ref[:, 1024 * p + 512 : 1024 * p + 1024])
-        out_ref[p, 0:32, :] = jnp.where(first, left, right)
-        out_ref[p, 32:64, :] = jnp.where(first, right, left)
-        w = proto_ref[:, 1024 * p : 1024 * p + 1024].astype(F32)
-        out_ref[p, 64:80, :] = jnp.concatenate([w[:, :512], w[:, 512:]], axis=0).astype(BF16)
-        out_ref[p, 80:160, :] = unit_ref[...]
-
-
-def first_kernel(core_ref, own_ref, mate_ref, mass_ref, out_ref):
-    first = core_ref[0] == 0
-    for j in range(4):
-        own = decode_exp(own_ref[4 * j : 4 * j + 4].reshape(128, 512)).T
-        mate = decode_exp(mate_ref[4 * j : 4 * j + 4].reshape(128, 512)).T
-        mass_ref[:, 128 * j : 128 * j + 128] = jnp.where(first, own, mate)
-        mass_ref[:, 512 + 128 * j : 640 + 128 * j] = jnp.where(first, mate, own)
+        unit_ref[...] = unit.astype(BF16)
+
+    for p in range(16):
+        cols = 512 * p
+        out_ref[p, 0:32, :] = encode_logits(teacher_ref[:, cols : cols + 256]).astype(BF16)
+        out_ref[p, 32:64, :] = encode_logits(teacher_ref[:, cols + 256 : cols + 512]).astype(BF16)
+        w = proto_ref[:, cols : cols + 512].astype(F32)
+        out_ref[p, 64:80, :] = jnp.concatenate([w[:, :256], w[:, 256:]], axis=0).astype(BF16)
+        out_ref[p, 80:160, :] = unit_ref[80 * (p % 2) : 80 * (p % 2) + 80, :]
+
+
+def first_kernel(own_ref, mass_ref, out_ref):
+    for h in range(2):
+        for j in range(4):
+            cols = slice(512 * h + 128 * j, 512 * h + 128 * j + 128)
+            for side in range(2):
+                low = 32 * side + 16 * h
+                block = own_ref[8 * j : 8 * j + 8, low : low + 16, :].reshape(128, 256)
+                mass_ref[256 * side : 256 * side + 256, cols] = decode_exp(block).T
     part = rows8(sweep(mass_ref, None))
     out_ref[...] = jnp.broadcast_to(part[None], (32, 8, 128))
 
 
-def second_kernel(came_ref, mass_hbm, pack_ref, out_ref, mass_ref, sems):
+def second_kernel(came_ref, sum_ref, mass_hbm, pack_ref, out_ref, mass_ref, sems):
     copies = [
         pltpu.make_async_copy(mass_hbm.at[pl.ds(64 * i, 64), :], mass_ref.at[pl.ds(64 * i, 64), :], sems.at[i])
         for i in range(8)
@@ -159,40 +155,57 @@
     for copy in copies:
         copy.start()
     row_inv = lanes(1.0 / jnp.sum(came_ref[...], axis=0))
-    row = padded(split_row(rows8(sweep(mass_ref, row_inv, copies=copies))))
-    out_ref[...] = jnp.broadcast_to(row[None], (16, 16, 256))
+    part = rows8(sweep(mass_ref, row_inv, copies=copies) * row_inv)
+    part = root_code(part * WIDE)
+    part = jnp.concatenate([part[:, :64], part[:, 64:]], axis=0)
+    row = jnp.concatenate([sum_code(sum_ref[...])[:, :192], part], axis=1).astype(BF16)
+    out_ref[...] = jnp.broadcast_to(row[None], (32, 16, 256))
 
 
 def home_kernel(place_ref, came_ref, out_ref):
+    core = place_ref[2]
     pick = lax.broadcasted_iota(jnp.int32, (16, 256), 0) == place_ref[0]
+    row_sum = jnp.zeros((16, 256), F32)
+    parts = [[], []]
+    for p in range(32):
+        row_sum = row_sum + root_decode(came_ref[p, 80:96, :])
+        exp_part = sum_decode(came_ref[p, 80:96, :])
+        parts[p % 2].append(jnp.sum(jnp.where(pick, exp_part, 0.0), axis=0, keepdims=True))
     exp_sum = jnp.zeros((16, 256), F32)
-    row_sum = jnp.zeros((8, 256), F32)
-    parts = []
     for p in range(16):
-        exp_part = sum_decode(came_ref[p, 160:176, :])
-        exp_sum = exp_sum + exp_part
-        row_sum = row_sum + came_ref[p, 176:192, :].astype(F32)[:8]
-        parts.append(jnp.sum(jnp.where(pick, exp_part, 0.0), axis=0, keepdims=True))
-    parts = columns(jnp.concatenate(parts, axis=0) * (1.0 / ROOT))
-    scale = 1.0 / jnp.sum(parts, axis=1, keepdims=True)
+        exp_sum = exp_sum + sum_decode(came_ref[2 * p + core, 80:96, :])
     code = []
-    for low in range(0, 160, 32):
-        home = jnp.zeros((32, 256), F32)
-        for p in range(16):
-            home = home + root_decode(came_ref[p, low : low + 32, :]) * parts[low : low + 32, p : p + 1]
-        code.append(fine_code(home * scale[low : low + 32]))
+    home_sum = []
+    for half in range(2):
+        x = jnp.concatenate(parts[half], axis=0)
+        x = jnp.where(core == 0, x[:, :80], x[:, 80:160])
+        home_sum.append(jnp.sum(x, axis=0, keepdims=True))
+        x = jnp.concatenate([x, jnp.ones((16, 176), F32)], axis=1)
+        x = columns(x * (1.0 / ROOT))[:80]
+        scale = 1.0 / jnp.sum(x, axis=1, keepdims=True)
+        for low in range(0, 80, 16):
+            home = jnp.zeros((16, 256), F32)
+            for p in range(16):
+                part = root_decode(came_ref[2 * p + half, low : low + 16, :])
+                home = home + part * x[low : low + 16, p : p + 1]
+            code.append(fine_code(home * scale[low : low + 16]))
     code = jnp.concatenate(code, axis=0)
-    tail = [jnp.zeros((4, 256), F32), split_row(join_row(row_sum)), sum_code(exp_sum * (1.0 / 16.0))]
+    home_sum = jnp.concatenate(home_sum + [jnp.ones((1, 96), F32)], axis=1)
+    row_sum = jnp.concatenate([row_sum[:8, 192:], row_sum[8:, 192:]], axis=1)
+    lane = lax.broadcasted_iota(jnp.int32, (16, 256), 1)
+    exp_sum = jnp.where(lane < 160, exp_sum, 1.0)
+    tail = [
+        sum_code(home_sum * (1.0 / 16.0)),
+        jnp.zeros((3, 256), F32),
+        split_row(row_sum),
+        sum_code(exp_sum * (1.0 / 16.0)),
+    ]
     for z in range(8):
         out_ref[z] = jnp.concatenate([code[20 * z : 20 * z + 20]] + tail, axis=0).astype(BF16)
 
 
 def slice_kernel(place_ref, came_ref, out_ref):
-    pick = lax.broadcasted_iota(jnp.int32, (16, 256), 0) == place_ref[0]
-    parts = []
-    for p in range(8):
-        exp_part = sum_decode(came_ref[p, 32:48, :]) * 16.0
-        parts.append(jnp.sum(jnp.where(pick, exp_part, 0.0), axis=0, keepdims=True))
+    parts = [sum_decode(came_ref[p, 16:32, :])[4:5] * 16.0 for p in range(8)]
     parts = pltpu.roll(jnp.concatenate(parts, axis=0), (256 - 20 * place_ref[1]) % 256, 1)
     parts = columns(parts)[:32]
     home = jnp.zeros((32, 256), F32)
@@ -203,37 +216,44 @@
     out_ref[...] = fine_code(home * (weight / jnp.sum(parts, axis=1, keepdims=True)))[:24]
 
 
-def third_kernel(came_ref, came_mate_ref, mass_ref, hi_ref, lo_ref, keep_ref, out_ref):
+def third_kernel(came_ref, came_one_ref, mass_ref, hi_ref, lo_ref, keep_ref, out_ref):
     rows = jnp.zeros((16, 256), F32)
     for p in range(8):
-        rows = rows + (came_ref[p, 16:32, :].astype(F32) + came_mate_ref[p, 16:32, :].astype(F32))
-    row_inv = lanes(1.0 / join_row(rows[8:]))
+        rows = rows + came_ref[p, 16:32, :].astype(F32)
+    row_inv = lanes(WIDE / (join_row(rows[8:]) * jnp.sum(came_one_ref[...], axis=0)))
     part = sweep(mass_ref, row_inv, keep_ref)
     scale = ROOT / part
     tail = split_row(rows8(part))
-    for j in range(8):
-        keep = keep_ref[:, 128 * j : 128 * j + 128]
-        x = jnp.dot(hi_ref[...], keep, preferred_element_type=F32)
-        x = x + jnp.dot(lo_ref[...], keep, preferred_element_type=F32)
-        x = (x * scale[:, 128 * j : 128 * j + 128]).T
-        x = root_code(x)
-        for i in range(4):
-            block = 4 * j + i
-            out_ref[block % 16 * 2 + block // 16] = jnp.concatenate([x[32 * i : 32 * i + 32], tail], axis=0).astype(BF16)
+    for j in range(4):
+        both = []
+        for h in range(2):
+            cols = slice(512 * h + 128 * j, 512 * h + 128 * j + 128)
+            keep = keep_ref[:, cols]
+            x = jnp.dot(hi_ref[...], keep, preferred_element_type=F32)
+            x = x + jnp.dot(lo_ref[...], keep, preferred_element_type=F32)
+            both.append(root_code((x * scale[:, cols]).T))
+        for i in range(8):
+            rows = slice(16 * i, 16 * i + 16)
+            out_ref[8 * j + i] = jnp.concatenate([both[0][rows], both[1][rows], tail], axis=0).astype(BF16)
+
+
+def home_columns(rows, index, turn_ref):
+    pick = lax.broadcasted_iota(jnp.int32, (8, 128), 0) - index // 8
+    pad = jnp.zeros((128 - len(rows), 128), F32)
+    both = []
+    for h in range(2):
+        picked = [jnp.sum(jnp.where(pick == 4 * h, row, 0.0), axis=0, keepdims=True) for row in rows]
+        turn_ref[...] = jnp.concatenate(picked + [pad], axis=0).T
+        both.append(turn_ref[pl.ds(pl.multiple_of(index % 8 * 16, 16), 16), :])
+    return jnp.concatenate(both, axis=0)
 
 
 def target_kernel(index_ref, came_ref, slice_ref, out_ref, turn_ref):
-    index = index_ref[0]
-    pick = lax.broadcasted_iota(jnp.int32, (8, 128), 0) == index // 4
-    row_sum = jnp.zeros((8, 128), F32)
-    parts = []
-    for p in range(32):
-        row = join_row(came_ref[p].astype(F32)[32:])
-        row_sum = row_sum + row
-        parts.append(jnp.sum(jnp.where(pick, row, 0.0), axis=0, keepdims=True))
-    parts = jnp.concatenate(parts, axis=0) * (1.0 / ROOT)
-    turn_ref[...] = jnp.concatenate([parts, jnp.zeros((96, 128), F32)], axis=0).T
-    parts = turn_ref[pl.ds(pl.multiple_of(index % 4 * 32, 32), 32), :]
+    rows = [join_row(came_ref[p].astype(F32)[32:]) for p in range(32)]
+    row_sum = rows[0]
+    for p in range(1, 32):
+        row_sum = row_sum + rows[p]
+    parts = home_columns(rows, index_ref[0], turn_ref) * (1.0 / ROOT)
     total = jnp.zeros((32, 256), F32)
     for p in range(32):
         total = total + root_decode(came_ref[p])[:32] * parts[:, p : p + 1]
@@ -243,15 +263,8 @@
 
 
 def feat_kernel(index_ref, came_ref, feat_ref, out_ref, turn_ref):
-    index = index_ref[0]
-    pick = lax.broadcasted_iota(jnp.int32, (8, 128), 0) == index // 4
-    parts = []
-    for p in range(8):
-        row = join_row(came_ref[p, 48:64, :].astype(F32)[8:])
-        parts.append(jnp.sum(jnp.where(pick, row, 0.0), axis=0, keepdims=True))
-    parts = jnp.concatenate(parts + [jnp.zeros((120, 128), F32)], axis=0)
-    turn_ref[...] = parts.T
-    parts = turn_ref[pl.ds(pl.multiple_of(index % 4 * 32, 32), 32), :]
+    rows = [join_row(came_ref[p, 48:64, :].astype(F32)[8:]) for p in range(8)]
+    parts = home_columns(rows, index_ref[0], turn_ref)
     target = jnp.zeros((32, 256), F32)
     for p in range(8):
         target = target + fine_decode(came_ref[p, 0:32, :]) * parts[:, p : p + 1]
@@ -306,16 +319,19 @@
         first = core_ref[0] == 0
         squares = jnp.zeros((8, 1024), F32)
         for p in range(16):
-            own = own_ref[p].astype(F32)
-            mate = mate_ref[p].astype(F32)
-            low = jnp.where(first, own, mate)
-            high = jnp.where(first, mate, own)
-            left = jnp.concatenate([low[:8], high[:8]], axis=0)
-            right = jnp.concatenate([low[8:], high[8:]], axis=0)
+            block = []
+            for ref in (own_ref, mate_ref):
+                x = ref[2 * p].astype(F32)
+                y = ref[2 * p + 1].astype(F32)
+                top = jnp.concatenate([x[:8], x[8:]], axis=1)
+                block.append(jnp.concatenate([top, jnp.concatenate([y[:8], y[8:]], axis=1)], axis=0))
+            own, mate = block
+            left = jnp.where(first, own, mate)
+            right = jnp.where(first, mate, own)
             rows = slice(16 * p, 16 * p + 16)
             all_ref[rows, :512] = left.astype(BF16)
             all_ref[rows, 512:] = right.astype(BF16)
-            my_ref[rows, :] = jnp.where(first, left, right).astype(BF16)
+            my_ref[rows, :] = own.astype(BF16)
             both = jnp.concatenate([left, right], axis=1)
             both = both * both
             squares = squares + (both[:8] + both[8:])
@@ -336,7 +352,7 @@
     sums = []
     for p in range(4):
         for half in range(2):
-            raw = dot(unit_ref[p, :, 256 * half : 256 * half + 256], all_ref[...], NN)
+            raw = dot(unit_ref[2 * p + half], all_ref[...], NN)
             prob = jnp.exp2(raw * power)
             sums.append(jnp.sum(prob, axis=1, keepdims=True))
             out_ref[160 * p + 80 * half : 160 * p + 80 * half + 80, :] = (prob * scale).astype(BF16)
@@ -347,27 +363,22 @@
     sum_ref[...] = jnp.where(row // 4 == step, jnp.concatenate([sums] * 4, axis=0), sum_ref[...])
 
 
-def student_kernel(grad_ref, weight_ref, part_ref, sum_ref, out_ref):
+def student_kernel(grad_ref, weight_ref, part_ref, out_ref):
     scale = columns(ROOT / part_ref[...])
-    sums = sum_code(sum_ref[...]).astype(BF16)
     for p in range(8):
         x = dot(grad_ref[160 * p : 160 * p + 160, :], weight_ref[...], NT)
-        out_ref[p, 0:160, :] = root_code(x * scale[:160, p : p + 1]).astype(BF16)
-        out_ref[p, 160:176, :] = sums
+        x = root_code(x * scale[:160, p : p + 1]).astype(BF16)
+        out_ref[2 * p, 0:80, :] = x[:80]
+        out_ref[2 * p + 1, 0:80, :] = x[80:]
 
 
 def seen_kernel(unit_ref, out_ref):
-    row = lax.broadcasted_iota(jnp.int32, (32, 80), 0)
-    col = lax.broadcasted_iota(jnp.int32, (32, 80), 1)
+    row = lax.broadcasted_iota(jnp.int32, (16, 80), 0)
+    col = lax.broadcasted_iota(jnp.int32, (16, 80), 1)
     keep = (col // CROPS == row // GLOBAL) & (col % CROPS != row % GLOBAL)
-    after = (col // CROPS + 80 // CROPS == row // GLOBAL) & (col % CROPS != row % GLOBAL)
     keep = jnp.where(keep, 1.0, 0.0).astype(BF16)
-    after = jnp.where(after, 1.0, 0.0).astype(BF16)
     for j in range(4):
-        block = [
-            dot(keep, unit_ref[p, :, :256], NN) + dot(after, unit_ref[p, :, 256:], NN)
-            for p in range(4 * j, 4 * j + 4)
-        ]
+        block = [dot(keep, unit_ref[p], NN) for p in range(8 * j, 8 * j + 8)]
         out_ref[:, 128 * j : 128 * j + 128] = jnp.concatenate(block, axis=0).T
 
 
@@ -384,7 +395,7 @@
     for j in range(2):
         parts = []
         for p in range(4 * j, 4 * j + 4):
-            unit = jnp.concatenate([unit_ref[p, :, :256], unit_ref[p, :, 256:]], axis=0).astype(F32)
+            unit = jnp.concatenate([unit_ref[2 * p], unit_ref[2 * p + 1]], axis=0).astype(F32)
             parts.append(unit * factor[:160, p : p + 1])
         hi, lo = split(jnp.concatenate(parts, axis=0))
         grad = grad_ref[640 * j : 640 * j + 640, :]
@@ -430,50 +441,40 @@
 def shards(student_feat, prototypes, teacher_logits):
     core = lax.axis_index("core")
     core_arg = core.reshape(1)
-    chip = lax.axis_index(PLANE)
-    block = core * 16 + chip
-    place = jnp.stack([chip, lax.axis_index("proto")])
+    index = lax.axis_index(BATCH).reshape(1)
+    place = jnp.stack([lax.axis_index(PLANE), lax.axis_index("proto"), core])
+    whole = lambda *dims: pl.BlockSpec(dims, lambda i: (0,) * len(dims))
 
     send = call(
         pack_kernel,
-        shape((16, 160, 512), BF16),
+        shape((32, 160, 256), BF16),
         10**7,
         5 * 10**6,
-        core_arg,
         teacher_logits,
         prototypes,
         student_feat,
-        specs=[
-            SMEM,
-            pl.BlockSpec((32, 8192), lambda i: (0, i)),
-            pl.BlockSpec((8, 8192), lambda i: (0, i)),
-            pl.BlockSpec((160, 256), lambda i: (0, 0)),
-        ],
-        out_specs=pl.BlockSpec((8, 160, 512), lambda i: (i, 0, 0)),
-        scratch_shapes=[pltpu.VMEM((80, 512), BF16)],
+        specs=[pl.BlockSpec((32, 8192), lambda i: (0, i)), pl.BlockSpec((8, 8192), lambda i: (0, i)), whole(160, 256)],
+        out_specs=pl.BlockSpec((16, 160, 256), lambda i: (i, 0, 0)),
+        scratch_shapes=[pltpu.VMEM((160, 256), BF16)],
         grid=(2,),
         room=56,
     )
-    got = lax.all_to_all(send, PLANE, 0, 0, tiled=True)
-    mate = lax.ppermute(got[:, 32:80], "core", SWAP)
-    half = pl.BlockSpec((16, 32, 512), lambda i: (0, 0, 0))
-
+    got = lax.all_to_all(send, BATCH, 0, 0, tiled=True)
+
+    mate = lax.ppermute(got[:, 64:80], "core", SWAP)
     mass, pack = call(
         first_kernel,
         (shape((512, 1024)), shape((32, 8, 128))),
         10**7,
         3 * 10**6,
-        core_arg,
         got,
-        mate,
-        specs=[SMEM, half, half],
+        specs=[whole(32, 64, 256)],
         out_specs=(VMEM, VMEM),
         grid=(1,),
     )
+    got, mate, pack = lax.optimization_barrier((got, mate, pack))
     came = lax.all_to_all(pack, BATCH, 0, 0, tiled=True)
     row_sum = jnp.sum(came, axis=0)
-    got, mate, _ = lax.optimization_barrier((got, mate, pack))
-    whole = lambda *dims: pl.BlockSpec(dims, lambda i: (0,) * len(dims))
     grad_prob, exp_part, weights, my_weights, my_scale, my_inv, unit_hi, unit_lo = call(
         exp_kernel,
         (
@@ -494,9 +495,9 @@
         got,
         specs=[
             SMEM,
-            pl.BlockSpec((16, 16, 512), lambda i: (0, 4, 0)),
-            pl.BlockSpec((16, 16, 512), lambda i: (0, 2, 0)),
-            pl.BlockSpec((4, 80, 512), lambda i: (i, 1, 0)),
+            pl.BlockSpec((32, 16, 256), lambda i: (0, 4, 0)),
+            whole(32, 16, 256),
+            pl.BlockSpec((8, 80, 256), lambda i: (i, 1, 0)),
         ],
         out_specs=(
             pl.BlockSpec((640, 1024), lambda i: (i, 0)),
@@ -511,45 +512,44 @@
         scratch_shapes=[pltpu.VMEM((1, 1024), F32)],
         grid=(4,),
     )
-    unit_spec = pl.BlockSpec((8, 80, 512), lambda i: (i, 1, 0))
+    unit_spec = pl.BlockSpec((16, 80, 256), lambda i: (i, 1, 0))
 
     grad_prob, row_sum = lax.optimization_barrier((grad_prob, row_sum))
     came_one = lax.all_to_all(jnp.broadcast_to(row_sum[None], (8, 8, 128)), "proto", 0, 0, tiled=True)
     student_pack = call(
         student_kernel,
-        shape((16, 192, 256), BF16),
+        shape((32, 96, 256), BF16),
         2 * 10**9,
         7 * 10**6,
         hbm(grad_prob),
         hbm(weights),
         exp_part,
-        exp_part,
         specs=[
             pl.BlockSpec((1280, 1024), lambda i: (i, 0)),
             whole(256, 1024),
             pl.BlockSpec((8, 256), lambda i: (i, 0)),
-            VMEM,
         ],
-        out_specs=pl.BlockSpec((8, 192, 256), lambda i: (i, 0, 0)),
+        out_specs=pl.BlockSpec((16, 96, 256), lambda i: (i, 0, 0)),
         grid=(2,),
     )
     came_one, student_pack = lax.optimization_barrier((came_one, student_pack))
 
     pack = call(
         second_kernel,
-        shape((16, 192, 256), BF16),
+        shape((32, 96, 256), BF16),
         10**7,
         2 * 10**6,
         came_one,
+        exp_part,
         hbm(mass),
         hbm(student_pack),
-        specs=[VMEM, pl.BlockSpec(memory_space=pltpu.HBM), pl.BlockSpec(memory_space=pltpu.HBM)],
-        out_specs=pl.BlockSpec((16, 16, 256), lambda i: (0, 11, 0)),
+        specs=[VMEM, VMEM, pl.BlockSpec(memory_space=pltpu.HBM), pl.BlockSpec(memory_space=pltpu.HBM)],
+        out_specs=pl.BlockSpec((32, 16, 256), lambda i: (0, 5, 0)),
         scratch_shapes=[pltpu.VMEM((512, 1024), F32), pltpu.SemaphoreType.DMA((8,))],
         grid=(1,),
-        input_output_aliases={2: 0},
-    )
-    came = lax.all_to_all(pack, PLANE, 0, 0, tiled=True)
+        input_output_aliases={3: 0},
+    )
+    came = lax.all_to_all(pack, BATCH, 0, 0, tiled=True)
 
     got, _ = lax.optimization_barrier((got, pack))
     seen = call(
@@ -558,7 +558,7 @@
         10**8,
         2 * 10**6,
         got,
-        specs=[pl.BlockSpec((16, 80, 512), lambda i: (0, 1, 0))],
+        specs=[pl.BlockSpec((32, 80, 256), lambda i: (0, 1, 0))],
         out_specs=VMEM,
         grid=(1,),
     )
@@ -571,7 +571,7 @@
         2 * 10**6,
         place,
         hbm(came),
-        specs=[SMEM, whole(16, 192, 256)],
+        specs=[SMEM, whole(32, 96, 256)],
         out_specs=whole(8, 48, 256),
         grid=(1,),
     )
@@ -583,7 +583,7 @@
         10**9,
         4 * 10**6,
         came_two,
-        lax.ppermute(came_two, "core", SWAP),
+        came_one,
         mass,
         unit_hi,
         unit_lo,
@@ -614,7 +614,7 @@
         shape((8, 64, 256), BF16),
         10**7,
         10**6,
-        block.reshape(1),
+        index,
         came,
         home_slice,
         out_specs=VMEM,
@@ -649,7 +649,7 @@
         shape((160, 256)),
         10**7,
         10**6,
-        block.reshape(1),
+        index,
         came,
         student_feat,
         out_specs=VMEM,

time: 193 us -> 191 us (0.990)
    all_to_all x2 -> x3, waiting for transfers between devices: 3.32 us -> 25.5 us  [shards(): came = lax.all_to_all(pack, BATCH, 0, 0, tiled=True)]
    all_to_all x1 -> x0, waiting for transfers between devices: 20.5 us -> none  [shards(): came = lax.all_to_all(pack, PLANE, 0, 0, tiled=True)]
    all_to_all x2 -> x3, starting transfers between devices: 8.06 us -> 18.7 us  [shards(): came = lax.all_to_all(pack, BATCH, 0, 0, tiled=True)]
    ppermute x2 -> x1, starting transfers between devices: 6.57 us -> 0.53 us  [shards(): mate = lax.ppermute(got[:, 64:80], 'core', SWAP)]
    all_to_all x1 -> x0, starting transfers between devices: 5.84 us -> none  [shards(): came = lax.all_to_all(pack, PLANE, 0, 0, tiled=True)]
    ppermute x2 -> x1, waiting for transfers between devices: 2.98 us -> 0.01 us  [shards(): mate = lax.ppermute(got[:, 64:80], 'core', SWAP)]
    all_to_all x1, blocking collectives: 16.7 us -> 14.4 us  [shards(): came_two = lax.all_to_all(pack, 'proto', 0, 0, tiled=True)]
    all_to_all x1, blocking collectives: 40.6 us -> 42.6 us  [shards(): got = lax.all_to_all(send, BATCH, 0, 0, tiled=True)]
  transfers between devices with their start and end apart: 10 -> 9, of which waited for: 8 -> 6; matrix products, arithmetic and copies ran while one was open for 0% -> 0% of each run, Pallas kernels for 13% -> 14%
where the time goes in v4:
time: 191 us; the launch traced here: 190 us
  blocking collectives  57 us (30%)
  waiting for transfers between devices  47.6 us (25%)
  Pallas kernels  44.2 us (23%)
  starting transfers between devices  37.1 us (19%)
  local copies, waits for them, and re-layouts  2.92 us (2%)
    pallas_call x13, Pallas kernels, call(): pl.pallas_call(kernel, out_shape=shapes, in_specs=specs, cost_estimate=pl...  44.2 us
    all_to_all x1, blocking collectives, shards(): got = lax.all_to_all(send, BATCH, 0, 0, tiled=True)  42.6 us
    all_to_all x3, waiting for transfers between devices, shards(): came = lax.all_to_all(pack, BATCH, 0, 0, tiled=True)  25.5 us
    all_to_all x3, starting transfers between devices, shards(): came = lax.all_to_all(pack, BATCH, 0, 0, tiled=True)  18.7 us
    all_to_all x1, blocking collectives, shards(): came_two = lax.all_to_all(pack, 'proto', 0, 0, tiled=True)  14.4 us
    all_to_all x1, waiting for transfers between devices, shards(): came = lax.all_to_all(pack, 'proto', 0, 0, tiled=True)  11.7 us
    all_to_all x1, waiting for transfers between devices, shards(): grad = lax.all_to_all(grad.reshape(32, 8, 512), BATCH, 0, 0, tiled=True)  10.2 us
    all_to_all x1, starting transfers between devices, shards(): lax.all_to_all(jnp.broadcast_to(row_sum[None], (8, 8, 128)), 'proto', 0,...  8.19 us
  transfers between devices with their start and end apart: 9, of which 6 were waited for; matrix products, arithmetic and copies ran while one was open for 0% of the time, Pallas kernels for 14%

profile of v4, /device:TPU:1, one launch (start us, length us, event | category | flops | bytes accessed | tf_op | source)
XLA Modules:
  0.0 189.8 jit_solution(4433294947562430680)
XLA Ops:
  0.6 3.1 %shard_map.50 = bf16[32,160,256]{2,1,0:T(8,128)(2,1)} custom-call(f32[32,16384]{1,0:T(8,128)} %teacher_ref.1, bf16[8,16384]{1,0:T(8,128)(2,1)} %proto_ref.1, bf16[160,256]{1,0:T(8,128)(2,1)} %feat_ref.2), custom_call_target="tpu_custom_call" | custom-call | flops 10000000 | bytes 5000000 | tf_op jit(solution)/shard_map/pallas_call | solution.py:423
  3.8 42.6 %all_to_all.40.own_ref.unit_ref = bf16[32,160,256]{2,1,0:T(8,128)(2,1)S(1)} all-to-all(bf16[32,160,256]{2,1,0:T(8,128)(2,1)} %shard_map.50), channel_id=1, replica_groups=mesh['y'=4,'x'=4,'core'=2,'proto'=8] {'y','x','core'}, dimensions={0} | all-to-all | bytes 5242880 | tf_op jit(solution)/shard_map/all_to_all | solution.py:462
  46.4 0.5 collective-permute-start
  46.9 2.0 %shard_map.51 = (f32[512,1024]{1,0:T(8,128)}, f32[32,8,128]{2,1,0:T(8,128)}) custom-call(bf16[32,160,256]{2,1,0:T(8,128)(2,1)S(1)} %all_to_all.40.own_ref.unit_ref), custom_call_target="tpu_custom_call" | custom-call | flops 10000000 | bytes 3000000 | tf_op jit(solution)/shard_map/pallas_call | solution.py:423
  49.0 3.7 %all-to-all-start.1 = ((f32[32,8,128]{2,1,0:T(8,128)}), f32[32,8,128]{2,1,0:T(8,128)S(1)}, u32[]{:S(2)}, u32[]{:S(2)}) async-start(f32[32,8,128]{2,1,0:T(8,128)} %get-tuple-element.31), calls=%async_computation.1 | async-start | bytes 262144 | tf_op jit(solution)/shard_map/all_to_all | solution.py:476
  52.7 6.6 %shard_map.52 = (bf16[2560,1024]{1,0:T(8,128)(2,1)}, f32[16,256]{1,0:T(8,128)}, bf16[256,1024]{1,0:T(8,128)(2,1)}, bf16[256,512]{1,0:T(8,128)(2,1)}, f32[1,512]{...) custom-call(s32[1]{0:T(128)} %bitcast.3.core_ref, ...), custom_call_target="tpu_custom_call" | custom-call | flops 2000000000 | bytes 9000000 | tf_op jit(solution)/shard_map/pallas_call | solution.py:423
  59.2 1.1 all-to-all-done.1
  60.3 0.6 broadcast_in_dim.2
  61.0 8.2 %all-to-all-start.2 = ((f32[8,8,128]{2,1,0:T(8,128)}), f32[8,8,128]{2,1,0:T(8,128)S(1)}, u32[]{:S(2)}, u32[]{:S(2)}) async-start(f32[8,8,128]{2,1,0:T(8,128)} %broadcast_in_dim.2), calls=%async_computation.2 | async-start | bytes 65536 | tf_op jit(solution)/shard_map/all_to_all | solution.py:518
  69.2 0.7 copy-done.3
  69.9 6.0 %shard_map.53.pack_ref = bf16[32,96,256]{2,1,0:T(8,128)(2,1)} custom-call(bf16[2560,1024]{1,0:T(8,128)(2,1)} %get-tuple-element.33.grad_ref, bf16[256,1024]{1,0:T(8,128)(2,1)} %get-tuple-element.34.weight_ref, f32[16,256]{1,0:T(8,128)S(1)} %copy-done.3), custom_call_target="tpu_custom_call" | custom-call | flops 2000000000 | bytes 7000000 | tf_op jit(solution)/shard_map/pallas_call | solution.py:423
  76.1 2.8 %shard_map.54 = bf16[32,96,256]{2,1,0:T(8,128)(2,1)} custom-call(f32[8,8,128]{2,1,0:T(8,128)S(1)} %all-to-all-done.2.came_ref.came_one_ref, f32[16,256]{1,0:T(8,128)S(1)} %copy-done.4, f32[512,1024]{1,0:T(8,128)} %get-tuple-element.37.mass_hbm.mass_ref, bf16[32,96,256]{2,1,0:T(8,128)(2,1)} %shard_map.53.pack_ref), custom_call_target="tpu_custom_call", output_to_operand_aliasing={{}: (3, {})} | custom-call | flops 10000000 | bytes 2000000 | tf_op jit(solution)/shard_map/pallas_call | solution.py:423
  79.0 7.9 %all-to-all-start.3 = ((bf16[32,96,256]{2,1,0:T(8,128)(2,1)}), bf16[32,96,256]{2,1,0:T(8,128)(2,1)}, u32[]{:S(2)}, u32[]{:S(2)}) async-start(bf16[32,96,256]{2,1,0:T(8,128)(2,1)} %shard_map.54), calls=%async_computation.3 | async-start | bytes 3145728 | tf_op jit(solution)/shard_map/all_to_all | solution.py:552
  86.9 22.2 %all-to-all-done.3.came_ref = bf16[32,96,256]{2,1,0:T(8,128)(2,1)} async-done(((bf16[32,96,256]{2,1,0:T(8,128)(2,1)}), bf16[32,96,256]{2,1,0:T(8,128)(2,1)}, u32[]{:S(2)}, u32[]{:S(2)}) %all-to-all-start.3) | async-done | bytes 1572896 | tf_op jit(solution)/shard_map/all_to_all | solution.py:552
  109.1 4.1 %shard_map.55 = bf16[8,48,256]{2,1,0:T(8,128)(2,1)} custom-call(s32[3]{0:T(128)S(1)} %pad_add_fusion.place_ref, bf16[32,96,256]{2,1,0:T(8,128)(2,1)} %all-to-all-done.3.came_ref), custom_call_target="tpu_custom_call" | custom-call | flops 10000000 | bytes 2000000 | tf_op jit(solution)/shard_map/pallas_call | solution.py:423
  113.2 14.4 %all_to_all.41.came_ref = bf16[8,48,256]{2,1,0:T(8,128)(2,1)S(1)} all-to-all(bf16[8,48,256]{2,1,0:T(8,128)(2,1)} %shard_map.55), channel_id=1, replica_groups=mesh['y'=4,'x'=4,'core'=2,'proto'=8] {'proto'}, dimensions={0} | all-to-all | bytes 393216 | tf_op jit(solution)/shard_map/all_to_all | solution.py:578
  127.7 2.7 %shard_map.56 = (bf16[512,1024]{1,0:T(8,128)(2,1)}, bf16[32,40,256]{2,1,0:T(8,128)(2,1)}) custom-call(bf16[8,48,256]{2,1,0:T(8,128)(2,1)S(1)} %all_to_all.41.came_ref, f32[8,8,128]{2,1,0:T(8,128)S(1)} %all-to-all-done.2.came_ref.came_one_ref, f32[512,1024]{1,0:T(8,128)S(1)} %copy-done, bf16[256,512]{1,0:T(8,128)(2,1)S(1)} %copy-done.7, ...), custom_call_target="tpu_custom_call" | custom-call | flops 1000000000 | bytes 4000000 | tf_op jit(solution)/shard_map/pallas_call | solution.py:423
  130.3 7.2 %all-to-all-start.5 = ((bf16[32,40,256]{2,1,0:T(8,128)(2,1)}), bf16[32,40,256]{2,1,0:T(8,128)(2,1)S(1)}, u32[]{:S(2)}, u32[]{:S(2)}) async-start(bf16[32,40,256]{2,1,0:T(8,128)(2,1)} %get-tuple-element.41), calls=%async_computation.5 | async-start | bytes 1310720 | tf_op jit(solution)/shard_map/all_to_all | solution.py:592
  137.5 1.2 shard_map.59.seen_ref
  138.9 7.5 %shard_map.60 = (f32[256,512]{1,0:T(8,128)}, f32[256,512]{1,0:T(8,128)}) custom-call(s32[1]{0:T(128)} %bitcast.3.core_ref, bf16[32,160,256]{2,1,0:T(8,128)(2,1)S(1)} %all_to_all.40.own_ref.unit_ref, bf16[2560,1024]{1,0:T(8,128)(2,1)} %get-tuple-element.33.grad_ref, bf16[8,48,256]{2,1,0:T(8,128)(2,1)S(1)} %all_to_all.41.came_ref), custom_call_target="tpu_custom_call" | custom-call | flops 3000000000 | bytes 7000000 | tf_op jit(solution)/shard_map/pallas_call | solution.py:423
  146.4 0.3 collective-permute-start.2
  146.6 1.5 shard_map.57.slice_ref
  148.1 2.3 %all-to-all-done.5.came_ref = bf16[32,40,256]{2,1,0:T(8,128)(2,1)S(1)} async-done(((bf16[32,40,256]{2,1,0:T(8,128)(2,1)}), bf16[32,40,256]{2,1,0:T(8,128)(2,1)S(1)}, u32[]{:S(2)}, u32[]{:S(2)}) %all-to-all-start.5) | async-done | bytes 655392 | tf_op jit(solution)/shard_map/all_to_all | solution.py:592
  150.4 0.7 copy-done.2
  151.2 1.3 shard_map.58
  152.4 3.4 %all-to-all-start.6 = ((bf16[8,64,256]{2,1,0:T(8,128)(2,1)}), bf16[8,64,256]{2,1,0:T(8,128)(2,1)S(1)}, u32[]{:S(2)}, u32[]{:S(2)}) async-start(bf16[8,64,256]{2,1,0:T(8,128)(2,1)} %shard_map.58), calls=%async_computation.6 | async-start | bytes 524288 | tf_op jit(solution)/shard_map/all_to_all | solution.py:623
  155.9 11.7 %all-to-all-done.6.came_ref = bf16[8,64,256]{2,1,0:T(8,128)(2,1)S(1)} async-done(((bf16[8,64,256]{2,1,0:T(8,128)(2,1)}), bf16[8,64,256]{2,1,0:T(8,128)(2,1)S(1)}, u32[]{:S(2)}, u32[]{:S(2)}) %all-to-all-start.6) | async-done | bytes 262176 | tf_op jit(solution)/shard_map/all_to_all | solution.py:623
  167.6 4.1 %shard_map.61 = f32[256,512]{1,0:T(8,128)} custom-call(s32[1]{0:T(128)} %bitcast.3.core_ref, bf16[8,64,256]{2,1,0:T(8,128)(2,1)S(1)} %all-to-all-done.6.came_ref, bf16[512,1024]{1,0:T(8,128)(2,1)} %get-tuple-element.43.keep_ref, f32[256,512]{1,0:T(8,128)} %shard_map.59.seen_ref, f32[256,512]{1,0:T(8,128)} %collective-permute-done.1.mate_ref, ...), custom_call_target="tpu_custom_call" | custom-call | flops 1000000000 | bytes 4000000 | tf_op jit(solution)/shard_map/pallas_call | solution.py:423
  171.6 5.8 %all-to-all-start.7 = ((f32[32,8,512]{2,1,0:T(8,128)}), f32[32,8,512]{2,1,0:T(8,128)S(1)}, u32[]{:S(2)}, u32[]{:S(2)}) async-start(f32[32,8,512]{2,1,0:T(8,128)} %bitcast.8), calls=%async_computation.7 | async-start | bytes 1048576 | tf_op jit(solution)/shard_map/all_to_all | solution.py:645
  177.4 1.3 shard_map.62
  178.8 10.2 %all-to-all-done.7 = f32[32,8,512]{2,1,0:T(8,128)S(1)} async-done(((f32[32,8,512]{2,1,0:T(8,128)}), f32[32,8,512]{2,1,0:T(8,128)S(1)}, u32[]{:S(2)}, u32[]{:S(2)}) %all-to-all-start.7) | async-done | bytes 524320 | tf_op jit(solution)/shard_map/all_to_all | solution.py:645
  189.0 0.8 copy.8
  (26 shorter events, 0.6 us)
Async XLA Ops:
  46.4 2.6 %collective-permute-start = (bf16[32,16,256]{2,1,0:T(8,128)(2,1)S(1)}, bf16[32,16,256]{2,1,0:T(8,128)(2,1)S(1)}, u32[]{:S(2)}, u32[]{:S(2)}) collective-permute-start(bf16[32,16,256]{2,1,0:T(8,128)(2,1)S(1)} %slice.4), channel_id=1, source_target_pairs={{0,8},{8,0},{1,9},{9,1},{2,10},{10,2},{3,11},{11,3},{4,12},{12,4},... | collective-permute-start | bytes 786440 | tf_op jit(solution)/shard_map/ppermute | solution.py:464
  49.0 11.3 %all-to-all-start.1 = ((f32[32,8,128]{2,1,0:T(8,128)}), f32[32,8,128]{2,1,0:T(8,128)S(1)}, u32[]{:S(2)}, u32[]{:S(2)}) async-start(f32[32,8,128]{2,1,0:T(8,128)} %get-tuple-element.31), calls=%async_computation.1 | async-start | bytes 262144 | tf_op jit(solution)/shard_map/all_to_all | solution.py:476
  61.0 15.2 %all-to-all-start.2 = ((f32[8,8,128]{2,1,0:T(8,128)}), f32[8,8,128]{2,1,0:T(8,128)S(1)}, u32[]{:S(2)}, u32[]{:S(2)}) async-start(f32[8,8,128]{2,1,0:T(8,128)} %broadcast_in_dim.2), calls=%async_computation.2 | async-start | bytes 65536 | tf_op jit(solution)/shard_map/all_to_all | solution.py:518
  69.2 0.7 copy-start.3
  69.9 6.3 %copy-start.4 = (f32[16,256]{1,0:T(8,128)S(1)}, f32[16,256]{1,0:T(8,128)}, u32[]{:S(2)}) copy-start(f32[16,256]{1,0:T(8,128)} %get-tuple-element.35.part_ref.sum_ref) | copy-start | bytes 49156
  79.0 48.7 %copy-start.7 = (bf16[256,512]{1,0:T(8,128)(2,1)S(1)}, bf16[256,512]{1,0:T(8,128)(2,1)}, u32[]{:S(2)}) copy-start(bf16[256,512]{1,0:T(8,128)(2,1)} %get-tuple-element.39.hi_ref) | copy-start | bytes 786436
  79.0 48.7 %copy-start.8 = (bf16[256,512]{1,0:T(8,128)(2,1)S(1)}, bf16[256,512]{1,0:T(8,128)(2,1)}, u32[]{:S(2)}) copy-start(bf16[256,512]{1,0:T(8,128)(2,1)} %get-tuple-element.40.lo_ref) | copy-start | bytes 786436
  79.0 30.1 %all-to-all-start.3 = ((bf16[32,96,256]{2,1,0:T(8,128)(2,1)}), bf16[32,96,256]{2,1,0:T(8,128)(2,1)}, u32[]{:S(2)}, u32[]{:S(2)}) async-start(bf16[32,96,256]{2,1,0:T(8,128)(2,1)} %shard_map.54), calls=%async_computation.3 | async-start | bytes 3145728 | tf_op jit(solution)/shard_map/all_to_all | solution.py:552
  109.1 18.6 %copy-start = (f32[512,1024]{1,0:T(8,128)S(1)}, f32[512,1024]{1,0:T(8,128)}, u32[]{:S(2)}) copy-start(f32[512,1024]{1,0:T(8,128)} %get-tuple-element.37.mass_hbm.mass_ref) | copy-start | bytes 6291460
  130.3 20.1 %all-to-all-start.5 = ((bf16[32,40,256]{2,1,0:T(8,128)(2,1)}), bf16[32,40,256]{2,1,0:T(8,128)(2,1)S(1)}, u32[]{:S(2)}, u32[]{:S(2)}) async-start(bf16[32,40,256]{2,1,0:T(8,128)(2,1)} %get-tuple-element.41), calls=%async_computation.5 | async-start | bytes 1310720 | tf_op jit(solution)/shard_map/all_to_all | solution.py:592
  138.7 28.9 %copy-start.5 = (f32[1,512]{1,0:T(1,128)S(1)}, f32[1,512]{1,0:T(1,128)}, u32[]{:S(2)}) copy-start(f32[1,512]{1,0:T(1,128)} %get-tuple-element.48.scale_ref) | copy-start | bytes 6148
  138.7 28.9 %copy-start.6 = (f32[1,512]{1,0:T(1,128)S(1)}, f32[1,512]{1,0:T(1,128)}, u32[]{:S(2)}) copy-start(f32[1,512]{1,0:T(1,128)} %get-tuple-element.49.inv_ref) | copy-start | bytes 6148
  138.7 17.2 %collective-permute-start.1 = (f32[256,512]{1,0:T(8,128)}, f32[256,512]{1,0:T(8,128)}, u32[]{:S(2)}, u32[]{:S(2)}) collective-permute-start(f32[256,512]{1,0:T(8,128)} %shard_map.59.seen_ref), channel_id=1, source_target_pairs={{0,8},{8,0},{1,9},{9,1},{2,10},{10,2},{3,11},{11,3},{4,12},{12,4},... | collective-permute-start | bytes 1572872 | tf_op jit(solution)/shard_map/ppermute | solution.py:565
  146.4 9.5 %collective-permute-start.2 = (f32[256,512]{1,0:T(8,128)}, f32[256,512]{1,0:T(8,128)S(1)}, u32[]{:S(2)}, u32[]{:S(2)}) collective-permute-start(f32[256,512]{1,0:T(8,128)} %get-tuple-element.46), channel_id=1, source_target_pairs={{0,8},{8,0},{1,9},{9,1},{2,10},{10,2},{3,11},{11,3},{4,12},{12,4},... | collective-permute-start | bytes 1572872 | tf_op jit(solution)/shard_map/ppermute | solution.py:609
  150.4 0.7 copy-start.2
  152.4 15.1 %all-to-all-start.6 = ((bf16[8,64,256]{2,1,0:T(8,128)(2,1)}), bf16[8,64,256]{2,1,0:T(8,128)(2,1)S(1)}, u32[]{:S(2)}, u32[]{:S(2)}) async-start(bf16[8,64,256]{2,1,0:T(8,128)(2,1)} %shard_map.58), calls=%async_computation.6 | async-start | bytes 524288 | tf_op jit(solution)/shard_map/all_to_all | solution.py:623
  155.9 11.7 %copy-start.9 = (f32[256,512]{1,0:T(8,128)}, f32[256,512]{1,0:T(8,128)S(1)}, u32[]{:S(2)}) copy-start(f32[256,512]{1,0:T(8,128)S(1)} %collective-permute-done.2.term_mate_ref) | copy-start | bytes 1572868
  167.6 9.9 %copy-start.1 = (bf16[160,256]{1,0:T(8,128)(2,1)S(1)}, bf16[160,256]{1,0:T(8,128)(2,1)}, u32[]{:S(2)}) copy-start(bf16[160,256]{1,0:T(8,128)(2,1)} %feat_ref.2) | copy-start | bytes 245764
  171.6 17.4 %all-to-all-start.7 = ((f32[32,8,512]{2,1,0:T(8,128)}), f32[32,8,512]{2,1,0:T(8,128)S(1)}, u32[]{:S(2)}, u32[]{:S(2)}) async-start(f32[32,8,512]{2,1,0:T(8,128)} %bitcast.8), calls=%async_computation.7 | async-start | bytes 1048576 | tf_op jit(solution)/shard_map/all_to_all | solution.py:645

commit v5 on v4

--- a/solution.py
+++ b/solution.py
@@ -105,11 +105,9 @@
     return jnp.concatenate([x8, jnp.zeros_like(x8)], axis=0).astype(BF16)
 
 
-def sweep(mass_ref, row_inv, keep_ref=None, copies=None):
+def sweep(mass_ref, row_inv, keep_ref=None):
     total = jnp.zeros((8, 1024), F32)
     for low in range(0, 512, 32):
-        if copies is not None and low % 64 == 0:
-            copies[low // 64].wait()
         x = mass_ref[low : low + 32, :]
         y = x if row_inv is None else x * row_inv
         x = x * (1.0 / jnp.sum(y, axis=1, keepdims=True))
@@ -135,7 +133,7 @@
         out_ref[p, 80:160, :] = unit_ref[80 * (p % 2) : 80 * (p % 2) + 80, :]
 
 
-def first_kernel(own_ref, mass_ref, out_ref):
+def fill(own_ref, mass_ref):
     for h in range(2):
         for j in range(4):
             cols = slice(512 * h + 128 * j, 512 * h + 128 * j + 128)
@@ -143,19 +141,18 @@
                 low = 32 * side + 16 * h
                 block = own_ref[8 * j : 8 * j + 8, low : low + 16, :].reshape(128, 256)
                 mass_ref[256 * side : 256 * side + 256, cols] = decode_exp(block).T
+
+
+def first_kernel(own_ref, out_ref, mass_ref):
+    fill(own_ref, mass_ref)
     part = rows8(sweep(mass_ref, None))
     out_ref[...] = jnp.broadcast_to(part[None], (32, 8, 128))
 
 
-def second_kernel(came_ref, sum_ref, mass_hbm, pack_ref, out_ref, mass_ref, sems):
-    copies = [
-        pltpu.make_async_copy(mass_hbm.at[pl.ds(64 * i, 64), :], mass_ref.at[pl.ds(64 * i, 64), :], sems.at[i])
-        for i in range(8)
-    ]
-    for copy in copies:
-        copy.start()
+def second_kernel(came_ref, sum_ref, own_ref, pack_ref, out_ref, mass_ref):
+    fill(own_ref, mass_ref)
     row_inv = lanes(1.0 / jnp.sum(came_ref[...], axis=0))
-    part = rows8(sweep(mass_ref, row_inv, copies=copies) * row_inv)
+    part = rows8(sweep(mass_ref, row_inv) * row_inv)
     part = root_code(part * WIDE)
     part = jnp.concatenate([part[:, :64], part[:, 64:]], axis=0)
     row = jnp.concatenate([sum_code(sum_ref[...])[:, :192], part], axis=1).astype(BF16)
@@ -165,15 +162,14 @@
 def home_kernel(place_ref, came_ref, out_ref):
     core = place_ref[2]
     pick = lax.broadcasted_iota(jnp.int32, (16, 256), 0) == place_ref[0]
-    row_sum = jnp.zeros((16, 256), F32)
+    row_sum = jnp.zeros((16, 128), F32)
     parts = [[], []]
+    exp_sum = jnp.zeros((16, 256), F32)
     for p in range(32):
-        row_sum = row_sum + root_decode(came_ref[p, 80:96, :])
+        row_sum = row_sum + root_decode(came_ref[p, 80:96, 128:])
         exp_part = sum_decode(came_ref[p, 80:96, :])
+        exp_sum = exp_sum + jnp.where(core == p % 2, exp_part, 0.0)
         parts[p % 2].append(jnp.sum(jnp.where(pick, exp_part, 0.0), axis=0, keepdims=True))
-    exp_sum = jnp.zeros((16, 256), F32)
-    for p in range(16):
-        exp_sum = exp_sum + sum_decode(came_ref[2 * p + core, 80:96, :])
     code = []
     home_sum = []
     for half in range(2):
@@ -191,7 +187,7 @@
             code.append(fine_code(home * scale[low : low + 16]))
     code = jnp.concatenate(code, axis=0)
     home_sum = jnp.concatenate(home_sum + [jnp.ones((1, 96), F32)], axis=1)
-    row_sum = jnp.concatenate([row_sum[:8, 192:], row_sum[8:, 192:]], axis=1)
+    row_sum = jnp.concatenate([row_sum[:8, 64:], row_sum[8:, 64:]], axis=1)
     lane = lax.broadcasted_iota(jnp.int32, (16, 256), 1)
     exp_sum = jnp.where(lane < 160, exp_sum, 1.0)
     tail = [
@@ -282,7 +278,7 @@
 
 
 def final_kernel(
-    core_ref, came_ref, keep_ref, seen_ref, mate_ref, term_ref, term_mate_ref, weight_ref, scale_ref, inv_ref, out_ref
+    core_ref, came_ref, keep_ref, seen_ref, mate_ref, term_ref, weight_ref, scale_ref, inv_ref, out_ref
 ):
     first = core_ref[0] == 0
     rows = came_ref[0, 48:64, :].astype(F32)
@@ -298,7 +294,7 @@
         keep = keep_ref[cols, :]
         x = dot(low_hi, keep[:, :512], NT) + dot(low_lo, keep[:, :512], NT)
         x = x + (dot(high_hi, keep[:, 512:], NT) + dot(high_lo, keep[:, 512:], NT))
-        x = term_ref[:, cols] + term_mate_ref[:, cols] - x * scale_ref[:, cols]
+        x = term_ref[:, cols] - x * scale_ref[:, cols]
         w = weight_ref[:, cols].astype(F32)
         dots = jnp.sum(w * x, axis=0, keepdims=True) * inv_ref[:, cols]
         out_ref[:, cols] = x - w * dots
@@ -462,14 +458,16 @@
     got = lax.all_to_all(send, BATCH, 0, 0, tiled=True)
 
     mate = lax.ppermute(got[:, 64:80], "core", SWAP)
-    mass, pack = call(
+    teacher_spec = whole(32, 64, 256)
+    pack = call(
         first_kernel,
-        (shape((512, 1024)), shape((32, 8, 128))),
+        shape((32, 8, 128)),
         10**7,
-        3 * 10**6,
+        10**6,
         got,
-        specs=[whole(32, 64, 256)],
-        out_specs=(VMEM, VMEM),
+        specs=[teacher_spec],
+        out_specs=VMEM,
+        scratch_shapes=[pltpu.VMEM((512, 1024), F32)],
         grid=(1,),
     )
     got, mate, pack = lax.optimization_barrier((got, mate, pack))
@@ -541,11 +539,11 @@
         2 * 10**6,
         came_one,
         exp_part,
-        hbm(mass),
+        got,
         hbm(student_pack),
-        specs=[VMEM, VMEM, pl.BlockSpec(memory_space=pltpu.HBM), pl.BlockSpec(memory_space=pltpu.HBM)],
+        specs=[VMEM, VMEM, teacher_spec, pl.BlockSpec(memory_space=pltpu.HBM)],
         out_specs=pl.BlockSpec((32, 16, 256), lambda i: (0, 5, 0)),
-        scratch_shapes=[pltpu.VMEM((512, 1024), F32), pltpu.SemaphoreType.DMA((8,))],
+        scratch_shapes=[pltpu.VMEM((512, 1024), F32)],
         grid=(1,),
         input_output_aliases={3: 0},
     )
@@ -563,7 +561,9 @@
         grid=(1,),
     )
     seen_mate = lax.ppermute(seen, "core", SWAP)
-
+    mass = call(fill, shape((512, 1024)), 10**7, 3 * 10**6, got, specs=[teacher_spec], out_specs=VMEM, grid=(1,))
+
+    came, mass = lax.optimization_barrier((came, mass))
     pack = call(
         home_kernel,
         shape((8, 48, 256), BF16),
@@ -606,7 +606,7 @@
         scratch_shapes=[pltpu.VMEM((256, 1024), F32)],
         grid=(2,),
     )
-    term_mate = lax.ppermute(other, "core", SWAP)
+    term = term + lax.ppermute(other, "core", SWAP)
     home_slice = call(slice_kernel, shape((24, 256)), 10**6, 10**5, place, came_two, out_specs=VMEM)
 
     pack = call(
@@ -633,11 +633,10 @@
         hbm(seen),
         hbm(seen_mate),
         hbm(term),
-        hbm(term_mate),
         hbm(my_weights),
         my_scale,
         my_inv,
-        specs=[SMEM, VMEM, whole(512, 1024)] + [whole(256, 512)] * 5 + [VMEM, VMEM],
+        specs=[SMEM, VMEM, whole(512, 1024)] + [whole(256, 512)] * 4 + [VMEM, VMEM],
         out_specs=whole(256, 512),
         grid=(1,),
     )

time: 191 us -> 189 us (0.990)
  waiting for transfers between devices: 47.6 us -> 43.6 us
  other arithmetic: 0.11 us -> 2.2 us
    add x0 -> x1, other arithmetic: none -> 2.08 us  [shards(): term = term + lax.ppermute(other, 'core', SWAP)]
    all_to_all x1, waiting for transfers between devices: 11.7 us -> 9.6 us  [shards(): came = lax.all_to_all(pack, 'proto', 0, 0, tiled=True)]
    all_to_all x3, waiting for transfers between devices: 25.5 us -> 23.5 us  [shards(): came = lax.all_to_all(pack, BATCH, 0, 0, tiled=True)]
    pallas_call x13 -> x14, Pallas kernels: 44.2 us -> 44.6 us  [call(): pl.pallas_call(kernel, out_shape=shapes, in_specs=specs, cost_estimate=pl...]
  transfers between devices with their start and end apart: 9 -> 9, of which waited for: 6 -> 6; matrix products, arithmetic and copies ran while one was open for 0% -> 1% of each run, Pallas kernels for 14% -> 15%
where the time goes in v5:
time: 189 us; the launch traced here: 188 us
  blocking collectives  57 us (30%)
  Pallas kernels  44.6 us (24%)
  waiting for transfers between devices  43.6 us (23%)
  starting transfers between devices  36.9 us (20%)
  local copies, waits for them, and re-layouts  2.92 us (2%)
  other arithmetic  2.2 us (1%)
    pallas_call x14, Pallas kernels, call(): pl.pallas_call(kernel, out_shape=shapes, in_specs=specs, cost_estimate=pl...  44.6 us
    all_to_all x1, blocking collectives, shards(): got = lax.all_to_all(send, BATCH, 0, 0, tiled=True)  42.6 us
    all_to_all x3, waiting for transfers between devices, shards(): came = lax.all_to_all(pack, BATCH, 0, 0, tiled=True)  23.5 us
    all_to_all x3, starting transfers between devices, shards(): came = lax.all_to_all(pack, BATCH, 0, 0, tiled=True)  18.6 us
    all_to_all x1, blocking collectives, shards(): came_two = lax.all_to_all(pack, 'proto', 0, 0, tiled=True)  14.4 us
    all_to_all x1, waiting for transfers between devices, shards(): grad = lax.all_to_all(grad.reshape(32, 8, 512), BATCH, 0, 0, tiled=True)  10.2 us
    all_to_all x1, waiting for transfers between devices, shards(): came = lax.all_to_all(pack, 'proto', 0, 0, tiled=True)  9.6 us
    all_to_all x1, starting transfers between devices, shards(): lax.all_to_all(jnp.broadcast_to(row_sum[None], (8, 8, 128)), 'proto', 0,...  8.19 us
  transfers between devices with their start and end apart: 9, of which 6 were waited for; matrix products, arithmetic and copies ran while one was open for 1% of the time, Pallas kernels for 15%

profile of v5, /device:TPU:1, one launch (start us, length us, event | category | flops | bytes accessed | tf_op | source)
XLA Modules:
  0.0 188.0 jit_solution(500730163761111986)
XLA Ops:
  0.6 3.2 %shard_map.50 = bf16[32,160,256]{2,1,0:T(8,128)(2,1)} custom-call(f32[32,16384]{1,0:T(8,128)} %teacher_ref.1, bf16[8,16384]{1,0:T(8,128)(2,1)} %proto_ref.1, bf16[160,256]{1,0:T(8,128)(2,1)} %feat_ref.2), custom_call_target="tpu_custom_call" | custom-call | flops 10000000 | bytes 5000000 | tf_op jit(solution)/shard_map/pallas_call | solution.py:419
  3.8 42.6 %all_to_all.40.own_ref.unit_ref = bf16[32,160,256]{2,1,0:T(8,128)(2,1)S(1)} all-to-all(bf16[32,160,256]{2,1,0:T(8,128)(2,1)} %shard_map.50), channel_id=1, replica_groups=mesh['y'=4,'x'=4,'core'=2,'proto'=8] {'y','x','core'}, dimensions={0} | all-to-all | bytes 5242880 | tf_op jit(solution)/shard_map/all_to_all | solution.py:458
  47.0 1.6 shard_map.51
  48.6 3.7 %all-to-all-start.1 = ((f32[32,8,128]{2,1,0:T(8,128)}), f32[32,8,128]{2,1,0:T(8,128)S(1)}, u32[]{:S(2)}, u32[]{:S(2)}) async-start(f32[32,8,128]{2,1,0:T(8,128)} %shard_map.51), calls=%async_computation.1 | async-start | bytes 262144 | tf_op jit(solution)/shard_map/all_to_all | solution.py:474
  52.3 6.6 %shard_map.52 = (bf16[2560,1024]{1,0:T(8,128)(2,1)}, f32[16,256]{1,0:T(8,128)}, bf16[256,1024]{1,0:T(8,128)(2,1)}, bf16[256,512]{1,0:T(8,128)(2,1)}, f32[1,512]{...) custom-call(s32[1]{0:T(128)} %bitcast.3.core_ref, ...), custom_call_target="tpu_custom_call" | custom-call | flops 2000000000 | bytes 9000000 | tf_op jit(solution)/shard_map/pallas_call | solution.py:419
  58.8 1.1 all-to-all-done.1
  59.9 0.6 broadcast_in_dim.2
  60.6 8.2 %all-to-all-start.2 = ((f32[8,8,128]{2,1,0:T(8,128)}), f32[8,8,128]{2,1,0:T(8,128)S(1)}, u32[]{:S(2)}, u32[]{:S(2)}) async-start(f32[8,8,128]{2,1,0:T(8,128)} %broadcast_in_dim.2), calls=%async_computation.2 | async-start | bytes 65536 | tf_op jit(solution)/shard_map/all_to_all | solution.py:516
  68.8 0.7 copy-done.3
  69.5 6.0 %shard_map.53.pack_ref = bf16[32,96,256]{2,1,0:T(8,128)(2,1)} custom-call(bf16[2560,1024]{1,0:T(8,128)(2,1)} %get-tuple-element.32.grad_ref, bf16[256,1024]{1,0:T(8,128)(2,1)} %get-tuple-element.33.weight_ref, f32[16,256]{1,0:T(8,128)S(1)} %copy-done.3), custom_call_target="tpu_custom_call" | custom-call | flops 2000000000 | bytes 7000000 | tf_op jit(solution)/shard_map/pallas_call | solution.py:419
  75.7 1.9 shard_map.54
  77.6 7.7 %all-to-all-start.3 = ((bf16[32,96,256]{2,1,0:T(8,128)(2,1)}), bf16[32,96,256]{2,1,0:T(8,128)(2,1)}, u32[]{:S(2)}, u32[]{:S(2)}) async-start(bf16[32,96,256]{2,1,0:T(8,128)(2,1)} %shard_map.54), calls=%async_computation.3 | async-start | bytes 3145728 | tf_op jit(solution)/shard_map/all_to_all | solution.py:550
  85.4 2.0 %shard_map.55.mass_ref = f32[512,1024]{1,0:T(8,128)} custom-call(bf16[32,160,256]{2,1,0:T(8,128)(2,1)S(1)} %all_to_all.40.own_ref.unit_ref), custom_call_target="tpu_custom_call" | custom-call | flops 10000000 | bytes 3000000 | tf_op jit(solution)/shard_map/pallas_call | solution.py:419
  87.4 20.1 %all-to-all-done.3.came_ref = bf16[32,96,256]{2,1,0:T(8,128)(2,1)} async-done(((bf16[32,96,256]{2,1,0:T(8,128)(2,1)}), bf16[32,96,256]{2,1,0:T(8,128)(2,1)}, u32[]{:S(2)}, u32[]{:S(2)}) %all-to-all-start.3) | async-done | bytes 1572896 | tf_op jit(solution)/shard_map/all_to_all | solution.py:550
  107.6 4.1 %shard_map.56 = bf16[8,48,256]{2,1,0:T(8,128)(2,1)} custom-call(s32[3]{0:T(128)S(1)} %pad_add_fusion.place_ref, bf16[32,96,256]{2,1,0:T(8,128)(2,1)} %all-to-all-done.3.came_ref), custom_call_target="tpu_custom_call" | custom-call | flops 10000000 | bytes 2000000 | tf_op jit(solution)/shard_map/pallas_call | solution.py:419
  111.6 14.4 %all_to_all.41.came_ref = bf16[8,48,256]{2,1,0:T(8,128)(2,1)S(1)} all-to-all(bf16[8,48,256]{2,1,0:T(8,128)(2,1)} %shard_map.56), channel_id=1, replica_groups=mesh['y'=4,'x'=4,'core'=2,'proto'=8] {'proto'}, dimensions={0} | all-to-all | bytes 393216 | tf_op jit(solution)/shard_map/all_to_all | solution.py:578
  126.0 2.7 %shard_map.57 = (bf16[512,1024]{1,0:T(8,128)(2,1)}, bf16[32,40,256]{2,1,0:T(8,128)(2,1)}) custom-call(bf16[8,48,256]{2,1,0:T(8,128)(2,1)S(1)} %all_to_all.41.came_ref, f32[8,8,128]{2,1,0:T(8,128)S(1)} %all-to-all-done.2.came_ref.came_one_ref, f32[512,1024]{1,0:T(8,128)S(1)} %copy-done, bf16[256,512]{1,0:T(8,128)(2,1)S(1)} %copy-done.7, ...), custom_call_target="tpu_custom_call" | custom-call | flops 1000000000 | bytes 4000000 | tf_op jit(solution)/shard_map/pallas_call | solution.py:419
  128.8 7.2 %all-to-all-start.5 = ((bf16[32,40,256]{2,1,0:T(8,128)(2,1)}), bf16[32,40,256]{2,1,0:T(8,128)(2,1)S(1)}, u32[]{:S(2)}, u32[]{:S(2)}) async-start(bf16[32,40,256]{2,1,0:T(8,128)(2,1)} %get-tuple-element.42), calls=%async_computation.5 | async-start | bytes 1310720 | tf_op jit(solution)/shard_map/all_to_all | solution.py:592
  135.9 7.4 %shard_map.61 = (f32[256,512]{1,0:T(8,128)}, f32[256,512]{1,0:T(8,128)}) custom-call(s32[1]{0:T(128)} %bitcast.3.core_ref, bf16[32,160,256]{2,1,0:T(8,128)(2,1)S(1)} %all_to_all.40.own_ref.unit_ref, bf16[2560,1024]{1,0:T(8,128)(2,1)} %get-tuple-element.32.grad_ref, bf16[8,48,256]{2,1,0:T(8,128)(2,1)S(1)} %all_to_all.41.came_ref), custom_call_target="tpu_custom_call" | custom-call | flops 3000000000 | bytes 7000000 | tf_op jit(solution)/shard_map/pallas_call | solution.py:419
  143.7 1.2 shard_map.60.seen_ref
  145.0 1.5 shard_map.58.slice_ref
  146.5 2.4 %all-to-all-done.5.came_ref = bf16[32,40,256]{2,1,0:T(8,128)(2,1)S(1)} async-done(((bf16[32,40,256]{2,1,0:T(8,128)(2,1)}), bf16[32,40,256]{2,1,0:T(8,128)(2,1)S(1)}, u32[]{:S(2)}, u32[]{:S(2)}) %all-to-all-start.5) | async-done | bytes 655392 | tf_op jit(solution)/shard_map/all_to_all | solution.py:592
  148.8 0.7 copy-done.2
  149.6 1.3 shard_map.59
  150.9 3.4 %all-to-all-start.6 = ((bf16[8,64,256]{2,1,0:T(8,128)(2,1)}), bf16[8,64,256]{2,1,0:T(8,128)(2,1)S(1)}, u32[]{:S(2)}, u32[]{:S(2)}) async-start(bf16[8,64,256]{2,1,0:T(8,128)(2,1)} %shard_map.59), calls=%async_computation.6 | async-start | bytes 524288 | tf_op jit(solution)/shard_map/all_to_all | solution.py:623
  154.3 2.1 %add.15.term_ref = f32[256,512]{1,0:T(8,128)} add(f32[256,512]{1,0:T(8,128)} %get-tuple-element.45, f32[256,512]{1,0:T(8,128)} %collective-permute-done.2) | non-fusion elementwise | flops 131072 | bytes 1572864 | tf_op jit(solution)/shard_map/add | solution.py:609
  156.4 9.6 %all-to-all-done.6.came_ref = bf16[8,64,256]{2,1,0:T(8,128)(2,1)S(1)} async-done(((bf16[8,64,256]{2,1,0:T(8,128)(2,1)}), bf16[8,64,256]{2,1,0:T(8,128)(2,1)S(1)}, u32[]{:S(2)}, u32[]{:S(2)}) %all-to-all-start.6) | async-done | bytes 262176 | tf_op jit(solution)/shard_map/all_to_all | solution.py:623
  166.0 3.9 %shard_map.62 = f32[256,512]{1,0:T(8,128)} custom-call(s32[1]{0:T(128)} %bitcast.3.core_ref, bf16[8,64,256]{2,1,0:T(8,128)(2,1)S(1)} %all-to-all-done.6.came_ref, bf16[512,1024]{1,0:T(8,128)(2,1)} %get-tuple-element.44.keep_ref, f32[256,512]{1,0:T(8,128)} %shard_map.60.seen_ref, f32[256,512]{1,0:T(8,128)} %copy-done.9, f32[256,512]{1,0:T(8,128)} %add.15.term_ref, ...), custom_call_target="tpu_custom_call" | custom-call | flops 1000000000 | bytes 4000000 | tf_op jit(solution)/shard_map/pallas_call | solution.py:419
  169.9 5.7 %all-to-all-start.7 = ((f32[32,8,512]{2,1,0:T(8,128)}), f32[32,8,512]{2,1,0:T(8,128)S(1)}, u32[]{:S(2)}, u32[]{:S(2)}) async-start(f32[32,8,512]{2,1,0:T(8,128)} %bitcast.9), calls=%async_computation.7 | async-start | bytes 1048576 | tf_op jit(solution)/shard_map/all_to_all | solution.py:644
  175.7 1.3 shard_map.63
  177.0 10.2 %all-to-all-done.7 = f32[32,8,512]{2,1,0:T(8,128)S(1)} async-done(((f32[32,8,512]{2,1,0:T(8,128)}), f32[32,8,512]{2,1,0:T(8,128)S(1)}, u32[]{:S(2)}, u32[]{:S(2)}) %all-to-all-start.7) | async-done | bytes 524320 | tf_op jit(solution)/shard_map/all_to_all | solution.py:644
  187.2 0.8 copy.8
  (28 shorter events, 1.5 us)
Async XLA Ops:
  46.4 2.2 %collective-permute-start = (bf16[32,16,256]{2,1,0:T(8,128)(2,1)S(1)}, bf16[32,16,256]{2,1,0:T(8,128)(2,1)S(1)}, u32[]{:S(2)}, u32[]{:S(2)}) collective-permute-start(bf16[32,16,256]{2,1,0:T(8,128)(2,1)S(1)} %slice.4), channel_id=1, source_target_pairs={{0,8},{8,0},{1,9},{9,1},{2,10},{10,2},{3,11},{11,3},{4,12},{12,4},... | collective-permute-start | bytes 786440 | tf_op jit(solution)/shard_map/ppermute | solution.py:460
  48.6 11.3 %all-to-all-start.1 = ((f32[32,8,128]{2,1,0:T(8,128)}), f32[32,8,128]{2,1,0:T(8,128)S(1)}, u32[]{:S(2)}, u32[]{:S(2)}) async-start(f32[32,8,128]{2,1,0:T(8,128)} %shard_map.51), calls=%async_computation.1 | async-start | bytes 262144 | tf_op jit(solution)/shard_map/all_to_all | solution.py:474
  60.6 15.2 %all-to-all-start.2 = ((f32[8,8,128]{2,1,0:T(8,128)}), f32[8,8,128]{2,1,0:T(8,128)S(1)}, u32[]{:S(2)}, u32[]{:S(2)}) async-start(f32[8,8,128]{2,1,0:T(8,128)} %broadcast_in_dim.2), calls=%async_computation.2 | async-start | bytes 65536 | tf_op jit(solution)/shard_map/all_to_all | solution.py:516
  68.7 0.7 copy-start.3
  69.5 6.3 %copy-start.4 = (f32[16,256]{1,0:T(8,128)S(1)}, f32[16,256]{1,0:T(8,128)}, u32[]{:S(2)}) copy-start(f32[16,256]{1,0:T(8,128)} %get-tuple-element.34.part_ref.sum_ref) | copy-start | bytes 49156
  77.6 30.0 %all-to-all-start.3 = ((bf16[32,96,256]{2,1,0:T(8,128)(2,1)}), bf16[32,96,256]{2,1,0:T(8,128)(2,1)}, u32[]{:S(2)}, u32[]{:S(2)}) async-start(bf16[32,96,256]{2,1,0:T(8,128)(2,1)} %shard_map.54), calls=%async_computation.3 | async-start | bytes 3145728 | tf_op jit(solution)/shard_map/all_to_all | solution.py:550
  85.4 40.6 %copy-start.7 = (bf16[256,512]{1,0:T(8,128)(2,1)S(1)}, bf16[256,512]{1,0:T(8,128)(2,1)}, u32[]{:S(2)}) copy-start(bf16[256,512]{1,0:T(8,128)(2,1)} %get-tuple-element.40.hi_ref) | copy-start | bytes 786436
  85.4 40.6 %copy-start.8 = (bf16[256,512]{1,0:T(8,128)(2,1)S(1)}, bf16[256,512]{1,0:T(8,128)(2,1)}, u32[]{:S(2)}) copy-start(bf16[256,512]{1,0:T(8,128)(2,1)} %get-tuple-element.41.lo_ref) | copy-start | bytes 786436
  107.6 18.4 %copy-start = (f32[512,1024]{1,0:T(8,128)S(1)}, f32[512,1024]{1,0:T(8,128)}, u32[]{:S(2)}) copy-start(f32[512,1024]{1,0:T(8,128)} %shard_map.55.mass_ref) | copy-start | bytes 6291460
  128.8 20.1 %all-to-all-start.5 = ((bf16[32,40,256]{2,1,0:T(8,128)(2,1)}), bf16[32,40,256]{2,1,0:T(8,128)(2,1)S(1)}, u32[]{:S(2)}, u32[]{:S(2)}) async-start(bf16[32,40,256]{2,1,0:T(8,128)(2,1)} %get-tuple-element.42), calls=%async_computation.5 | async-start | bytes 1310720 | tf_op jit(solution)/shard_map/all_to_all | solution.py:592
  143.3 11.0 %collective-permute-start.2 = (f32[256,512]{1,0:T(8,128)}, f32[256,512]{1,0:T(8,128)}, u32[]{:S(2)}, u32[]{:S(2)}) collective-permute-start(f32[256,512]{1,0:T(8,128)} %get-tuple-element.46), channel_id=1, source_target_pairs={{0,8},{8,0},{1,9},{9,1},{2,10},{10,2},{3,11},{11,3},{4,12},{12,4},... | collective-permute-start | bytes 1572872 | tf_op jit(solution)/shard_map/ppermute | solution.py:609
  144.9 21.1 %copy-start.5 = (f32[1,512]{1,0:T(1,128)S(1)}, f32[1,512]{1,0:T(1,128)}, u32[]{:S(2)}) copy-start(f32[1,512]{1,0:T(1,128)} %get-tuple-element.48.scale_ref) | copy-start | bytes 6148
  144.9 21.1 %copy-start.6 = (f32[1,512]{1,0:T(1,128)S(1)}, f32[1,512]{1,0:T(1,128)}, u32[]{:S(2)}) copy-start(f32[1,512]{1,0:T(1,128)} %get-tuple-element.49.inv_ref) | copy-start | bytes 6148
  144.9 11.5 %collective-permute-start.1 = (f32[256,512]{1,0:T(8,128)}, f32[256,512]{1,0:T(8,128)S(1)}, u32[]{:S(2)}, u32[]{:S(2)}) collective-permute-start(f32[256,512]{1,0:T(8,128)} %shard_map.60.seen_ref), channel_id=1, source_target_pairs={{0,8},{8,0},{1,9},{9,1},{2,10},{10,2},{3,11},{11,3},{4,12},{12,4},... | collective-permute-start | bytes 1572872 | tf_op jit(solution)/shard_map/ppermute | solution.py:563
  148.8 0.7 copy-start.2
  150.9 15.1 %all-to-all-start.6 = ((bf16[8,64,256]{2,1,0:T(8,128)(2,1)}), bf16[8,64,256]{2,1,0:T(8,128)(2,1)S(1)}, u32[]{:S(2)}, u32[]{:S(2)}) async-start(bf16[8,64,256]{2,1,0:T(8,128)(2,1)} %shard_map.59), calls=%async_computation.6 | async-start | bytes 524288 | tf_op jit(solution)/shard_map/all_to_all | solution.py:623
  156.4 9.6 %copy-start.9 = (f32[256,512]{1,0:T(8,128)}, f32[256,512]{1,0:T(8,128)S(1)}, u32[]{:S(2)}) copy-start(f32[256,512]{1,0:T(8,128)S(1)} %collective-permute-done.1.mate_ref) | copy-start | bytes 1572868
  166.0 9.7 %copy-start.1 = (bf16[160,256]{1,0:T(8,128)(2,1)S(1)}, bf16[160,256]{1,0:T(8,128)(2,1)}, u32[]{:S(2)}) copy-start(bf16[160,256]{1,0:T(8,128)(2,1)} %feat_ref.2) | copy-start | bytes 245764
  169.9 17.3 %all-to-all-start.7 = ((f32[32,8,512]{2,1,0:T(8,128)}), f32[32,8,512]{2,1,0:T(8,128)S(1)}, u32[]{:S(2)}, u32[]{:S(2)}) async-start(f32[32,8,512]{2,1,0:T(8,128)} %bitcast.9), calls=%async_computation.7 | async-start | bytes 1048576 | tf_op jit(solution)/shard_map/all_to_all | solution.py:644

commit v6 on v5

--- a/solution.py
+++ b/solution.py
@@ -159,32 +159,46 @@
     out_ref[...] = jnp.broadcast_to(row[None], (32, 16, 256))
 
 
-def home_kernel(place_ref, came_ref, out_ref):
+def home_kernel(place_ref, came_hbm, out_ref, sum_ref, part_ref, sems):
+    copies = [pltpu.make_async_copy(came_hbm.at[:, pl.ds(80, 16), :], sum_ref, sems.at[0])]
+    for i in range(4):
+        some = pl.ds(8 * i, 8)
+        copies.append(
+            pltpu.make_async_copy(came_hbm.at[some, pl.ds(0, 80), :], part_ref.at[some], sems.at[i + 1])
+        )
+    for copy in copies:
+        copy.start()
+    copies[0].wait()
     core = place_ref[2]
     pick = lax.broadcasted_iota(jnp.int32, (16, 256), 0) == place_ref[0]
     row_sum = jnp.zeros((16, 128), F32)
     parts = [[], []]
     exp_sum = jnp.zeros((16, 256), F32)
     for p in range(32):
-        row_sum = row_sum + root_decode(came_ref[p, 80:96, 128:])
-        exp_part = sum_decode(came_ref[p, 80:96, :])
+        row_sum = row_sum + root_decode(sum_ref[p, :, 128:])
+        exp_part = sum_decode(sum_ref[p])
         exp_sum = exp_sum + jnp.where(core == p % 2, exp_part, 0.0)
         parts[p % 2].append(jnp.sum(jnp.where(pick, exp_part, 0.0), axis=0, keepdims=True))
-    code = []
     home_sum = []
+    factors = []
     for half in range(2):
         x = jnp.concatenate(parts[half], axis=0)
         x = jnp.where(core == 0, x[:, :80], x[:, 80:160])
         home_sum.append(jnp.sum(x, axis=0, keepdims=True))
         x = jnp.concatenate([x, jnp.ones((16, 176), F32)], axis=1)
-        x = columns(x * (1.0 / ROOT))[:80]
-        scale = 1.0 / jnp.sum(x, axis=1, keepdims=True)
-        for low in range(0, 80, 16):
-            home = jnp.zeros((16, 256), F32)
-            for p in range(16):
-                part = root_decode(came_ref[2 * p + half, low : low + 16, :])
-                home = home + part * x[low : low + 16, p : p + 1]
-            code.append(fine_code(home * scale[low : low + 16]))
+        factors.append(columns(x * (1.0 / ROOT))[:80])
+    home = [jnp.zeros((16, 256), F32)] * 10
+    for i in range(4):
+        copies[i + 1].wait()
+        for p in range(8 * i, 8 * i + 8):
+            half = p % 2
+            for j in range(5):
+                rows = slice(16 * j, 16 * j + 16)
+                part = root_decode(part_ref[p, rows, :]) * factors[half][rows, p // 2 : p // 2 + 1]
+                home[5 * half + j] = home[5 * half + j] + part
+    home = jnp.concatenate(home, axis=0)
+    scale = [1.0 / jnp.sum(x, axis=1, keepdims=True) for x in factors]
+    code = [fine_code(home * jnp.concatenate(scale, axis=0))]
     code = jnp.concatenate(code, axis=0)
     home_sum = jnp.concatenate(home_sum + [jnp.ones((1, 96), F32)], axis=1)
     row_sum = jnp.concatenate([row_sum[:8, 64:], row_sum[8:, 64:]], axis=1)
@@ -571,8 +585,13 @@
         2 * 10**6,
         place,
         hbm(came),
-        specs=[SMEM, whole(32, 96, 256)],
+        specs=[SMEM, pl.BlockSpec(memory_space=pltpu.HBM)],
         out_specs=whole(8, 48, 256),
+        scratch_shapes=[
+            pltpu.VMEM((32, 16, 256), BF16),
+            pltpu.VMEM((32, 80, 256), BF16),
+            pltpu.SemaphoreType.DMA((5,)),
+        ],
         grid=(1,),
     )
     came_two = lax.all_to_all(pack, "proto", 0, 0, tiled=True)

time: 189 us -> 189 us (level)
  no operation moved by 1% of the time
where the time goes in v6:
time: 189 us; the launch traced here: 188 us
  blocking collectives  57 us (30%)
  Pallas kernels  44.2 us (23%)
  waiting for transfers between devices  43.6 us (23%)
  starting transfers between devices  36.9 us (20%)
  local copies, waits for them, and re-layouts  2.92 us (2%)
  other arithmetic  2.2 us (1%)
    pallas_call x14, Pallas kernels, call(): pl.pallas_call(kernel, out_shape=shapes, in_specs=specs, cost_estimate=pl...  44.2 us
    all_to_all x1, blocking collectives, shards(): got = lax.all_to_all(send, BATCH, 0, 0, tiled=True)  42.6 us
    all_to_all x3, waiting for transfers between devices, shards(): came = lax.all_to_all(pack, BATCH, 0, 0, tiled=True)  23.5 us
    all_to_all x3, starting transfers between devices, shards(): came = lax.all_to_all(pack, BATCH, 0, 0, tiled=True)  18.6 us
    all_to_all x1, blocking collectives, shards(): came_two = lax.all_to_all(pack, 'proto', 0, 0, tiled=True)  14.4 us
    all_to_all x1, waiting for transfers between devices, shards(): grad = lax.all_to_all(grad.reshape(32, 8, 512), BATCH, 0, 0, tiled=True)  10.2 us
    all_to_all x1, waiting for transfers between devices, shards(): came = lax.all_to_all(pack, 'proto', 0, 0, tiled=True)  9.6 us
    all_to_all x1, starting transfers between devices, shards(): lax.all_to_all(jnp.broadcast_to(row_sum[None], (8, 8, 128)), 'proto', 0,...  8.19 us
  transfers between devices with their start and end apart: 9, of which 6 were waited for; matrix products, arithmetic and copies ran while one was open for 1% of the time, Pallas kernels for 15%

profile of v6, /device:TPU:1, one launch (start us, length us, event | category | flops | bytes accessed | tf_op | source)
XLA Modules:
  0.0 187.7 jit_solution(7406505248538322649)
XLA Ops:
  0.6 3.2 %shard_map.50 = bf16[32,160,256]{2,1,0:T(8,128)(2,1)} custom-call(f32[32,16384]{1,0:T(8,128)} %teacher_ref.1, bf16[8,16384]{1,0:T(8,128)(2,1)} %proto_ref.1, bf16[160,256]{1,0:T(8,128)(2,1)} %feat_ref.2), custom_call_target="tpu_custom_call" | custom-call | flops 10000000 | bytes 5000000 | tf_op jit(solution)/shard_map/pallas_call | solution.py:433
  3.8 42.6 %all_to_all.40.own_ref.unit_ref = bf16[32,160,256]{2,1,0:T(8,128)(2,1)S(1)} all-to-all(bf16[32,160,256]{2,1,0:T(8,128)(2,1)} %shard_map.50), channel_id=1, replica_groups=mesh['y'=4,'x'=4,'core'=2,'proto'=8] {'y','x','core'}, dimensions={0} | all-to-all | bytes 5242880 | tf_op jit(solution)/shard_map/all_to_all | solution.py:472
  47.0 1.6 shard_map.51
  48.6 3.7 %all-to-all-start.1 = ((f32[32,8,128]{2,1,0:T(8,128)}), f32[32,8,128]{2,1,0:T(8,128)S(1)}, u32[]{:S(2)}, u32[]{:S(2)}) async-start(f32[32,8,128]{2,1,0:T(8,128)} %shard_map.51), calls=%async_computation.1 | async-start | bytes 262144 | tf_op jit(solution)/shard_map/all_to_all | solution.py:488
  52.3 6.6 %shard_map.52 = (bf16[2560,1024]{1,0:T(8,128)(2,1)}, f32[16,256]{1,0:T(8,128)}, bf16[256,1024]{1,0:T(8,128)(2,1)}, bf16[256,512]{1,0:T(8,128)(2,1)}, f32[1,512]{...) custom-call(s32[1]{0:T(128)} %bitcast.3.core_ref, ...), custom_call_target="tpu_custom_call" | custom-call | flops 2000000000 | bytes 9000000 | tf_op jit(solution)/shard_map/pallas_call | solution.py:433
  58.8 1.1 all-to-all-done.1
  59.9 0.6 broadcast_in_dim.2
  60.6 8.2 %all-to-all-start.2 = ((f32[8,8,128]{2,1,0:T(8,128)}), f32[8,8,128]{2,1,0:T(8,128)S(1)}, u32[]{:S(2)}, u32[]{:S(2)}) async-start(f32[8,8,128]{2,1,0:T(8,128)} %broadcast_in_dim.2), calls=%async_computation.2 | async-start | bytes 65536 | tf_op jit(solution)/shard_map/all_to_all | solution.py:530
  68.8 0.7 copy-done.3
  69.5 6.0 %shard_map.53.pack_ref = bf16[32,96,256]{2,1,0:T(8,128)(2,1)} custom-call(bf16[2560,1024]{1,0:T(8,128)(2,1)} %get-tuple-element.32.grad_ref, bf16[256,1024]{1,0:T(8,128)(2,1)} %get-tuple-element.33.weight_ref, f32[16,256]{1,0:T(8,128)S(1)} %copy-done.3), custom_call_target="tpu_custom_call" | custom-call | flops 2000000000 | bytes 7000000 | tf_op jit(solution)/shard_map/pallas_call | solution.py:433
  75.7 1.9 shard_map.54
  77.6 7.7 %all-to-all-start.3 = ((bf16[32,96,256]{2,1,0:T(8,128)(2,1)}), bf16[32,96,256]{2,1,0:T(8,128)(2,1)}, u32[]{:S(2)}, u32[]{:S(2)}) async-start(bf16[32,96,256]{2,1,0:T(8,128)(2,1)} %shard_map.54), calls=%async_computation.3 | async-start | bytes 3145728 | tf_op jit(solution)/shard_map/all_to_all | solution.py:564
  85.4 2.0 %shard_map.55.mass_ref = f32[512,1024]{1,0:T(8,128)} custom-call(bf16[32,160,256]{2,1,0:T(8,128)(2,1)S(1)} %all_to_all.40.own_ref.unit_ref), custom_call_target="tpu_custom_call" | custom-call | flops 10000000 | bytes 3000000 | tf_op jit(solution)/shard_map/pallas_call | solution.py:433
  87.4 20.1 %all-to-all-done.3.came_hbm = bf16[32,96,256]{2,1,0:T(8,128)(2,1)} async-done(((bf16[32,96,256]{2,1,0:T(8,128)(2,1)}), bf16[32,96,256]{2,1,0:T(8,128)(2,1)}, u32[]{:S(2)}, u32[]{:S(2)}) %all-to-all-start.3) | async-done | bytes 1572896 | tf_op jit(solution)/shard_map/all_to_all | solution.py:564
  107.6 3.7 %shard_map.56 = bf16[8,48,256]{2,1,0:T(8,128)(2,1)} custom-call(s32[3]{0:T(128)S(1)} %pad_add_fusion.place_ref, bf16[32,96,256]{2,1,0:T(8,128)(2,1)} %all-to-all-done.3.came_hbm), custom_call_target="tpu_custom_call" | custom-call | flops 10000000 | bytes 2000000 | tf_op jit(solution)/shard_map/pallas_call | solution.py:433
  111.3 14.4 %all_to_all.41.came_ref = bf16[8,48,256]{2,1,0:T(8,128)(2,1)S(1)} all-to-all(bf16[8,48,256]{2,1,0:T(8,128)(2,1)} %shard_map.56), channel_id=1, replica_groups=mesh['y'=4,'x'=4,'core'=2,'proto'=8] {'proto'}, dimensions={0} | all-to-all | bytes 393216 | tf_op jit(solution)/shard_map/all_to_all | solution.py:597
  125.7 2.7 %shard_map.57 = (bf16[512,1024]{1,0:T(8,128)(2,1)}, bf16[32,40,256]{2,1,0:T(8,128)(2,1)}) custom-call(bf16[8,48,256]{2,1,0:T(8,128)(2,1)S(1)} %all_to_all.41.came_ref, f32[8,8,128]{2,1,0:T(8,128)S(1)} %all-to-all-done.2.came_ref.came_one_ref, f32[512,1024]{1,0:T(8,128)S(1)} %copy-done, bf16[256,512]{1,0:T(8,128)(2,1)S(1)} %copy-done.7, ...), custom_call_target="tpu_custom_call" | custom-call | flops 1000000000 | bytes 4000000 | tf_op jit(solution)/shard_map/pallas_call | solution.py:433
  128.4 7.2 %all-to-all-start.5 = ((bf16[32,40,256]{2,1,0:T(8,128)(2,1)}), bf16[32,40,256]{2,1,0:T(8,128)(2,1)S(1)}, u32[]{:S(2)}, u32[]{:S(2)}) async-start(bf16[32,40,256]{2,1,0:T(8,128)(2,1)} %get-tuple-element.42), calls=%async_computation.5 | async-start | bytes 1310720 | tf_op jit(solution)/shard_map/all_to_all | solution.py:611
  135.6 7.4 %shard_map.61 = (f32[256,512]{1,0:T(8,128)}, f32[256,512]{1,0:T(8,128)}) custom-call(s32[1]{0:T(128)} %bitcast.3.core_ref, bf16[32,160,256]{2,1,0:T(8,128)(2,1)S(1)} %all_to_all.40.own_ref.unit_ref, bf16[2560,1024]{1,0:T(8,128)(2,1)} %get-tuple-element.32.grad_ref, bf16[8,48,256]{2,1,0:T(8,128)(2,1)S(1)} %all_to_all.41.came_ref), custom_call_target="tpu_custom_call" | custom-call | flops 3000000000 | bytes 7000000 | tf_op jit(solution)/shard_map/pallas_call | solution.py:433
  143.4 1.2 shard_map.60.seen_ref
  144.7 1.5 shard_map.58.slice_ref
  146.2 2.4 %all-to-all-done.5.came_ref = bf16[32,40,256]{2,1,0:T(8,128)(2,1)S(1)} async-done(((bf16[32,40,256]{2,1,0:T(8,128)(2,1)}), bf16[32,40,256]{2,1,0:T(8,128)(2,1)S(1)}, u32[]{:S(2)}, u32[]{:S(2)}) %all-to-all-start.5) | async-done | bytes 655392 | tf_op jit(solution)/shard_map/all_to_all | solution.py:611
  148.5 0.7 copy-done.2
  149.3 1.3 shard_map.59
  150.5 3.4 %all-to-all-start.6 = ((bf16[8,64,256]{2,1,0:T(8,128)(2,1)}), bf16[8,64,256]{2,1,0:T(8,128)(2,1)S(1)}, u32[]{:S(2)}, u32[]{:S(2)}) async-start(bf16[8,64,256]{2,1,0:T(8,128)(2,1)} %shard_map.59), calls=%async_computation.6 | async-start | bytes 524288 | tf_op jit(solution)/shard_map/all_to_all | solution.py:642
  154.0 2.1 %add.15.term_ref = f32[256,512]{1,0:T(8,128)} add(f32[256,512]{1,0:T(8,128)} %get-tuple-element.45, f32[256,512]{1,0:T(8,128)} %collective-permute-done.2) | non-fusion elementwise | flops 131072 | bytes 1572864 | tf_op jit(solution)/shard_map/add | solution.py:628
  156.1 9.6 %all-to-all-done.6.came_ref = bf16[8,64,256]{2,1,0:T(8,128)(2,1)S(1)} async-done(((bf16[8,64,256]{2,1,0:T(8,128)(2,1)}), bf16[8,64,256]{2,1,0:T(8,128)(2,1)S(1)}, u32[]{:S(2)}, u32[]{:S(2)}) %all-to-all-start.6) | async-done | bytes 262176 | tf_op jit(solution)/shard_map/all_to_all | solution.py:642
  165.7 3.9 %shard_map.62 = f32[256,512]{1,0:T(8,128)} custom-call(s32[1]{0:T(128)} %bitcast.3.core_ref, bf16[8,64,256]{2,1,0:T(8,128)(2,1)S(1)} %all-to-all-done.6.came_ref, bf16[512,1024]{1,0:T(8,128)(2,1)} %get-tuple-element.44.keep_ref, f32[256,512]{1,0:T(8,128)} %shard_map.60.seen_ref, f32[256,512]{1,0:T(8,128)} %copy-done.9, f32[256,512]{1,0:T(8,128)} %add.15.term_ref, ...), custom_call_target="tpu_custom_call" | custom-call | flops 1000000000 | bytes 4000000 | tf_op jit(solution)/shard_map/pallas_call | solution.py:433
  169.6 5.7 %all-to-all-start.7 = ((f32[32,8,512]{2,1,0:T(8,128)}), f32[32,8,512]{2,1,0:T(8,128)S(1)}, u32[]{:S(2)}, u32[]{:S(2)}) async-start(f32[32,8,512]{2,1,0:T(8,128)} %bitcast.9), calls=%async_computation.7 | async-start | bytes 1048576 | tf_op jit(solution)/shard_map/all_to_all | solution.py:663
  175.3 1.3 shard_map.63
  176.7 10.2 %all-to-all-done.7 = f32[32,8,512]{2,1,0:T(8,128)S(1)} async-done(((f32[32,8,512]{2,1,0:T(8,128)}), f32[32,8,512]{2,1,0:T(8,128)S(1)}, u32[]{:S(2)}, u32[]{:S(2)}) %all-to-all-start.7) | async-done | bytes 524320 | tf_op jit(solution)/shard_map/all_to_all | solution.py:663
  186.9 0.8 copy.8
  (28 shorter events, 1.5 us)
Async XLA Ops:
  46.4 2.2 %collective-permute-start = (bf16[32,16,256]{2,1,0:T(8,128)(2,1)S(1)}, bf16[32,16,256]{2,1,0:T(8,128)(2,1)S(1)}, u32[]{:S(2)}, u32[]{:S(2)}) collective-permute-start(bf16[32,16,256]{2,1,0:T(8,128)(2,1)S(1)} %slice.4), channel_id=1, source_target_pairs={{0,8},{8,0},{1,9},{9,1},{2,10},{10,2},{3,11},{11,3},{4,12},{12,4},... | collective-permute-start | bytes 786440 | tf_op jit(solution)/shard_map/ppermute | solution.py:474
  48.6 11.3 %all-to-all-start.1 = ((f32[32,8,128]{2,1,0:T(8,128)}), f32[32,8,128]{2,1,0:T(8,128)S(1)}, u32[]{:S(2)}, u32[]{:S(2)}) async-start(f32[32,8,128]{2,1,0:T(8,128)} %shard_map.51), calls=%async_computation.1 | async-start | bytes 262144 | tf_op jit(solution)/shard_map/all_to_all | solution.py:488
  60.6 15.2 %all-to-all-start.2 = ((f32[8,8,128]{2,1,0:T(8,128)}), f32[8,8,128]{2,1,0:T(8,128)S(1)}, u32[]{:S(2)}, u32[]{:S(2)}) async-start(f32[8,8,128]{2,1,0:T(8,128)} %broadcast_in_dim.2), calls=%async_computation.2 | async-start | bytes 65536 | tf_op jit(solution)/shard_map/all_to_all | solution.py:530
  68.7 0.7 copy-start.3
  69.5 6.3 %copy-start.4 = (f32[16,256]{1,0:T(8,128)S(1)}, f32[16,256]{1,0:T(8,128)}, u32[]{:S(2)}) copy-start(f32[16,256]{1,0:T(8,128)} %get-tuple-element.34.part_ref.sum_ref) | copy-start | bytes 49156
  77.6 30.0 %all-to-all-start.3 = ((bf16[32,96,256]{2,1,0:T(8,128)(2,1)}), bf16[32,96,256]{2,1,0:T(8,128)(2,1)}, u32[]{:S(2)}, u32[]{:S(2)}) async-start(bf16[32,96,256]{2,1,0:T(8,128)(2,1)} %shard_map.54), calls=%async_computation.3 | async-start | bytes 3145728 | tf_op jit(solution)/shard_map/all_to_all | solution.py:564
  85.4 40.3 %copy-start.7 = (bf16[256,512]{1,0:T(8,128)(2,1)S(1)}, bf16[256,512]{1,0:T(8,128)(2,1)}, u32[]{:S(2)}) copy-start(bf16[256,512]{1,0:T(8,128)(2,1)} %get-tuple-element.40.hi_ref) | copy-start | bytes 786436
  85.4 40.3 %copy-start.8 = (bf16[256,512]{1,0:T(8,128)(2,1)S(1)}, bf16[256,512]{1,0:T(8,128)(2,1)}, u32[]{:S(2)}) copy-start(bf16[256,512]{1,0:T(8,128)(2,1)} %get-tuple-element.41.lo_ref) | copy-start | bytes 786436
  107.6 18.1 %copy-start = (f32[512,1024]{1,0:T(8,128)S(1)}, f32[512,1024]{1,0:T(8,128)}, u32[]{:S(2)}) copy-start(f32[512,1024]{1,0:T(8,128)} %shard_map.55.mass_ref) | copy-start | bytes 6291460
  128.4 20.1 %all-to-all-start.5 = ((bf16[32,40,256]{2,1,0:T(8,128)(2,1)}), bf16[32,40,256]{2,1,0:T(8,128)(2,1)S(1)}, u32[]{:S(2)}, u32[]{:S(2)}) async-start(bf16[32,40,256]{2,1,0:T(8,128)(2,1)} %get-tuple-element.42), calls=%async_computation.5 | async-start | bytes 1310720 | tf_op jit(solution)/shard_map/all_to_all | solution.py:611
  143.0 11.0 %collective-permute-start.2 = (f32[256,512]{1,0:T(8,128)}, f32[256,512]{1,0:T(8,128)}, u32[]{:S(2)}, u32[]{:S(2)}) collective-permute-start(f32[256,512]{1,0:T(8,128)} %get-tuple-element.46), channel_id=1, source_target_pairs={{0,8},{8,0},{1,9},{9,1},{2,10},{10,2},{3,11},{11,3},{4,12},{12,4},... | collective-permute-start | bytes 1572872 | tf_op jit(solution)/shard_map/ppermute | solution.py:628
  144.6 21.1 %copy-start.5 = (f32[1,512]{1,0:T(1,128)S(1)}, f32[1,512]{1,0:T(1,128)}, u32[]{:S(2)}) copy-start(f32[1,512]{1,0:T(1,128)} %get-tuple-element.48.scale_ref) | copy-start | bytes 6148
  144.6 21.1 %copy-start.6 = (f32[1,512]{1,0:T(1,128)S(1)}, f32[1,512]{1,0:T(1,128)}, u32[]{:S(2)}) copy-start(f32[1,512]{1,0:T(1,128)} %get-tuple-element.49.inv_ref) | copy-start | bytes 6148
  144.6 11.5 %collective-permute-start.1 = (f32[256,512]{1,0:T(8,128)}, f32[256,512]{1,0:T(8,128)S(1)}, u32[]{:S(2)}, u32[]{:S(2)}) collective-permute-start(f32[256,512]{1,0:T(8,128)} %shard_map.60.seen_ref), channel_id=1, source_target_pairs={{0,8},{8,0},{1,9},{9,1},{2,10},{10,2},{3,11},{11,3},{4,12},{12,4},... | collective-permute-start | bytes 1572872 | tf_op jit(solution)/shard_map/ppermute | solution.py:577
  148.5 0.7 copy-start.2
  150.5 15.1 %all-to-all-start.6 = ((bf16[8,64,256]{2,1,0:T(8,128)(2,1)}), bf16[8,64,256]{2,1,0:T(8,128)(2,1)S(1)}, u32[]{:S(2)}, u32[]{:S(2)}) async-start(bf16[8,64,256]{2,1,0:T(8,128)(2,1)} %shard_map.59), calls=%async_computation.6 | async-start | bytes 524288 | tf_op jit(solution)/shard_map/all_to_all | solution.py:642
  156.1 9.6 %copy-start.9 = (f32[256,512]{1,0:T(8,128)}, f32[256,512]{1,0:T(8,128)S(1)}, u32[]{:S(2)}) copy-start(f32[256,512]{1,0:T(8,128)S(1)} %collective-permute-done.1.mate_ref) | copy-start | bytes 1572868
  165.7 9.7 %copy-start.1 = (bf16[160,256]{1,0:T(8,128)(2,1)S(1)}, bf16[160,256]{1,0:T(8,128)(2,1)}, u32[]{:S(2)}) copy-start(bf16[160,256]{1,0:T(8,128)(2,1)} %feat_ref.2) | copy-start | bytes 245764
  169.6 17.3 %all-to-all-start.7 = ((f32[32,8,512]{2,1,0:T(8,128)}), f32[32,8,512]{2,1,0:T(8,128)S(1)}, u32[]{:S(2)}, u32[]{:S(2)}) async-start(f32[32,8,512]{2,1,0:T(8,128)} %bitcast.9), calls=%async_computation.7 | async-start | bytes 1048576 | tf_op jit(solution)/shard_map/all_to_all | solution.py:663
